TPU v7x, 32 devices: a whole 2x2x4 slice. The times are simulated.
32 devices in a mesh: groups: 2 (over x), seq: 16 (over z, y, core).
Axes of the slice: x: 2, y: 2, z: 4, core: 2. Of those that a mesh axis runs over, the one named last changes fastest.
Arguments:
- block_mask: int32 [64, 32], P(('groups', 'seq')), parts along dimension 0, may hold values from 0 to 1, as said below
- queries: bfloat16 [8192, 20, 128], P(('groups', 'seq')), parts along dimension 0, may hold values from -64 to 64
- keys: bfloat16 [8192, 4, 128], P(('groups', 'seq')), parts along dimension 0, may hold values from -64 to 64
- values: bfloat16 [8192, 4, 128], P(('groups', 'seq')), parts along dimension 0, may hold values from -6 to 6
- output_gradient: bfloat16 [8192, 20, 128], P(('groups', 'seq')), parts along dimension 0, may hold values from -6 to 6
Outputs:
- attended: bfloat16 [8192, 20, 128], P(('groups', 'seq')), parts along dimension 0
- grad_queries: bfloat16 [8192, 20, 128], P(('groups', 'seq')), parts along dimension 0
- grad_keys: bfloat16 [8192, 4, 128], P(('groups', 'seq')), parts along dimension 0
- grad_values: bfloat16 [8192, 4, 128], P(('groups', 'seq')), parts along dimension 0
There are 2 independent parts, one for each index of `groups`. A program takes and returns all parts, laid end to end along the dimension named above; each array names one. Nothing has to cross between parts.
Inputs may be any that keep to these rules, and one draw needn't show every extreme that they name: `block_mask`: entries are 0 or 1. Let device(b) = b // 2. An entry [a, b] is 1 only where device(b) equals device(a) or device(a) XOR 2**k for k in 0, 1, log2(16) - 2, log2(16) - 1; every diagonal entry is 1. The share of ones differs from one query device to another.
All inputs are finite; a program needn't handle non-finite values.
Results may differ from a plain program's by a relative error of at most 0.03.
Values may be sent and summed in bfloat16 or wider, within the bound.
No kernel may reach another device: no remote copies, remote signals or barrier semaphores. Data moves between devices by JAX's collectives and lax.ppermute only.
A program may use at most 128 MiB of HBM per device.

v0:
```python
import jax
import jax.numpy as jnp
from jax import lax
from jax.sharding import PartitionSpec as P


def from_partner(value, axis, apart):
    mask = 2**apart
    pairs = [(source, source ^ mask) for source in range(lax.axis_size(axis))]
    return lax.ppermute(value, axis, pairs)


def partner_bits(count):
    level = count.bit_length() - 1
    return (0, 1, level - 2, level - 1)


def product(form, left, right):
    return jnp.einsum(form, left, right, preferred_element_type=jnp.float32)


def token_mask(blocks, width):
    return jnp.repeat(jnp.repeat(blocks > 0, width, axis=0), width, axis=1)


def widened(term):
    return lax.optimization_barrier(term).astype(jnp.float32)


def softmax_weights(scores, allowed_mask, top, total):
    masked = jnp.where(allowed_mask, scores, -1e30)
    return (jnp.where(allowed_mask, jnp.exp(masked - top), 0.0) / total).astype(jnp.bfloat16)


def score_grads(dout, value_row_block, weights, delta, softmax_scale):
    dprob = product("qgd,kd->gqk", dout, value_row_block)
    return (weights.astype(jnp.float32) * (dprob - delta) * softmax_scale).astype(jnp.bfloat16)


def attend_single_head(query, dout, key_row_block, value_row_block, allowed_mask, softmax_scale):
    scores = product("qgd,kd->gqk", query, key_row_block) * softmax_scale
    masked = jnp.where(allowed_mask, scores, -1e30)
    top = jnp.max(masked, axis=-1, keepdims=True)
    total = jnp.sum(jnp.where(allowed_mask, jnp.exp(masked - top), 0.0), axis=-1, keepdims=True)
    weights = softmax_weights(scores, allowed_mask, top, total)
    attended = product("gqk,kd->qgd", weights, value_row_block).astype(jnp.bfloat16)
    delta = jnp.sum(dout.astype(jnp.float32) * attended.astype(jnp.float32), axis=-1)
    delta = jnp.transpose(delta)[:, :, None]
    dscore = score_grads(dout, value_row_block, weights, delta, softmax_scale)
    grad_query = product("gqk,kd->qgd", dscore, key_row_block).astype(jnp.bfloat16)
    key_gradient = product("gqk,qgd->kd", dscore, query)
    value_gradient = product("gqk,qgd->kd", weights, dout)
    return (attended, grad_query, key_gradient, value_gradient, top, total, delta)


def shards(block_mask, queries, keys, values, output_gradient):
    count = lax.axis_size("seq")
    me = lax.axis_index("seq")
    rows = block_mask.shape[0]
    tok_rows = queries.shape[0]
    width = tok_rows // rows
    kv_heads = keys.shape[1]
    head_dim = keys.shape[2]
    head_group = queries.shape[1] // kv_heads
    softmax_scale = head_dim ** (-0.5)
    query = queries.reshape(tok_rows, kv_heads, head_group, head_dim)
    dout = output_gradient.reshape(tok_rows, kv_heads, head_group, head_dim)
    bits = partner_bits(count)

    def columns(device):
        return lax.dynamic_slice_in_dim(block_mask, device * rows, rows, 1)

    key_list = [keys]
    value_list = [values]
    block_list = [columns(me)]
    for bit in bits:
        got_keys, got_values = from_partner((keys, values), "seq", bit)
        key_list.append(got_keys)
        value_list.append(got_values)
        block_list.append(columns(jnp.bitwise_xor(me, 1 << bit)))
    key_row_block = jnp.concatenate(key_list, axis=0)
    value_row_block = jnp.concatenate(value_list, axis=0)
    allowed_mask = token_mask(jnp.concatenate(block_list, axis=1), width)[None]
    collected_results = [
        attend_single_head(
            query[:, head_number],
            dout[:, head_number],
            key_row_block[:, head_number],
            value_row_block[:, head_number],
            allowed_mask,
            softmax_scale,
        )
        for head_number in range(kv_heads)
    ]
    attended = jnp.stack([r[0] for r in collected_results], axis=1)
    grad_query = jnp.stack([r[1] for r in collected_results], axis=1)
    key_all = jnp.stack([r[2] for r in collected_results], axis=1).astype(jnp.bfloat16)
    value_all = jnp.stack([r[3] for r in collected_results], axis=1).astype(jnp.bfloat16)
    key_gradient = widened(key_all[:tok_rows])
    value_gradient = widened(value_all[:tok_rows])
    for slot, bit in enumerate(bits):
        lower = (slot + 1) * tok_rows
        back_keys, back_values = from_partner(
            (key_all[lower : lower + tok_rows], value_all[lower : lower + tok_rows]), "seq", bit
        )
        key_gradient = key_gradient + widened(back_keys)
        value_gradient = value_gradient + widened(back_values)
    return (
        attended.reshape(queries.shape),
        grad_query.reshape(queries.shape),
        key_gradient.astype(jnp.bfloat16),
        value_gradient.astype(jnp.bfloat16),
    )


def solution(mesh):
    return jax.shard_map(
        shards,
        mesh=mesh,
        in_specs=(
            P(("groups", "seq"), None),
            P(("groups", "seq"), None, None),
            P(("groups", "seq"), None, None),
            P(("groups", "seq"), None, None),
            P(("groups", "seq"), None, None),
        ),
        out_specs=(
            P(("groups", "seq"), None, None),
            P(("groups", "seq"), None, None),
            P(("groups", "seq"), None, None),
            P(("groups", "seq"), None, None),
        ),
        check_vma=False,
    )
```

profile of v0, /device:TPU:0, one launch (start us, length us, event | category | flops | bytes accessed | tf_op | source)
XLA Modules:
  0.0 114.7 jit_solution(3321360175792495714)
XLA Ops:
  2.2 2.6 %collective-permute-start.5 = (bf16[256,4,128]{2,0,1:T(8,128)(2,1)S(1)}, bf16[256,4,128]{2,0,1:T(8,128)(2,1)S(1)}, u32[]{:S(2)}, u32[]{:S(2)}) collective-permute-start(bf16[256,4,128]{2,0,1:T(8,128)(2,1)S(1)} %get-tuple-element.26), channel_id=1, source_target_pairs={{0,2},{1,3},{2,0},{3,1},{4,6},{5,7},{6,4},{7,5},{8,10},{9,11},{10,... | collective-permute-start | bytes 786440 | tf_op jit(solution)/shard_map/ppermute | solution.py:10
  4.8 1.6 %collective-permute-start.6 = (bf16[256,4,128]{2,0,1:T(8,128)(2,1)S(1)}, bf16[256,4,128]{2,0,1:T(8,128)(2,1)S(1)}, u32[]{:S(2)}, u32[]{:S(2)}) collective-permute-start(bf16[256,4,128]{2,0,1:T(8,128)(2,1)S(1)} %get-tuple-element.26), channel_id=1, source_target_pairs={{0,4},{1,5},{2,6},{3,7},{4,0},{5,1},{6,2},{7,3},{8,12},{9,13},{10,... | collective-permute-start | bytes 786440 | tf_op jit(solution)/shard_map/ppermute | solution.py:10
  6.3 2.6 %collective-permute-start.7 = (bf16[256,4,128]{2,0,1:T(8,128)(2,1)S(1)}, bf16[256,4,128]{2,0,1:T(8,128)(2,1)S(1)}, u32[]{:S(2)}, u32[]{:S(2)}) collective-permute-start(bf16[256,4,128]{2,0,1:T(8,128)(2,1)S(1)} %get-tuple-element.26), channel_id=1, source_target_pairs={{0,8},{1,9},{2,10},{3,11},{4,12},{5,13},{6,14},{7,15},{8,0},{9,1},... | collective-permute-start | bytes 786440 | tf_op jit(solution)/shard_map/ppermute | solution.py:10
  12.1 2.4 %copy.64 = bf16[256,20,128]{0,2,1:T(8,128)(2,1)} copy(bf16[256,20,128]{2,0,1:T(8,128)(2,1)} %param.9) | data formatting | bytes 2621440 | tf_op args[4]
  15.7 3.6 %collective-permute-done.6 = bf16[256,4,128]{2,0,1:T(8,128)(2,1)S(1)} collective-permute-done((bf16[256,4,128]{2,0,1:T(8,128)(2,1)S(1)}, bf16[256,4,128]{2,0,1:T(8,128)(2,1)S(1)}, u32[]{:S(2)}, u32[]{:S(2)}) %collective-permute-start.6) | collective-permute-done | bytes 262176 | tf_op jit(solution)/shard_map/ppermute | solution.py:10
  20.6 7.5 %fusion.76 = (f32[5,256]{1,0:T(8,128)}, f32[5,256,1280]{1,2,0:T(8,128)}) fusion(pred[256,1280]{0,1:T(8,128)(4,1)S(1)} %bitcast.344, bf16[1280,4,128]{2,0,1:T(8,128)(2,1)S(1)} %constant_dynamic-update-slice_fusion.5, bf16[256,4,5,128]{3,0,2,1:T(8,128)(2,1)} %bitcast.350), kind=kOutput, calls=%fused_computation.147 | convolution fusion | flops 427623680 | bytes 7869440 | tf_op jit(solution)/shard_map/sub | solution.py:32
  28.1 5.6 %fusion.77 = (f32[5,256]{1,0:T(8,128)S(1)}, f32[5,256,1280]{1,2,0:T(8,128)}) fusion(pred[256,1280]{0,1:T(8,128)(4,1)S(1)} %bitcast.345, bf16[1280,4,128]{2,0,1:T(8,128)(2,1)S(1)} %constant_dynamic-update-slice_fusion.5, bf16[256,4,5,128]{3,0,2,1:T(8,128)(2,1)S(1)} %bitcast.352), kind=kOutput, calls=%fused_computation.148 | convolution fusion | flops 427623680 | bytes 7869440 | tf_op jit(solution)/shard_map/sub | solution.py:32
  33.7 5.6 %fusion.78 = (f32[5,256]{1,0:T(8,128)S(1)}, f32[5,256,1280]{1,2,0:T(8,128)}) fusion(pred[256,1280]{0,1:T(8,128)(4,1)S(1)} %bitcast.346, bf16[1280,4,128]{2,0,1:T(8,128)(2,1)S(1)} %constant_dynamic-update-slice_fusion.5, bf16[256,4,5,128]{3,0,2,1:T(8,128)(2,1)S(1)} %bitcast.353), kind=kOutput, calls=%fused_computation.149 | convolution fusion | flops 427623680 | bytes 7869440 | tf_op jit(solution)/shard_map/sub | solution.py:32
  39.3 3.6 %divide_convert_fusion.1 = bf16[5,256,1280]{1,2,0:T(8,128)(2,1)S(1)} fusion(f32[5,256,1280]{1,2,0:T(8,128)} %get-tuple-element.36, f32[5,256]{1,0:T(8,128)} %get-tuple-element.35), kind=kLoop, calls=%fused_computation.26 | loop fusion | flops 3276800 | bytes 9835520 | tf_op jit(solution)/shard_map/convert_element_type | solution.py:32
  44.0 2.3 %divide_convert_fusion.2 = bf16[5,256,1280]{1,2,0:T(8,128)(2,1)} fusion(f32[5,256,1280]{1,2,0:T(8,128)S(1)} %copy-done.1, f32[5,256]{1,0:T(8,128)S(1)} %get-tuple-element.37), kind=kLoop, calls=%fused_computation.28 | loop fusion | flops 3276800 | bytes 9835520 | tf_op jit(solution)/shard_map/convert_element_type | solution.py:32
  46.3 7.0 %fusion.75 = (f32[5,256]{1,0:T(8,128)S(1)}, f32[5,256,1280]{1,2,0:T(8,128)}) fusion(pred[256,1280]{0,1:T(8,128)(4,1)} %bitcast.347, bf16[1280,4,128]{2,0,1:T(8,128)(2,1)} %copy-done.2, bf16[256,4,5,128]{3,0,2,1:T(8,128)(2,1)} %bitcast.351), kind=kOutput, calls=%fused_computation.146 | convolution fusion | flops 427623680 | bytes 7869440 | tf_op jit(solution)/shard_map/sub | solution.py:32
  53.4 1.7 %constant_dynamic-update-slice_fusion.3 = bf16[1280,4,128]{0,2,1:T(8,128)(2,1)} fusion(bf16[1280,4,128]{0,2,1:T(8,128)(2,1)} %constant_dynamic-update-slice_fusion.4, bf16[256,4,128]{0,2,1:T(8,128)(2,1)} %collective-permute-done), kind=kLoop, calls=%fused_computation.121 | loop fusion | bytes 524288
  55.1 1.8 %constant_dynamic-update-slice_fusion.2 = bf16[1280,4,128]{0,2,1:T(8,128)(2,1)} fusion(bf16[1280,4,128]{0,2,1:T(8,128)(2,1)} %constant_dynamic-update-slice_fusion.3, bf16[256,4,128]{0,2,1:T(8,128)(2,1)} %collective-permute-done.1), kind=kLoop, calls=%fused_computation.120 | loop fusion | bytes 524288
  56.9 2.1 %fusion.41 = bf16[1280,1,128]{2,0,1:T(8,128)(2,1)S(1)} fusion(bf16[5,256,1280]{1,2,0:T(8,128)(2,1)S(1)} %divide_convert_fusion.1, bf16[256,4,5,128]{0,3,2,1:T(8,128)(2,1)} %bitcast.331), kind=kOutput, calls=%fused_computation.65 | convolution fusion | flops 419594240 | bytes 3932160 | tf_op jit(solution)/shard_map/gqk,qgd->kd/dot_general | solution.py:19
  60.0 1.8 %fusion.42 = bf16[1280,1,128]{2,0,1:T(8,128)(2,1)} fusion(bf16[5,256,1280]{1,2,0:T(8,128)(2,1)S(1)} %copy-done, bf16[256,4,5,128]{0,3,2,1:T(8,128)(2,1)S(1)} %bitcast.332), kind=kOutput, calls=%fused_computation.66 | convolution fusion | flops 419594240 | bytes 3932160 | tf_op jit(solution)/shard_map/gqk,qgd->kd/dot_general | solution.py:19
  68.8 1.4 %multiply_reduce_fusion.3 = (f32[256,5]{0,1:T(8,128)S(1)}, f32[256,5]{0,1:T(8,128)S(1)}, f32[256,5]{0,1:T(8,128)S(1)}, f32[256,5]{0,1:T(8,128)S(1)}, bf16[128,5,256]{2,0,1:T(8,128)(2,1)}) fusion(bf16[256,4,5,128]{0,3,2,1:T(8,128)(2,1)S(1)} %bitcast.335, bf16[128,5,256]{2,0,1:T(8,128)(2,1)S(1)} %convolution_convert_fusion.4, ...), kind=kOutput, calls=%fused_computation.95 | convolution fusion | flops 422210560 | bytes 6246400 | tf_op jit(solution)/shard_map/gqk,kd->qgd/dot_general | solution.py:19
  84.2 2.5 %collective-permute-start.14 = (bf16[256,4,128]{2,0,1:T(8,128)(2,1)}, bf16[256,4,128]{2,0,1:T(8,128)(2,1)}, u32[]{:S(2)}, u32[]{:S(2)}) collective-permute-start(bf16[256,4,128]{2,0,1:T(8,128)(2,1)} %get-tuple-element.18), channel_id=1, source_target_pairs={{0,4},{1,5},{2,6},{3,7},{4,0},{5,1},{6,2},{7,3},{8,12},{9,13},{10,... | collective-permute-start | bytes 786440 | tf_op jit(solution)/shard_map/ppermute | solution.py:10
  89.4 1.4 %copy.86 = bf16[256,20,128]{2,0,1:T(8,128)(2,1)} copy(bf16[256,20,128]{0,2,1:T(8,128)(2,1)S(1)} %bitcast.329) | data formatting | bytes 2621440
  91.0 1.4 %copy.85 = bf16[256,20,128]{2,0,1:T(8,128)(2,1)} copy(bf16[256,20,128]{0,2,1:T(8,128)(2,1)S(1)} %bitcast.330) | data formatting | bytes 2621440
  92.5 1.5 %collective-permute-start.9 = (bf16[256,4,128]{2,0,1:T(8,128)(2,1)}, bf16[256,4,128]{2,0,1:T(8,128)(2,1)S(1)}, u32[]{:S(2)}, u32[]{:S(2)}) collective-permute-start(bf16[256,4,128]{2,0,1:T(8,128)(2,1)} %get-tuple-element.24), channel_id=1, source_target_pairs={{0,2},{1,3},{2,0},{3,1},{4,6},{5,7},{6,4},{7,5},{8,10},{9,11},{10,... | collective-permute-start | bytes 786440 | tf_op jit(solution)/shard_map/ppermute | solution.py:10
  95.2 3.1 %collective-permute-done.14 = bf16[256,4,128]{2,0,1:T(8,128)(2,1)} collective-permute-done((bf16[256,4,128]{2,0,1:T(8,128)(2,1)}, bf16[256,4,128]{2,0,1:T(8,128)(2,1)}, u32[]{:S(2)}, u32[]{:S(2)}) %collective-permute-start.14) | collective-permute-done | bytes 262176 | tf_op jit(solution)/shard_map/ppermute | solution.py:10
  98.3 2.2 %collective-permute-start.11 = (bf16[256,4,128]{2,0,1:T(8,128)(2,1)}, bf16[256,4,128]{2,0,1:T(8,128)(2,1)S(1)}, u32[]{:S(2)}, u32[]{:S(2)}) collective-permute-start(bf16[256,4,128]{2,0,1:T(8,128)(2,1)} %get-tuple-element.22), channel_id=1, source_target_pairs={{0,8},{1,9},{2,10},{3,11},{4,12},{5,13},{6,14},{7,15},{8,0},{9,1},... | collective-permute-start | bytes 786440 | tf_op jit(solution)/shard_map/ppermute | solution.py:10
  104.0 5.1 %collective-permute-done.10 = bf16[256,4,128]{2,0,1:T(8,128)(2,1)S(1)} collective-permute-done((bf16[256,4,128]{2,0,1:T(8,128)(2,1)}, bf16[256,4,128]{2,0,1:T(8,128)(2,1)S(1)}, u32[]{:S(2)}, u32[]{:S(2)}) %collective-permute-start.10) | collective-permute-done | bytes 262176 | tf_op jit(solution)/shard_map/ppermute | solution.py:10
  109.1 3.7 %collective-permute-done.11 = bf16[256,4,128]{2,0,1:T(8,128)(2,1)S(1)} collective-permute-done((bf16[256,4,128]{2,0,1:T(8,128)(2,1)}, bf16[256,4,128]{2,0,1:T(8,128)(2,1)S(1)}, u32[]{:S(2)}, u32[]{:S(2)}) %collective-permute-start.11) | collective-permute-done | bytes 262176 | tf_op jit(solution)/shard_map/ppermute | solution.py:10
  (112 shorter events, 39.5 us)
Async XLA Ops:
  1.7 12.9 %collective-permute-start.4 = (bf16[256,4,128]{2,0,1:T(8,128)(2,1)S(1)}, bf16[256,4,128]{2,0,1:T(8,128)(2,1)S(1)}, u32[]{:S(2)}, u32[]{:S(2)}) collective-permute-start(bf16[256,4,128]{2,0,1:T(8,128)(2,1)S(1)} %get-tuple-element.26), channel_id=1, source_target_pairs={{0,1},{1,0},{2,3},{3,2},{4,5},{5,4},{6,7},{7,6},{8,9},{9,8},{10,11... | collective-permute-start | bytes 786440 | tf_op jit(solution)/shard_map/ppermute | solution.py:10
  2.2 12.9 %collective-permute-start.5 = (bf16[256,4,128]{2,0,1:T(8,128)(2,1)S(1)}, bf16[256,4,128]{2,0,1:T(8,128)(2,1)S(1)}, u32[]{:S(2)}, u32[]{:S(2)}) collective-permute-start(bf16[256,4,128]{2,0,1:T(8,128)(2,1)S(1)} %get-tuple-element.26), channel_id=1, source_target_pairs={{0,2},{1,3},{2,0},{3,1},{4,6},{5,7},{6,4},{7,5},{8,10},{9,11},{10,... | collective-permute-start | bytes 786440 | tf_op jit(solution)/shard_map/ppermute | solution.py:10
  4.8 14.5 %collective-permute-start.6 = (bf16[256,4,128]{2,0,1:T(8,128)(2,1)S(1)}, bf16[256,4,128]{2,0,1:T(8,128)(2,1)S(1)}, u32[]{:S(2)}, u32[]{:S(2)}) collective-permute-start(bf16[256,4,128]{2,0,1:T(8,128)(2,1)S(1)} %get-tuple-element.26), channel_id=1, source_target_pairs={{0,4},{1,5},{2,6},{3,7},{4,0},{5,1},{6,2},{7,3},{8,12},{9,13},{10,... | collective-permute-start | bytes 786440 | tf_op jit(solution)/shard_map/ppermute | solution.py:10
  6.3 14.1 %collective-permute-start.7 = (bf16[256,4,128]{2,0,1:T(8,128)(2,1)S(1)}, bf16[256,4,128]{2,0,1:T(8,128)(2,1)S(1)}, u32[]{:S(2)}, u32[]{:S(2)}) collective-permute-start(bf16[256,4,128]{2,0,1:T(8,128)(2,1)S(1)} %get-tuple-element.26), channel_id=1, source_target_pairs={{0,8},{1,9},{2,10},{3,11},{4,12},{5,13},{6,14},{7,15},{8,0},{9,1},... | collective-permute-start | bytes 786440 | tf_op jit(solution)/shard_map/ppermute | solution.py:10
  10.0 43.3 %collective-permute-start = (bf16[256,4,128]{0,2,1:T(8,128)(2,1)S(1)}, bf16[256,4,128]{0,2,1:T(8,128)(2,1)}, u32[]{:S(2)}, u32[]{:S(2)}) collective-permute-start(bf16[256,4,128]{0,2,1:T(8,128)(2,1)S(1)} %copy.53), channel_id=1, source_target_pairs={{0,1},{1,0},{2,3},{3,2},{4,5},{5,4},{6,7},{7,6},{8,9},{9,8},{10,11... | collective-permute-start | bytes 786440 | tf_op jit(solution)/shard_map/ppermute | solution.py:10
  14.6 40.5 %collective-permute-start.1 = (bf16[256,4,128]{0,2,1:T(8,128)(2,1)S(1)}, bf16[256,4,128]{0,2,1:T(8,128)(2,1)}, u32[]{:S(2)}, u32[]{:S(2)}) collective-permute-start(bf16[256,4,128]{0,2,1:T(8,128)(2,1)S(1)} %copy.53), channel_id=1, source_target_pairs={{0,2},{1,3},{2,0},{3,1},{4,6},{5,7},{6,4},{7,5},{8,10},{9,11},{10,... | collective-permute-start | bytes 786440 | tf_op jit(solution)/shard_map/ppermute | solution.py:10
  15.1 43.8 %collective-permute-start.2 = (bf16[256,4,128]{0,2,1:T(8,128)(2,1)S(1)}, bf16[256,4,128]{0,2,1:T(8,128)(2,1)}, u32[]{:S(2)}, u32[]{:S(2)}) collective-permute-start(bf16[256,4,128]{0,2,1:T(8,128)(2,1)S(1)} %copy.53), channel_id=1, source_target_pairs={{0,4},{1,5},{2,6},{3,7},{4,0},{5,1},{6,2},{7,3},{8,12},{9,13},{10,... | collective-permute-start | bytes 786440 | tf_op jit(solution)/shard_map/ppermute | solution.py:10
  19.3 42.5 %collective-permute-start.3 = (bf16[256,4,128]{0,2,1:T(8,128)(2,1)S(1)}, bf16[256,4,128]{0,2,1:T(8,128)(2,1)}, u32[]{:S(2)}, u32[]{:S(2)}) collective-permute-start(bf16[256,4,128]{0,2,1:T(8,128)(2,1)S(1)} %copy.53), channel_id=1, source_target_pairs={{0,8},{1,9},{2,10},{3,11},{4,12},{5,13},{6,14},{7,15},{8,0},{9,1},... | collective-permute-start | bytes 786440 | tf_op jit(solution)/shard_map/ppermute | solution.py:10
  20.4 13.2 %copy-start.2 = (bf16[1280,4,128]{2,0,1:T(8,128)(2,1)}, bf16[1280,4,128]{2,0,1:T(8,128)(2,1)S(1)}, u32[]{:S(2)}) copy-start(bf16[1280,4,128]{2,0,1:T(8,128)(2,1)S(1)} %constant_dynamic-update-slice_fusion.5) | copy-start | bytes 3932164
  20.5 13.1 %copy-start.14 = (pred[256,10,128]{0,2,1:T(8,128)(4,1)}, pred[256,10,128]{0,2,1:T(8,128)(4,1)S(1)}, u32[]{:S(2)}) copy-start(pred[256,10,128]{0,2,1:T(8,128)(4,1)S(1)} %broadcast_in_dim.95) | copy-start | bytes 983044
  20.6 7.6 %copy-start.15 = (bf16[256,20,128]{2,0,1:T(8,128)(2,1)S(1)}, bf16[256,20,128]{2,0,1:T(8,128)(2,1)}, u32[]{:S(2)}) copy-start(bf16[256,20,128]{2,0,1:T(8,128)(2,1)} %param.6) | copy-start | bytes 3932164
  39.2 4.8 %copy-start.1 = (f32[5,256,1280]{1,2,0:T(8,128)S(1)}, f32[5,256,1280]{1,2,0:T(8,128)}, u32[]{:S(2)}) copy-start(f32[5,256,1280]{1,2,0:T(8,128)} %get-tuple-element.38) | copy-start | bytes 19660804
  55.0 4.9 %copy-start = (bf16[5,256,1280]{1,2,0:T(8,128)(2,1)S(1)}, bf16[5,256,1280]{1,2,0:T(8,128)(2,1)}, u32[]{:S(2)}) copy-start(bf16[5,256,1280]{1,2,0:T(8,128)(2,1)} %divide_convert_fusion.2) | copy-start | bytes 9830404
  55.0 4.9 %copy-start.4 = (bf16[256,20,128]{0,2,1:T(8,128)(2,1)S(1)}, bf16[256,20,128]{0,2,1:T(8,128)(2,1)}, u32[]{:S(2)}) copy-start(bf16[256,20,128]{0,2,1:T(8,128)(2,1)} %copy.64) | copy-start | bytes 3932164
  63.4 5.4 %copy-start.5 = (bf16[128,5,256]{2,0,1:T(8,128)(2,1)}, bf16[128,5,256]{2,0,1:T(8,128)(2,1)S(1)}, u32[]{:S(2)}) copy-start(bf16[128,5,256]{2,0,1:T(8,128)(2,1)S(1)} %convolution_convert_fusion.6) | copy-start | bytes 983044
  64.0 4.8 %copy-start.7 = (bf16[128,5,256]{2,0,1:T(8,128)(2,1)}, bf16[128,5,256]{2,0,1:T(8,128)(2,1)S(1)}, u32[]{:S(2)}) copy-start(bf16[128,5,256]{2,0,1:T(8,128)(2,1)S(1)} %convolution_convert_fusion.5) | copy-start | bytes 983044
  83.7 8.8 %collective-permute-start.12 = (bf16[256,4,128]{2,0,1:T(8,128)(2,1)}, bf16[256,4,128]{2,0,1:T(8,128)(2,1)}, u32[]{:S(2)}, u32[]{:S(2)}) collective-permute-start(bf16[256,4,128]{2,0,1:T(8,128)(2,1)} %get-tuple-element.20), channel_id=1, source_target_pairs={{0,1},{1,0},{2,3},{3,2},{4,5},{5,4},{6,7},{7,6},{8,9},{9,8},{10,11... | collective-permute-start | bytes 786440 | tf_op jit(solution)/shard_map/ppermute | solution.py:10
  83.7 10.3 %collective-permute-start.13 = (bf16[256,4,128]{2,0,1:T(8,128)(2,1)}, bf16[256,4,128]{2,0,1:T(8,128)(2,1)}, u32[]{:S(2)}, u32[]{:S(2)}) collective-permute-start(bf16[256,4,128]{2,0,1:T(8,128)(2,1)} %get-tuple-element.19), channel_id=1, source_target_pairs={{0,2},{1,3},{2,0},{3,1},{4,6},{5,7},{6,4},{7,5},{8,10},{9,11},{10,... | collective-permute-start | bytes 786440 | tf_op jit(solution)/shard_map/ppermute | solution.py:10
  84.2 14.1 %collective-permute-start.14 = (bf16[256,4,128]{2,0,1:T(8,128)(2,1)}, bf16[256,4,128]{2,0,1:T(8,128)(2,1)}, u32[]{:S(2)}, u32[]{:S(2)}) collective-permute-start(bf16[256,4,128]{2,0,1:T(8,128)(2,1)} %get-tuple-element.18), channel_id=1, source_target_pairs={{0,4},{1,5},{2,6},{3,7},{4,0},{5,1},{6,2},{7,3},{8,12},{9,13},{10,... | collective-permute-start | bytes 786440 | tf_op jit(solution)/shard_map/ppermute | solution.py:10
  86.7 15.0 %collective-permute-start.15 = (bf16[256,4,128]{2,0,1:T(8,128)(2,1)S(1)}, bf16[256,4,128]{2,0,1:T(8,128)(2,1)}, u32[]{:S(2)}, u32[]{:S(2)}) collective-permute-start(bf16[256,4,128]{2,0,1:T(8,128)(2,1)S(1)} %get-tuple-element.17), channel_id=1, source_target_pairs={{0,8},{1,9},{2,10},{3,11},{4,12},{5,13},{6,14},{7,15},{8,0},{9,1},... | collective-permute-start | bytes 786440 | tf_op jit(solution)/shard_map/ppermute | solution.py:10
  89.1 14.8 %collective-permute-start.8 = (bf16[256,4,128]{2,0,1:T(8,128)(2,1)}, bf16[256,4,128]{2,0,1:T(8,128)(2,1)}, u32[]{:S(2)}, u32[]{:S(2)}) collective-permute-start(bf16[256,4,128]{2,0,1:T(8,128)(2,1)} %get-tuple-element.25), channel_id=1, source_target_pairs={{0,1},{1,0},{2,3},{3,2},{4,5},{5,4},{6,7},{7,6},{8,9},{9,8},{10,11... | collective-permute-start | bytes 786440 | tf_op jit(solution)/shard_map/ppermute | solution.py:10
  92.5 11.5 %collective-permute-start.9 = (bf16[256,4,128]{2,0,1:T(8,128)(2,1)}, bf16[256,4,128]{2,0,1:T(8,128)(2,1)S(1)}, u32[]{:S(2)}, u32[]{:S(2)}) collective-permute-start(bf16[256,4,128]{2,0,1:T(8,128)(2,1)} %get-tuple-element.24), channel_id=1, source_target_pairs={{0,2},{1,3},{2,0},{3,1},{4,6},{5,7},{6,4},{7,5},{8,10},{9,11},{10,... | collective-permute-start | bytes 786440 | tf_op jit(solution)/shard_map/ppermute | solution.py:10
  94.0 15.1 %collective-permute-start.10 = (bf16[256,4,128]{2,0,1:T(8,128)(2,1)}, bf16[256,4,128]{2,0,1:T(8,128)(2,1)S(1)}, u32[]{:S(2)}, u32[]{:S(2)}) collective-permute-start(bf16[256,4,128]{2,0,1:T(8,128)(2,1)} %get-tuple-element.23), channel_id=1, source_target_pairs={{0,4},{1,5},{2,6},{3,7},{4,0},{5,1},{6,2},{7,3},{8,12},{9,13},{10,... | collective-permute-start | bytes 786440 | tf_op jit(solution)/shard_map/ppermute | solution.py:10
  98.3 14.4 %collective-permute-start.11 = (bf16[256,4,128]{2,0,1:T(8,128)(2,1)}, bf16[256,4,128]{2,0,1:T(8,128)(2,1)S(1)}, u32[]{:S(2)}, u32[]{:S(2)}) collective-permute-start(bf16[256,4,128]{2,0,1:T(8,128)(2,1)} %get-tuple-element.22), channel_id=1, source_target_pairs={{0,8},{1,9},{2,10},{3,11},{4,12},{5,13},{6,14},{7,15},{8,0},{9,1},... | collective-permute-start | bytes 786440 | tf_op jit(solution)/shard_map/ppermute | solution.py:10
  (13 other events, 25.7 us)
where the time goes:
time: 115 us
  matrix products  46.5 us (40%)
  local copies, waits for them, and re-layouts  21.4 us (19%)
  starting transfers between devices  18.3 us (16%)
  waiting for transfers between devices  17.1 us (15%)
  other arithmetic  10.4 us (9%)
    sub x4, matrix products, softmax_weights(): masked - top  25.7 us
    dot_general x20, matrix products, product(): return jnp.einsum(form, left, right, preferred_element_type=jnp.float32)  20.8 us
    ppermute x16, starting transfers between devices, from_partner(): return lax.ppermute(value, axis, pairs)  18.3 us
    unnamed x59, local copies, waits for them, and re-layouts  17.3 us
    ppermute x16, waiting for transfers between devices, from_partner(): return lax.ppermute(value, axis, pairs)  17.1 us
    convert_element_type x4, other arithmetic, softmax_weights(): (jnp.where(allowed_mask, jnp.exp(masked - top), 0.0) / total).astype(jnp....  7.25 us
  transfers between devices with their start and end apart: 16, of which 6 were waited for; matrix products, arithmetic and copies ran while one was open for 46% of the time, Pallas kernels for 0%

commit v1 on v0

v1 whole, which is shorter than its diff:
```python
import functools

import jax
import jax.numpy as jnp
from jax import lax
from jax.experimental import pallas as pl
from jax.experimental.pallas import tpu as pltpu
from jax.sharding import PartitionSpec as P

LOG2E = 1.4426950408889634
MASKED = -1e30
CHUNKS = 2
VMEM_LIMIT = 48 * 2**20


def from_partner(value, axis, apart):
    mask = 2**apart
    pairs = [(source, source ^ mask) for source in range(lax.axis_size(axis))]
    return lax.ppermute(value, axis, pairs)


def partner_bits(count):
    level = count.bit_length() - 1
    return (0, 1, level - 2, level - 1)


def product(left, right):
    return lax.dot_general(left, right, (((1,), (0,)), ((), ())), preferred_element_type=jnp.float32)


def product_nt(left, right):
    return lax.dot_general(left, right, (((1,), (1,)), ((), ())), preferred_element_type=jnp.float32)


def attend_kernel(head_group, rows, width, softmax_scale, bits, me_ref, mask_ref, q_ref, do_ref, *refs):
    sources = len(bits) + 1
    kv_refs = refs[:sources]
    o_ref, dq_ref = refs[sources : sources + 2]
    term_refs = refs[sources + 2 : 2 * sources + 2]
    dk_ref, dv_ref = refs[2 * sources + 2 :]
    scale2 = softmax_scale * LOG2E
    me = me_ref[0]
    devices = [me] + [jnp.bitwise_xor(me, 1 << bit) for bit in bits]
    bias = [
        [[jnp.where(mask_ref[a, device * rows + b] > 0, 0.0, MASKED) for b in range(rows)] for a in range(rows)]
        for device in devices
    ]

    def biased(x, s):
        return jnp.concatenate(
            [
                jnp.concatenate(
                    [x[a * width : (a + 1) * width, b * width : (b + 1) * width] + bias[s][a][b] for b in range(rows)],
                    axis=1,
                )
                for a in range(rows)
            ],
            axis=0,
        )

    for g in range(head_group):
        q = q_ref[g]
        do = do_ref[g]
        scores = [biased(product_nt(q, kv_refs[s][0, 0]), s) for s in range(sources)]
        top = jnp.max(functools.reduce(jnp.maximum, scores), axis=1, keepdims=True) * scale2
        exps = [jnp.exp2(x * scale2 - top) for x in scores]
        total = jnp.sum(functools.reduce(jnp.add, exps), axis=1, keepdims=True)
        inverse = 1.0 / total
        narrow = [e.astype(jnp.bfloat16) for e in exps]
        attended = functools.reduce(jnp.add, [product(narrow[s], kv_refs[s][1, 0]) for s in range(sources)])
        attended = (attended * inverse).astype(jnp.bfloat16)
        o_ref[g] = attended
        wide_do = do.astype(jnp.float32)
        delta = jnp.sum(wide_do * attended.astype(jnp.float32), axis=1, keepdims=True)
        q_scaled = (q.astype(jnp.float32) * (inverse * softmax_scale)).astype(jnp.bfloat16).T
        do_scaled = (wide_do * inverse).astype(jnp.bfloat16).T
        grad_q = 0.0
        for s in range(sources):
            dprob = product_nt(do, kv_refs[s][1, 0])
            dscore = (exps[s] * (dprob - delta)).astype(jnp.bfloat16)
            grad_q = grad_q + product(dscore, kv_refs[s][0, 0])
            dk = product(q_scaled, dscore)
            dv = product(do_scaled, narrow[s])
            if g == 0:
                dk_ref[s] = dk
                dv_ref[s] = dv
            else:
                dk_ref[s] += dk
                dv_ref[s] += dv
        dq_ref[g] = (grad_q * (inverse * softmax_scale)).astype(jnp.bfloat16)
    for s in range(sources):
        term_refs[s][0, 0] = dk_ref[s].T.astype(jnp.bfloat16)
        term_refs[s][1, 0] = dv_ref[s].T.astype(jnp.bfloat16)


def attend(me, block_mask, queries, output_gradient, kvs, first, width, bits):
    heads_all, tokens, size = queries.shape
    n = kvs[0].shape[1]
    head_group = heads_all // (CHUNKS * n)
    sources = len(kvs)
    rows = block_mask.shape[0]
    rows_in = pl.BlockSpec((head_group, tokens, size), lambda j: (first + j, 0, 0))
    rows_out = pl.BlockSpec((head_group, tokens, size), lambda j: (j, 0, 0))
    term = pl.BlockSpec((2, 1, tokens, size), lambda j: (0, j, 0, 0))
    smem = pl.BlockSpec(memory_space=pltpu.SMEM)
    out = jax.ShapeDtypeStruct((n * head_group, tokens, size), jnp.bfloat16)
    term_out = jax.ShapeDtypeStruct((2, n, tokens, size), jnp.bfloat16)
    body = functools.partial(attend_kernel, head_group, rows, width, size ** (-0.5), bits)
    scores = n * head_group * tokens * sources * tokens
    return pl.pallas_call(
        body,
        grid=(n,),
        in_specs=[smem, smem, rows_in, rows_in] + [term] * sources,
        out_specs=[rows_out, rows_out] + [term] * sources,
        out_shape=[out, out] + [term_out] * sources,
        scratch_shapes=[pltpu.VMEM((sources, size, tokens), jnp.float32)] * 2,
        compiler_params=pltpu.CompilerParams(vmem_limit_bytes=VMEM_LIMIT),
        cost_estimate=pl.CostEstimate(
            flops=12 * scores * size, bytes_accessed=8 * n * head_group * tokens * size, transcendentals=scores
        ),
    )(me, block_mask, queries, output_gradient, *kvs)


def shards(block_mask, queries, keys, values, output_gradient):
    count = lax.axis_size("seq")
    me = lax.axis_index("seq").astype(jnp.int32).reshape(1)
    width = queries.shape[0] // block_mask.shape[0]
    kv_heads = keys.shape[1]
    bits = partner_bits(count)
    q = jnp.transpose(queries, (1, 0, 2))
    dout = jnp.transpose(output_gradient, (1, 0, 2))
    per = kv_heads // CHUNKS
    own = [
        jnp.stack([jnp.transpose(x[:, c * per : (c + 1) * per], (1, 0, 2)) for x in (keys, values)])
        for c in range(CHUNKS)
    ]
    fetched = [[own[c]] + [from_partner(own[c], "seq", bit) for bit in bits] for c in range(CHUNKS)]
    results = [attend(me, block_mask, q, dout, fetched[c], c * per, width, bits) for c in range(CHUNKS)]
    grads = []
    for c in range(CHUNKS):
        terms = results[c][2:]
        total = terms[0].astype(jnp.float32)
        for bit, term in zip(bits, terms[1:]):
            total = total + from_partner(term, "seq", bit).astype(jnp.float32)
        grads.append(total.astype(jnp.bfloat16))
    both = jnp.concatenate(grads, axis=1)
    attended = jnp.transpose(jnp.concatenate([r[0] for r in results], axis=0), (1, 0, 2))
    grad_q = jnp.transpose(jnp.concatenate([r[1] for r in results], axis=0), (1, 0, 2))
    return (attended, grad_q, jnp.transpose(both[0], (1, 0, 2)), jnp.transpose(both[1], (1, 0, 2)))


def solution(mesh):
    rows = P(("groups", "seq"), None)
    cube = P(("groups", "seq"), None, None)
    return jax.shard_map(
        shards,
        mesh=mesh,
        in_specs=(rows, cube, cube, cube, cube),
        out_specs=(cube, cube, cube, cube),
        check_vma=False,
    )
```

time: 115 us -> 85.7 us (0.75)
  matrix products: 46.5 us -> 0 us
  Pallas kernels: 0 us -> 35.6 us
  local copies, waits for them, and re-layouts: 21.4 us -> 4.53 us
  other arithmetic: 10.4 us -> 2.79 us
  waiting for transfers between devices: 17.1 us -> 21.2 us
  starting transfers between devices: 18.3 us -> 20.6 us
    pallas_call x0 -> x2, Pallas kernels: none -> 35.6 us  [attend(): pl.pallas_call(body, grid=(n,), in_specs=[smem, smem, rows_in, rows_in] +...]
    sub x4 -> x0, matrix products: 25.7 us -> none  [softmax_weights(): masked - top]
    dot_general x20 -> x0, matrix products: 20.8 us -> none  [product(): return jnp.einsum(form, left, right, preferred_element_type=jnp.float32)]
    unnamed x59 -> x6, local copies, waits for them, and re-layouts: 17.3 us -> 1.83 us
    convert_element_type x6 -> x2, other arithmetic: 9.74 us -> 0.35 us  [shards(): grads.append(total.astype(jnp.bfloat16))]
    ppermute x16, waiting for transfers between devices: 17.1 us -> 21.2 us  [from_partner(): return lax.ppermute(value, axis, pairs)]
    transpose x0 -> x3, other arithmetic: none -> 2.39 us  [the longest x1 1.17 us: shards(): jnp.transpose(jnp.concatenate([r[0] for r in results], axis=0), (1, 0, 2))]
    ppermute x16, starting transfers between devices: 18.3 us -> 20.6 us  [from_partner(): return lax.ppermute(value, axis, pairs)]
  transfers between devices with their start and end apart: 16 -> 16, of which waited for: 6 -> 3; matrix products, arithmetic and copies ran while one was open for 46% -> 3% of each run, Pallas kernels for 0% -> 42%
where the time goes in v1:
time: 85.7 us; the launch traced here: 85.5 us
  Pallas kernels  35.6 us (42%)
  waiting for transfers between devices  21.2 us (25%)
  starting transfers between devices  20.6 us (24%)
  local copies, waits for them, and re-layouts  4.53 us (5%)
  other arithmetic  2.79 us (3%)
    pallas_call x2, Pallas kernels, attend(): pl.pallas_call(body, grid=(n,), in_specs=[smem, smem, rows_in, rows_in] +...  35.6 us
    ppermute x16, waiting for transfers between devices, from_partner(): return lax.ppermute(value, axis, pairs)  21.2 us
    ppermute x16, starting transfers between devices, from_partner(): return lax.ppermute(value, axis, pairs)  20.6 us
    slice x2, local copies, waits for them, and re-layouts, shards(): x[:, c * per:(c + 1) * per]  2.63 us
    unnamed x6, local copies, waits for them, and re-layouts  1.83 us
  transfers between devices with their start and end apart: 16, of which 3 were waited for; matrix products, arithmetic and copies ran while one was open for 3% of the time, Pallas kernels for 42%

profile of v1, /device:TPU:0, one launch (start us, length us, event | category | flops | bytes accessed | tf_op | source)
XLA Modules:
  0.0 85.5 jit_solution(16673523328564090417)
XLA Ops:
  0.6 1.3 %fusion.3 = (bf16[256,2,128]{2,1,0:T(2,128)(2,1)S(1)}, bf16[256,2,128]{2,1,0:T(2,128)(2,1)S(1)}) fusion(bf16[256,4,128]{2,1,0:T(4,128)(2,1)} %param.7), kind=kLoop, calls=%fused_computation.16 | loop fusion | bytes 524288 | tf_op jit(solution)/shard_map/slice | solution.py:134
  1.9 1.4 %fusion.4 = (bf16[256,2,128]{2,1,0:T(2,128)(2,1)S(1)}, bf16[256,2,128]{2,1,0:T(2,128)(2,1)S(1)}) fusion(bf16[256,4,128]{2,1,0:T(4,128)(2,1)} %param.8), kind=kLoop, calls=%fused_computation.17 | loop fusion | bytes 524288 | tf_op jit(solution)/shard_map/slice | solution.py:134
  3.4 4.1 %collective-permute-start.3 = (bf16[2,2,256,128]{3,2,1,0:T(8,128)(2,1)S(1)}, bf16[2,2,256,128]{3,2,1,0:T(8,128)(2,1)S(1)}, u32[]{:S(2)}, u32[]{:S(2)}) collective-permute-start(bf16[2,2,256,128]{3,2,1,0:T(8,128)(2,1)S(1)} %pad_maximum_fusion.1.refs_0_), channel_id=1, source_target_pairs={{0,8},{1,9},{2,10},{3,11},{4,12},{5,13},{6,14},{7,15},{8,0},{9,1},... | collective-permute-start | bytes 786440 | tf_op jit(solution)/shard_map/ppermute | solution.py:19
  7.5 1.6 %collective-permute-start.2 = (bf16[2,2,256,128]{3,2,1,0:T(8,128)(2,1)S(1)}, bf16[2,2,256,128]{3,2,1,0:T(8,128)(2,1)S(1)}, u32[]{:S(2)}, u32[]{:S(2)}) collective-permute-start(bf16[2,2,256,128]{3,2,1,0:T(8,128)(2,1)S(1)} %pad_maximum_fusion.1.refs_0_), channel_id=1, source_target_pairs={{0,4},{1,5},{2,6},{3,7},{4,0},{5,1},{6,2},{7,3},{8,12},{9,13},{10,... | collective-permute-start | bytes 786440 | tf_op jit(solution)/shard_map/ppermute | solution.py:19
  9.0 1.5 %collective-permute-start.1 = (bf16[2,2,256,128]{3,2,1,0:T(8,128)(2,1)S(1)}, bf16[2,2,256,128]{3,2,1,0:T(8,128)(2,1)S(1)}, u32[]{:S(2)}, u32[]{:S(2)}) collective-permute-start(bf16[2,2,256,128]{3,2,1,0:T(8,128)(2,1)S(1)} %pad_maximum_fusion.1.refs_0_), channel_id=1, source_target_pairs={{0,2},{1,3},{2,0},{3,1},{4,6},{5,7},{6,4},{7,5},{8,10},{9,11},{10,... | collective-permute-start | bytes 786440 | tf_op jit(solution)/shard_map/ppermute | solution.py:19
  10.6 0.4 collective-permute-start.7
  11.0 10.1 %collective-permute-done.3.refs_4_ = bf16[2,2,256,128]{3,2,1,0:T(8,128)(2,1)S(1)} collective-permute-done((bf16[2,2,256,128]{3,2,1,0:T(8,128)(2,1)S(1)}, bf16[2,2,256,128]{3,2,1,0:T(8,128)(2,1)S(1)}, u32[]{:S(2)}, u32[]{:S(2)}) %collective-permute-start.3) | collective-permute-done | bytes 262176 | tf_op jit(solution)/shard_map/ppermute | solution.py:19
  21.1 5.6 %collective-permute-start.5 = (bf16[2,2,256,128]{3,2,1,0:T(8,128)(2,1)S(1)}, bf16[2,2,256,128]{3,2,1,0:T(8,128)(2,1)S(1)}, u32[]{:S(2)}, u32[]{:S(2)}) collective-permute-start(bf16[2,2,256,128]{3,2,1,0:T(8,128)(2,1)S(1)} %pad_maximum_fusion.2.refs_0_), channel_id=1, source_target_pairs={{0,2},{1,3},{2,0},{3,1},{4,6},{5,7},{6,4},{7,5},{8,10},{9,11},{10,... | collective-permute-start | bytes 786440 | tf_op jit(solution)/shard_map/ppermute | solution.py:19
  26.7 17.7 %shard_map.84 = (bf16[10,256,128]{2,1,0:T(8,128)(2,1)S(1)}, bf16[10,256,128]{2,1,0:T(8,128)(2,1)S(1)}, bf16[2,2,256,128]{3,2,1,0:T(8,128)(2,1)S(1)}, bf16[2,2,25...) custom-call(s32[1]{0:T(128)} %bitcast.me_ref, ...), custom_call_target="tpu_custom_call" | custom-call | flops 5033164800 | bytes 2621440 | tf_op jit(solution)/shard_map/pallas_call | solution.py:110
  44.5 0.6 collective-permute-start.8
  45.0 0.1 collective-permute-start.9
  45.1 2.0 %collective-permute-start.10 = (bf16[2,2,256,128]{3,2,1,0:T(8,128)(2,1)S(1)}, bf16[2,2,256,128]{3,2,1,0:T(8,128)(2,1)S(1)}, u32[]{:S(2)}, u32[]{:S(2)}) collective-permute-start(bf16[2,2,256,128]{3,2,1,0:T(8,128)(2,1)S(1)} %get-tuple-element.25), channel_id=1, source_target_pairs={{0,4},{1,5},{2,6},{3,7},{4,0},{5,1},{6,2},{7,3},{8,12},{9,13},{10,... | collective-permute-start | bytes 786440 | tf_op jit(solution)/shard_map/ppermute | solution.py:19
  47.1 17.9 %shard_map.85 = (bf16[10,256,128]{2,1,0:T(8,128)(2,1)S(1)}, bf16[10,256,128]{2,1,0:T(8,128)(2,1)S(1)}, bf16[2,2,256,128]{3,2,1,0:T(8,128)(2,1)S(1)}, bf16[2,2,25...) custom-call(s32[1]{0:T(128)} %bitcast.me_ref, ...), custom_call_target="tpu_custom_call" | custom-call | flops 5033164800 | bytes 2621440 | tf_op jit(solution)/shard_map/pallas_call | solution.py:110
  65.1 1.2 %maximum_bitcast_fusion = bf16[256,20,128]{2,0,1:T(8,128)(2,1)} fusion(bf16[10,256,128]{2,1,0:T(8,128)(2,1)S(1)} %get-tuple-element.19, bf16[10,256,128]{2,1,0:T(8,128)(2,1)S(1)} %get-tuple-element.18), kind=kLoop, calls=%fused_computation | loop fusion | flops 655360 | bytes 2621440 | tf_op jit(solution)/shard_map/transpose | solution.py:147
  66.3 1.2 %maximum_bitcast_fusion.1 = bf16[256,20,128]{2,0,1:T(8,128)(2,1)} fusion(bf16[10,256,128]{2,1,0:T(8,128)(2,1)S(1)} %get-tuple-element.21, bf16[10,256,128]{2,1,0:T(8,128)(2,1)S(1)} %get-tuple-element.20), kind=kLoop, calls=%fused_computation.1 | loop fusion | flops 655360 | bytes 2621440 | tf_op jit(solution)/shard_map/transpose | solution.py:148
  67.5 2.0 %collective-permute-start.13 = (bf16[2,2,256,128]{3,2,1,0:T(8,128)(2,1)S(1)}, bf16[2,2,256,128]{3,2,1,0:T(8,128)(2,1)S(1)}, u32[]{:S(2)}, u32[]{:S(2)}) collective-permute-start(bf16[2,2,256,128]{3,2,1,0:T(8,128)(2,1)S(1)} %get-tuple-element.29), channel_id=1, source_target_pairs={{0,2},{1,3},{2,0},{3,1},{4,6},{5,7},{6,4},{7,5},{8,10},{9,11},{10,... | collective-permute-start | bytes 786440 | tf_op jit(solution)/shard_map/ppermute | solution.py:19
  69.4 0.1 collective-permute-start.14
  69.5 2.7 %collective-permute-start.15 = (bf16[2,2,256,128]{3,2,1,0:T(8,128)(2,1)S(1)}, bf16[2,2,256,128]{3,2,1,0:T(8,128)(2,1)S(1)}, u32[]{:S(2)}, u32[]{:S(2)}) collective-permute-start(bf16[2,2,256,128]{3,2,1,0:T(8,128)(2,1)S(1)} %get-tuple-element.31), channel_id=1, source_target_pairs={{0,8},{1,9},{2,10},{3,11},{4,12},{5,13},{6,14},{7,15},{8,0},{9,1},... | collective-permute-start | bytes 786440 | tf_op jit(solution)/shard_map/ppermute | solution.py:19
  72.2 0.2 add_convert_fusion.1
  72.4 4.0 %collective-permute-done.13 = bf16[2,2,256,128]{3,2,1,0:T(8,128)(2,1)S(1)} collective-permute-done((bf16[2,2,256,128]{3,2,1,0:T(8,128)(2,1)S(1)}, bf16[2,2,256,128]{3,2,1,0:T(8,128)(2,1)S(1)}, u32[]{:S(2)}, u32[]{:S(2)}) %collective-permute-start.13) | collective-permute-done | bytes 262176 | tf_op jit(solution)/shard_map/ppermute | solution.py:19
  76.4 7.1 %collective-permute-done.14 = bf16[2,2,256,128]{3,2,1,0:T(8,128)(2,1)S(1)} collective-permute-done((bf16[2,2,256,128]{3,2,1,0:T(8,128)(2,1)S(1)}, bf16[2,2,256,128]{3,2,1,0:T(8,128)(2,1)S(1)}, u32[]{:S(2)}, u32[]{:S(2)}) %collective-permute-start.14) | collective-permute-done | bytes 262176 | tf_op jit(solution)/shard_map/ppermute | solution.py:19
  83.5 0.2 add_convert_fusion
  83.7 0.9 %copy.14 = bf16[256,4,128]{2,1,0:T(4,128)(2,1)} copy(bf16[256,4,128]{2,0,1:T(8,128)(2,1)S(1)} %get-tuple-element.36) | data formatting | bytes 524288
  84.6 0.9 %copy.13 = bf16[256,4,128]{2,1,0:T(4,128)(2,1)} copy(bf16[256,4,128]{2,0,1:T(8,128)(2,1)S(1)} %get-tuple-element.37) | data formatting | bytes 524288
  (27 shorter events, 0.3 us)
Async XLA Ops:
  1.9 24.8 %copy-start = (bf16[256,20,128]{2,0,1:T(8,128)(2,1)S(1)}, bf16[256,20,128]{2,0,1:T(8,128)(2,1)}, u32[]{:S(2)}) copy-start(bf16[256,20,128]{2,0,1:T(8,128)(2,1)} %param.6) | copy-start | bytes 3932164
  1.9 24.8 %copy-start.1 = (s32[2,32]{1,0:T(2,128)S(1)}, s32[2,32]{1,0:T(2,128)}, u32[]{:S(2)}) copy-start(s32[2,32]{1,0:T(2,128)} %mask_ref.3) | copy-start | bytes 772
  3.4 17.8 %collective-permute-start.3 = (bf16[2,2,256,128]{3,2,1,0:T(8,128)(2,1)S(1)}, bf16[2,2,256,128]{3,2,1,0:T(8,128)(2,1)S(1)}, u32[]{:S(2)}, u32[]{:S(2)}) collective-permute-start(bf16[2,2,256,128]{3,2,1,0:T(8,128)(2,1)S(1)} %pad_maximum_fusion.1.refs_0_), channel_id=1, source_target_pairs={{0,8},{1,9},{2,10},{3,11},{4,12},{5,13},{6,14},{7,15},{8,0},{9,1},... | collective-permute-start | bytes 786440 | tf_op jit(solution)/shard_map/ppermute | solution.py:19
  7.5 13.7 %collective-permute-start.2 = (bf16[2,2,256,128]{3,2,1,0:T(8,128)(2,1)S(1)}, bf16[2,2,256,128]{3,2,1,0:T(8,128)(2,1)S(1)}, u32[]{:S(2)}, u32[]{:S(2)}) collective-permute-start(bf16[2,2,256,128]{3,2,1,0:T(8,128)(2,1)S(1)} %pad_maximum_fusion.1.refs_0_), channel_id=1, source_target_pairs={{0,4},{1,5},{2,6},{3,7},{4,0},{5,1},{6,2},{7,3},{8,12},{9,13},{10,... | collective-permute-start | bytes 786440 | tf_op jit(solution)/shard_map/ppermute | solution.py:19
  9.0 17.7 %collective-permute-start.1 = (bf16[2,2,256,128]{3,2,1,0:T(8,128)(2,1)S(1)}, bf16[2,2,256,128]{3,2,1,0:T(8,128)(2,1)S(1)}, u32[]{:S(2)}, u32[]{:S(2)}) collective-permute-start(bf16[2,2,256,128]{3,2,1,0:T(8,128)(2,1)S(1)} %pad_maximum_fusion.1.refs_0_), channel_id=1, source_target_pairs={{0,2},{1,3},{2,0},{3,1},{4,6},{5,7},{6,4},{7,5},{8,10},{9,11},{10,... | collective-permute-start | bytes 786440 | tf_op jit(solution)/shard_map/ppermute | solution.py:19
  10.6 16.2 %collective-permute-start = (bf16[2,2,256,128]{3,2,1,0:T(8,128)(2,1)S(1)}, bf16[2,2,256,128]{3,2,1,0:T(8,128)(2,1)S(1)}, u32[]{:S(2)}, u32[]{:S(2)}) collective-permute-start(bf16[2,2,256,128]{3,2,1,0:T(8,128)(2,1)S(1)} %pad_maximum_fusion.1.refs_0_), channel_id=1, source_target_pairs={{0,1},{1,0},{2,3},{3,2},{4,5},{5,4},{6,7},{7,6},{8,9},{9,8},{10,11... | collective-permute-start | bytes 786440 | tf_op jit(solution)/shard_map/ppermute | solution.py:19
  10.6 34.4 %collective-permute-start.7 = (bf16[2,2,256,128]{3,2,1,0:T(8,128)(2,1)S(1)}, bf16[2,2,256,128]{3,2,1,0:T(8,128)(2,1)S(1)}, u32[]{:S(2)}, u32[]{:S(2)}) collective-permute-start(bf16[2,2,256,128]{3,2,1,0:T(8,128)(2,1)S(1)} %pad_maximum_fusion.2.refs_0_), channel_id=1, source_target_pairs={{0,8},{1,9},{2,10},{3,11},{4,12},{5,13},{6,14},{7,15},{8,0},{9,1},... | collective-permute-start | bytes 786440 | tf_op jit(solution)/shard_map/ppermute | solution.py:19
  21.1 24.0 %collective-permute-start.6 = (bf16[2,2,256,128]{3,2,1,0:T(8,128)(2,1)S(1)}, bf16[2,2,256,128]{3,2,1,0:T(8,128)(2,1)S(1)}, u32[]{:S(2)}, u32[]{:S(2)}) collective-permute-start(bf16[2,2,256,128]{3,2,1,0:T(8,128)(2,1)S(1)} %pad_maximum_fusion.2.refs_0_), channel_id=1, source_target_pairs={{0,4},{1,5},{2,6},{3,7},{4,0},{5,1},{6,2},{7,3},{8,12},{9,13},{10,... | collective-permute-start | bytes 786440 | tf_op jit(solution)/shard_map/ppermute | solution.py:19
  21.1 26.0 %collective-permute-start.5 = (bf16[2,2,256,128]{3,2,1,0:T(8,128)(2,1)S(1)}, bf16[2,2,256,128]{3,2,1,0:T(8,128)(2,1)S(1)}, u32[]{:S(2)}, u32[]{:S(2)}) collective-permute-start(bf16[2,2,256,128]{3,2,1,0:T(8,128)(2,1)S(1)} %pad_maximum_fusion.2.refs_0_), channel_id=1, source_target_pairs={{0,2},{1,3},{2,0},{3,1},{4,6},{5,7},{6,4},{7,5},{8,10},{9,11},{10,... | collective-permute-start | bytes 786440 | tf_op jit(solution)/shard_map/ppermute | solution.py:19
  26.7 20.4 %collective-permute-start.4 = (bf16[2,2,256,128]{3,2,1,0:T(8,128)(2,1)S(1)}, bf16[2,2,256,128]{3,2,1,0:T(8,128)(2,1)S(1)}, u32[]{:S(2)}, u32[]{:S(2)}) collective-permute-start(bf16[2,2,256,128]{3,2,1,0:T(8,128)(2,1)S(1)} %pad_maximum_fusion.2.refs_0_), channel_id=1, source_target_pairs={{0,1},{1,0},{2,3},{3,2},{4,5},{5,4},{6,7},{7,6},{8,9},{9,8},{10,11... | collective-permute-start | bytes 786440 | tf_op jit(solution)/shard_map/ppermute | solution.py:19
  44.5 23.0 %collective-permute-start.8 = (bf16[2,2,256,128]{3,2,1,0:T(8,128)(2,1)S(1)}, bf16[2,2,256,128]{3,2,1,0:T(8,128)(2,1)S(1)}, u32[]{:S(2)}, u32[]{:S(2)}) collective-permute-start(bf16[2,2,256,128]{3,2,1,0:T(8,128)(2,1)S(1)} %get-tuple-element.23), channel_id=1, source_target_pairs={{0,1},{1,0},{2,3},{3,2},{4,5},{5,4},{6,7},{7,6},{8,9},{9,8},{10,11... | collective-permute-start | bytes 786440 | tf_op jit(solution)/shard_map/ppermute | solution.py:19
  45.0 24.4 %collective-permute-start.9 = (bf16[2,2,256,128]{3,2,1,0:T(8,128)(2,1)S(1)}, bf16[2,2,256,128]{3,2,1,0:T(8,128)(2,1)S(1)}, u32[]{:S(2)}, u32[]{:S(2)}) collective-permute-start(bf16[2,2,256,128]{3,2,1,0:T(8,128)(2,1)S(1)} %get-tuple-element.24), channel_id=1, source_target_pairs={{0,2},{1,3},{2,0},{3,1},{4,6},{5,7},{6,4},{7,5},{8,10},{9,11},{10,... | collective-permute-start | bytes 786440 | tf_op jit(solution)/shard_map/ppermute | solution.py:19
  45.1 24.4 %collective-permute-start.10 = (bf16[2,2,256,128]{3,2,1,0:T(8,128)(2,1)S(1)}, bf16[2,2,256,128]{3,2,1,0:T(8,128)(2,1)S(1)}, u32[]{:S(2)}, u32[]{:S(2)}) collective-permute-start(bf16[2,2,256,128]{3,2,1,0:T(8,128)(2,1)S(1)} %get-tuple-element.25), channel_id=1, source_target_pairs={{0,4},{1,5},{2,6},{3,7},{4,0},{5,1},{6,2},{7,3},{8,12},{9,13},{10,... | collective-permute-start | bytes 786440 | tf_op jit(solution)/shard_map/ppermute | solution.py:19
  47.1 25.1 %collective-permute-start.11 = (bf16[2,2,256,128]{3,2,1,0:T(8,128)(2,1)S(1)}, bf16[2,2,256,128]{3,2,1,0:T(8,128)(2,1)S(1)}, u32[]{:S(2)}, u32[]{:S(2)}) collective-permute-start(bf16[2,2,256,128]{3,2,1,0:T(8,128)(2,1)S(1)} %get-tuple-element.26), channel_id=1, source_target_pairs={{0,8},{1,9},{2,10},{3,11},{4,12},{5,13},{6,14},{7,15},{8,0},{9,1},... | collective-permute-start | bytes 786440 | tf_op jit(solution)/shard_map/ppermute | solution.py:19
  65.1 7.4 %collective-permute-start.12 = (bf16[2,2,256,128]{3,2,1,0:T(8,128)(2,1)S(1)}, bf16[2,2,256,128]{3,2,1,0:T(8,128)(2,1)S(1)}, u32[]{:S(2)}, u32[]{:S(2)}) collective-permute-start(bf16[2,2,256,128]{3,2,1,0:T(8,128)(2,1)S(1)} %get-tuple-element.28), channel_id=1, source_target_pairs={{0,1},{1,0},{2,3},{3,2},{4,5},{5,4},{6,7},{7,6},{8,9},{9,8},{10,11... | collective-permute-start | bytes 786440 | tf_op jit(solution)/shard_map/ppermute | solution.py:19
  67.5 8.9 %collective-permute-start.13 = (bf16[2,2,256,128]{3,2,1,0:T(8,128)(2,1)S(1)}, bf16[2,2,256,128]{3,2,1,0:T(8,128)(2,1)S(1)}, u32[]{:S(2)}, u32[]{:S(2)}) collective-permute-start(bf16[2,2,256,128]{3,2,1,0:T(8,128)(2,1)S(1)} %get-tuple-element.29), channel_id=1, source_target_pairs={{0,2},{1,3},{2,0},{3,1},{4,6},{5,7},{6,4},{7,5},{8,10},{9,11},{10,... | collective-permute-start | bytes 786440 | tf_op jit(solution)/shard_map/ppermute | solution.py:19
  69.4 14.0 %collective-permute-start.14 = (bf16[2,2,256,128]{3,2,1,0:T(8,128)(2,1)S(1)}, bf16[2,2,256,128]{3,2,1,0:T(8,128)(2,1)S(1)}, u32[]{:S(2)}, u32[]{:S(2)}) collective-permute-start(bf16[2,2,256,128]{3,2,1,0:T(8,128)(2,1)S(1)} %get-tuple-element.30), channel_id=1, source_target_pairs={{0,4},{1,5},{2,6},{3,7},{4,0},{5,1},{6,2},{7,3},{8,12},{9,13},{10,... | collective-permute-start | bytes 786440 | tf_op jit(solution)/shard_map/ppermute | solution.py:19
  69.5 14.0 %collective-permute-start.15 = (bf16[2,2,256,128]{3,2,1,0:T(8,128)(2,1)S(1)}, bf16[2,2,256,128]{3,2,1,0:T(8,128)(2,1)S(1)}, u32[]{:S(2)}, u32[]{:S(2)}) collective-permute-start(bf16[2,2,256,128]{3,2,1,0:T(8,128)(2,1)S(1)} %get-tuple-element.31), channel_id=1, source_target_pairs={{0,8},{1,9},{2,10},{3,11},{4,12},{5,13},{6,14},{7,15},{8,0},{9,1},... | collective-permute-start | bytes 786440 | tf_op jit(solution)/shard_map/ppermute | solution.py:19

commit v2 on v1

v2 whole, which is shorter than its diff:
```python
import functools

import jax
import jax.numpy as jnp
from jax import lax
from jax.experimental import pallas as pl
from jax.experimental.pallas import tpu as pltpu
from jax.sharding import PartitionSpec as P

LOG2E = 1.4426950408889634
MASKED = -1e30
VMEM_LIMIT = 24 * 2**20
FETCH = (((0, 4),), ((0, 4),), ((0, 2), (2, 4)), ((0, 2), (2, 4)))
RETURN = (((0, 4),), ((0, 4),), ((0, 2), (2, 4)), ((0, 2), (2, 4)))
KERNELS = ((0, 2), (2, 4))


def from_partner(value, axis, apart):
    mask = 2**apart
    pairs = [(source, source ^ mask) for source in range(lax.axis_size(axis))]
    return lax.ppermute(value, axis, pairs)


def partner_bits(count):
    level = count.bit_length() - 1
    return (0, 1, level - 2, level - 1)


def group_of(groups, head):
    return next(g for g in groups if g[0] <= head < g[1])


def product(left, right):
    return lax.dot_general(left, right, (((1,), (0,)), ((), ())), preferred_element_type=jnp.float32)


def product_nt(left, right):
    return lax.dot_general(left, right, (((1,), (1,)), ((), ())), preferred_element_type=jnp.float32)


VMEM = pl.BlockSpec(memory_space=pltpu.VMEM)
SMEM = pl.BlockSpec(memory_space=pltpu.SMEM)
ANY = pl.BlockSpec(memory_space=pl.ANY)
HBM = pl.BlockSpec(memory_space=pltpu.HBM)


def in_hbm(array):
    return pltpu.with_memory_space_constraint(array, pltpu.HBM)


def pack_kernel(groups, bits, me_ref, mask_ref, k_ref, v_ref, bias_ref, *refs):
    outs, wide_ref = refs[:-1], refs[-1]
    tokens, heads, size = k_ref.shape
    for i, ref in enumerate((k_ref, v_ref)):
        wide_ref[i] = ref[...].astype(jnp.float32).reshape(tokens * heads, size)
        for h in range(heads):
            rows = wide_ref[i, pl.ds(h, tokens, stride=heads), :].astype(jnp.bfloat16)
            for (low, high), out in zip(groups, outs):
                if low <= h < high:
                    out[h - low, i] = rows
    me = me_ref[0]
    blocks, columns = mask_ref.shape
    mask = mask_ref[...]
    column = lax.broadcasted_iota(jnp.int32, (blocks, columns), 1)
    for s, device in enumerate([me] + [jnp.bitwise_xor(me, 1 << bit) for bit in bits]):
        for b in range(blocks):
            ones = jnp.sum(jnp.where(column == device * blocks + b, mask, 0), axis=1, keepdims=True)
            width = tokens // blocks
            bias_ref[s, :, b * width : (b + 1) * width] = jnp.broadcast_to(
                jnp.where(ones > 0, 0.0, MASKED), (blocks, width)
            )


def pack(me, block_mask, keys, values, groups, bits):
    tokens, heads, size = keys.shape
    bias = jax.ShapeDtypeStruct((len(bits) + 1, block_mask.shape[0], tokens), jnp.float32)
    return pl.pallas_call(
        functools.partial(pack_kernel, groups, bits),
        in_specs=[SMEM] + [VMEM] * 3,
        out_specs=[VMEM] * (len(groups) + 1),
        out_shape=[bias]
        + [jax.ShapeDtypeStruct((high - low, 2, tokens, size), keys.dtype) for low, high in groups],
        scratch_shapes=[pltpu.VMEM((2, tokens * heads, size), jnp.float32)],
        compiler_params=pltpu.CompilerParams(vmem_limit_bytes=VMEM_LIMIT),
        cost_estimate=pl.CostEstimate(flops=0, bytes_accessed=6 * keys.size * 2, transcendentals=0),
    )(me, in_hbm(block_mask), in_hbm(keys), in_hbm(values))


def sum_kernel(groups, *refs):
    terms, (dk_ref, dv_ref, wide_ref) = refs[: len(groups)], refs[len(groups) :]
    tokens, heads, size = dk_ref.shape
    for i, ref in enumerate((dk_ref, dv_ref)):
        for h in range(heads):
            parts = [t[h - g[0], i].astype(jnp.float32) for g, t in zip(groups, terms) if g[0] <= h < g[1]]
            wide_ref[i, pl.ds(h, tokens, stride=heads), :] = functools.reduce(jnp.add, parts)
        ref[...] = wide_ref[i].astype(ref.dtype).reshape(tokens, heads, size)


def sum_terms(groups, terms, tokens, heads, size):
    out = jax.ShapeDtypeStruct((tokens, heads, size), jnp.bfloat16)
    return pl.pallas_call(
        functools.partial(sum_kernel, groups),
        in_specs=[VMEM] * len(groups),
        out_specs=[VMEM] * 2,
        out_shape=[out, out],
        scratch_shapes=[pltpu.VMEM((2, tokens * heads, size), jnp.float32)],
        compiler_params=pltpu.CompilerParams(vmem_limit_bytes=VMEM_LIMIT),
        cost_estimate=pl.CostEstimate(flops=0, bytes_accessed=12 * tokens * heads * size * 2, transcendentals=0),
    )(*terms)


def attend_kernel(sources, softmax_scale, unused, bias_ref, q_ref, do_ref, *refs):
    kv_refs = refs[:sources]
    refs = refs[sources + unused :]
    o_ref, dq_ref = refs[:2]
    term_refs = refs[2 : sources + 2]
    dk_ref, dv_ref, x_ref, e_ref, p_ref = refs[sources + 2 :]
    scale2 = softmax_scale * LOG2E
    blocks = bias_ref.shape[1]
    width = bias_ref.shape[2] // blocks
    head_group = q_ref.shape[0]
    state = {}

    def key(s):
        return kv_refs[s][0, 0]

    def value(s):
        return kv_refs[s][0, 1]

    def scores(g, s):
        x = product_nt(q_ref[g], key(s))
        x = jnp.concatenate([x[a * width : (a + 1) * width] + bias_ref[s, a : a + 1] for a in range(blocks)], axis=0)
        x_ref[g % 2, s] = x
        state["max", g] = jnp.maximum(state["max", g], x) if s else x
        p_ref[g % 2, s] = product_nt(do_ref[g], value(s))

    def scores_end(g):
        state["top", g] = jnp.max(state.pop(("max", g)), axis=1, keepdims=True) * scale2

    def forward(g, s):
        e = jnp.exp2(x_ref[g % 2, s] * scale2 - state["top", g])
        narrow = e.astype(jnp.bfloat16)
        e_ref[g % 2, s] = narrow
        state["total", g] = state["total", g] + e if s else e
        part = product(narrow, value(s))
        state["out", g] = state["out", g] + part if s else part

    def forward_end(g):
        q, do = q_ref[g], do_ref[g].astype(jnp.float32)
        inverse = 1.0 / jnp.sum(state.pop(("total", g)), axis=1, keepdims=True)
        attended = (state.pop(("out", g)) * inverse).astype(jnp.bfloat16)
        o_ref[g] = attended
        state["delta", g] = jnp.sum(do * attended.astype(jnp.float32), axis=1, keepdims=True)
        state["q", g] = (q.astype(jnp.float32) * (inverse * softmax_scale)).astype(jnp.bfloat16).T
        state["do", g] = (do * inverse).astype(jnp.bfloat16).T
        state["scale", g] = inverse * softmax_scale

    def backward(g, s):
        e = e_ref[g % 2, s]
        dv = product(state["do", g], e)
        dscore = (e.astype(jnp.float32) * (p_ref[g % 2, s] - state["delta", g])).astype(jnp.bfloat16)
        part = product(dscore, key(s))
        state["dq", g] = state["dq", g] + part if s else part
        dk = product(state["q", g], dscore)
        if g == 0:
            dk_ref[s] = dk
            dv_ref[s] = dv
        elif g < head_group - 1:
            dk_ref[s] += dk
            dv_ref[s] += dv
        else:
            term_refs[s][0, 0] = (dk_ref[s] + dk).T.astype(jnp.bfloat16)
            term_refs[s][0, 1] = (dv_ref[s] + dv).T.astype(jnp.bfloat16)

    def backward_end(g):
        dq_ref[g] = (state.pop(("dq", g)) * state["scale", g]).astype(jnp.bfloat16)

    every = range(sources)
    for s in every:
        scores(0, s)
    scores_end(0)
    for g in range(head_group):
        for s in every:
            forward(g, s)
            if g:
                backward(g - 1, s)
        if g:
            backward_end(g - 1)
        if g + 1 < head_group:
            for s in every:
                scores(g + 1, s)
        forward_end(g)
        if g + 1 < head_group:
            scores_end(g + 1)
    for s in every:
        backward(head_group - 1, s)
    backward_end(head_group - 1)

def attend(heads, head_group, bias, queries, output_gradient, kvs, outs, after):
    heads_all, tokens, size = queries.shape
    sources = len(kvs)
    first, last = heads
    rows = pl.BlockSpec((head_group, tokens, size), lambda j: (first + j, 0, 0))

    def block(begin):
        return pl.BlockSpec((1, 2, tokens, size), lambda j: (first - begin + j, 0, 0, 0))

    shapes = [(heads_all, tokens, size)] * 2 + [(g[1] - g[0], 2, tokens, size) for _, g in outs[2:]]
    chained = [(n, a) for n, (a, _) in enumerate(outs) if a is not None]
    scores = (last - first) * head_group * tokens * sources * tokens
    return pl.pallas_call(
        functools.partial(attend_kernel, sources, size ** (-0.5), len(chained) + len(after)),
        grid=(last - first,),
        in_specs=[VMEM, rows, rows] + [block(begin) for _, begin in kvs] + [ANY] * (len(chained) + len(after)),
        out_specs=[rows, rows] + [block(g[0]) for _, g in outs[2:]],
        out_shape=[jax.ShapeDtypeStruct(s, jnp.bfloat16) for s in shapes],
        scratch_shapes=[pltpu.VMEM((sources, size, tokens), jnp.float32)] * 2
        + [
            pltpu.VMEM((2, sources, tokens, tokens), jnp.float32),
            pltpu.VMEM((2, sources, tokens, tokens), jnp.bfloat16),
            pltpu.VMEM((2, sources, tokens, tokens), jnp.float32),
        ],
        input_output_aliases={3 + sources + i: n for i, (n, _) in enumerate(chained)},
        compiler_params=pltpu.CompilerParams(vmem_limit_bytes=VMEM_LIMIT),
        cost_estimate=pl.CostEstimate(
            flops=12 * scores * size,
            bytes_accessed=8 * (last - first) * head_group * tokens * size,
            transcendentals=scores,
        ),
    )(bias, in_hbm(queries), in_hbm(output_gradient), *[a for a, _ in kvs], *[a for _, a in chained], *after)


def shards(block_mask, queries, keys, values, output_gradient):
    count = lax.axis_size("seq")
    me = lax.axis_index("seq").astype(jnp.int32).reshape(1)
    tokens, kv_heads, size = keys.shape
    head_group = queries.shape[1] // kv_heads
    bits = partner_bits(count)
    q = jnp.transpose(queries, (1, 0, 2))
    dout = jnp.transpose(output_gradient, (1, 0, 2))
    whole = (0, kv_heads)
    groups = sorted({g for slot in FETCH for g in slot} | {whole})
    bias, *arrays = pack(me, block_mask, keys, values, groups, bits)
    packed = dict(zip(groups, arrays))
    fetched = [
        {group: from_partner(packed[group], "seq", bit) for group in slot} for bit, slot in zip(bits, FETCH)
    ]
    made = {}
    returned = {}
    for heads in KERNELS:
        kvs = [(packed[whole], 0)]
        for slot, got in zip(FETCH, fetched):
            group = group_of(slot, heads[0])
            kvs.append((got[group], group[0]))
        spots = [("o", whole), ("dq", whole), ("own", whole)]
        spots += [(slot, group_of(RETURN[slot], heads[0])) for slot in range(len(bits))]
        outs = [(made.get(spot), spot[1]) for spot in spots]
        results = attend(heads, head_group, bias, q, dout, kvs, outs, [])
        made.update(zip(spots, results))
        before = list(returned.values())
        for slot in reversed(range(len(bits))):
            for group in RETURN[slot]:
                if group[1] == heads[1]:
                    term = made[slot, group]
                    if before:
                        term = lax.optimization_barrier((term, *before))[0]
                    returned[slot, group] = from_partner(term, "seq", bits[slot])
    term_groups = [whole] + [group for _, group in returned]
    terms = [made["own", whole]] + list(returned.values())
    grad_keys, grad_values = sum_terms(term_groups, terms, tokens, kv_heads, size)
    attended = made["o", whole]
    grad_queries = made["dq", whole]
    return (jnp.transpose(attended, (1, 0, 2)), jnp.transpose(grad_queries, (1, 0, 2)), grad_keys, grad_values)


def solution(mesh):
    rows = P(("groups", "seq"), None)
    cube = P(("groups", "seq"), None, None)
    return jax.shard_map(
        shards,
        mesh=mesh,
        in_specs=(rows, cube, cube, cube, cube),
        out_specs=(cube, cube, cube, cube),
        check_vma=False,
    )
```

time: 85.7 us -> 70.9 us (0.83)
  starting transfers between devices: 20.6 us -> 13.8 us
  local copies, waits for them, and re-layouts: 4.53 us -> 0 us
  Pallas kernels: 35.6 us -> 31.5 us
  waiting for transfers between devices: 21.2 us -> 24.8 us
  other arithmetic: 2.79 us -> 0 us
    ppermute x16 -> x12, starting transfers between devices: 20.6 us -> 13.8 us  [from_partner(): return lax.ppermute(value, axis, pairs)]
    pallas_call x2 -> x4, Pallas kernels: 35.6 us -> 31.5 us  [the longest x2 28.7 us: attend(): pl.pallas_call(functools.partial(attend_kernel, sources, size ** (-0.5),...]
    ppermute x16 -> x12, waiting for transfers between devices: 21.2 us -> 24.8 us  [from_partner(): return lax.ppermute(value, axis, pairs)]
    slice x2 -> x0, local copies, waits for them, and re-layouts: 2.63 us -> none  [shards(): x[:, c * per:(c + 1) * per]]
    transpose x3 -> x0, other arithmetic: 2.39 us -> none  [the longest x1 1.17 us: shards(): jnp.transpose(jnp.concatenate([r[0] for r in results], axis=0), (1, 0, 2))]
    unnamed x6 -> x0, local copies, waits for them, and re-layouts: 1.83 us -> none
  transfers between devices with their start and end apart: 16 -> 12, of which waited for: 3 -> 3; matrix products, arithmetic and copies ran while one was open for 3% -> 0% of each run, Pallas kernels for 42% -> 41%
where the time goes in v2:
time: 70.9 us; the launch traced here: 70.8 us
  Pallas kernels  31.5 us (44%)
  waiting for transfers between devices  24.8 us (35%)
  starting transfers between devices  13.8 us (19%)
    pallas_call x2, Pallas kernels, attend(): pl.pallas_call(functools.partial(attend_kernel, sources, size ** (-0.5),...  28.7 us
    ppermute x12, waiting for transfers between devices, from_partner(): return lax.ppermute(value, axis, pairs)  24.8 us
    ppermute x12, starting transfers between devices, from_partner(): return lax.ppermute(value, axis, pairs)  13.8 us
  transfers between devices with their start and end apart: 12, of which 3 were waited for; matrix products, arithmetic and copies ran while one was open for 0% of the time, Pallas kernels for 41%

profile of v2, /device:TPU:0, one launch (start us, length us, event | category | flops | bytes accessed | tf_op | source)
XLA Modules:
  0.0 70.8 jit_solution(17431907392827116523)
XLA Ops:
  0.6 1.4 %shard_map.84 = (f32[5,2,256]{2,1,0:T(2,128)S(1)}, bf16[2,2,256,128]{3,2,1,0:T(8,128)(2,1)S(1)}, bf16[4,2,256,128]{3,2,1,0:T(8,128)(2,1)S(1)}, bf16[2,2,256,128]{3,2,1,0:T(8,128)(2,1)S(1)}) custom-call(s32[1]{0:T(128)} %bitcast.me_ref, s32[2,32]{1,0:T(2,128)} %mask_ref.1, bf16[256,4,128]{2,1,0:T(4,128)(2,1)} %k_ref.1, bf16[256,4,128]{2,1,0:T(4,128)(2,1)} %v_ref.1), custom_call_target="tpu_custom_call" | custom-call | bytes 1572864 | tf_op jit(solution)/shard_map/pallas_call | solution.py:77
  2.0 3.0 %collective-permute-start.1 = (bf16[4,2,256,128]{3,2,1,0:T(8,128)(2,1)S(1)}, bf16[4,2,256,128]{3,2,1,0:T(8,128)(2,1)S(1)}, u32[]{:S(2)}, u32[]{:S(2)}) collective-permute-start(bf16[4,2,256,128]{3,2,1,0:T(8,128)(2,1)S(1)} %get-tuple-element.29.refs_0_), channel_id=1, source_target_pairs={{0,2},{1,3},{2,0},{3,1},{4,6},{5,7},{6,4},{7,5},{8,10},{9,11},{10,... | collective-permute-start | bytes 1572872 | tf_op jit(solution)/shard_map/ppermute | solution.py:21
  5.0 2.6 %collective-permute-start.5 = (bf16[2,2,256,128]{3,2,1,0:T(8,128)(2,1)S(1)}, bf16[2,2,256,128]{3,2,1,0:T(8,128)(2,1)S(1)}, u32[]{:S(2)}, u32[]{:S(2)}) collective-permute-start(bf16[2,2,256,128]{3,2,1,0:T(8,128)(2,1)S(1)} %get-tuple-element.31), channel_id=1, source_target_pairs={{0,8},{1,9},{2,10},{3,11},{4,12},{5,13},{6,14},{7,15},{8,0},{9,1},... | collective-permute-start | bytes 786440 | tf_op jit(solution)/shard_map/ppermute | solution.py:21
  7.6 1.6 %collective-permute-start.4 = (bf16[2,2,256,128]{3,2,1,0:T(8,128)(2,1)S(1)}, bf16[2,2,256,128]{3,2,1,0:T(8,128)(2,1)S(1)}, u32[]{:S(2)}, u32[]{:S(2)}) collective-permute-start(bf16[2,2,256,128]{3,2,1,0:T(8,128)(2,1)S(1)} %get-tuple-element.31), channel_id=1, source_target_pairs={{0,4},{1,5},{2,6},{3,7},{4,0},{5,1},{6,2},{7,3},{8,12},{9,13},{10,... | collective-permute-start | bytes 786440 | tf_op jit(solution)/shard_map/ppermute | solution.py:21
  9.2 0.3 collective-permute-start.3
  9.5 11.2 %collective-permute-done.5.refs_4_ = bf16[2,2,256,128]{3,2,1,0:T(8,128)(2,1)S(1)} collective-permute-done((bf16[2,2,256,128]{3,2,1,0:T(8,128)(2,1)S(1)}, bf16[2,2,256,128]{3,2,1,0:T(8,128)(2,1)S(1)}, u32[]{:S(2)}, u32[]{:S(2)}) %collective-permute-start.5) | collective-permute-done | bytes 262176 | tf_op jit(solution)/shard_map/ppermute | solution.py:21
  20.8 0.4 collective-permute-start.2
  21.2 0.3 collective-permute-done.4.refs_3_
  21.5 0.0 collective-permute-done.1.refs_2_
  21.5 14.3 %shard_map.85 = (bf16[20,256,128]{2,1,0:T(8,128)(2,1)}, bf16[20,256,128]{2,1,0:T(8,128)(2,1)}, bf16[4,2,256,128]{3,2,1,0:T(8,128)(2,1)S(1)}, bf16[4,2,256,128]{3...) custom-call(f32[5,2,256]{2,1,0:T(2,128)S(1)} %get-tuple-element.28.b, ...), custom_call_target="tpu_custom_call" | custom-call | flops 5033164800 | bytes 2621440 | tf_op jit(solution)/shard_map/pallas_call | solution.py:211
  35.8 3.3 %collective-permute-start.6 = (bf16[2,2,256,128]{3,2,1,0:T(8,128)(2,1)S(1)}, bf16[2,2,256,128]{3,2,1,0:T(8,128)(2,1)S(1)}, u32[]{:S(2)}, u32[]{:S(2)}) collective-permute-start(bf16[2,2,256,128]{3,2,1,0:T(8,128)(2,1)S(1)} %get-tuple-element.40), channel_id=1, source_target_pairs={{0,8},{1,9},{2,10},{3,11},{4,12},{5,13},{6,14},{7,15},{8,0},{9,1},... | collective-permute-start | bytes 786440 | tf_op jit(solution)/shard_map/ppermute | solution.py:21
  39.1 0.0 collective-permute-start.7
  39.1 0.0 collective-permute-done.3.refs_4_
  39.1 0.0 collective-permute-done.2.refs_3_
  39.1 14.5 %shard_map.86 = (bf16[20,256,128]{2,1,0:T(8,128)(2,1)}, bf16[20,256,128]{2,1,0:T(8,128)(2,1)}, bf16[4,2,256,128]{3,2,1,0:T(8,128)(2,1)S(1)}, bf16[4,2,256,128]{3...) custom-call(f32[5,2,256]{2,1,0:T(2,128)S(1)} %get-tuple-element.28.b, ...), custom_call_target="tpu_custom_call", output_to_operand_aliasing={{0}: (8, {}), {1}: (9, {}), {2}: (10, {}), {3}: (11, {}), {... | custom-call | flops 5033164800 | bytes 2621440 | tf_op jit(solution)/shard_map/pallas_call | solution.py:211
  53.6 0.0 collective-permute-done.7.refs_2_
  53.6 0.6 collective-permute-start.10
  54.1 0.0 collective-permute-start.11
  54.1 0.7 collective-permute-start.8
  54.8 1.3 %collective-permute-start.9 = (bf16[2,2,256,128]{3,2,1,0:T(8,128)(2,1)S(1)}, bf16[2,2,256,128]{3,2,1,0:T(8,128)(2,1)S(1)}, u32[]{:S(2)}, u32[]{:S(2)}) collective-permute-start(bf16[2,2,256,128]{3,2,1,0:T(8,128)(2,1)S(1)} %get-tuple-element.45), channel_id=1, source_target_pairs={{0,4},{1,5},{2,6},{3,7},{4,0},{5,1},{6,2},{7,3},{8,12},{9,13},{10,... | collective-permute-start | bytes 786440 | tf_op jit(solution)/shard_map/ppermute | solution.py:21
  56.1 13.3 %collective-permute-done.8.refs_3_ = bf16[2,2,256,128]{3,2,1,0:T(8,128)(2,1)S(1)} collective-permute-done((bf16[2,2,256,128]{3,2,1,0:T(8,128)(2,1)S(1)}, bf16[2,2,256,128]{3,2,1,0:T(8,128)(2,1)S(1)}, u32[]{:S(2)}, u32[]{:S(2)}) %collective-permute-start.8) | collective-permute-done | bytes 262176 | tf_op jit(solution)/shard_map/ppermute | solution.py:21
  69.4 0.0 collective-permute-done.9.refs_4_
  69.4 0.0 collective-permute-done.10.refs_5_
  69.4 1.3 %shard_map.87 = (bf16[256,4,128]{2,1,0:T(4,128)(2,1)}, bf16[256,4,128]{2,1,0:T(4,128)(2,1)}) custom-call(bf16[4,2,256,128]{3,2,1,0:T(8,128)(2,1)S(1)} %get-tuple-element.39.refs_0_, bf16[2,2,256,128]{3,2,1,0:T(8,128)(2,1)S(1)} %collective-permute-done.6.refs_1_, bf16[2,2,256,128]{3,2,1,0:T(8,128)(2,1)S(1)} %collective-permute-done.7.refs_2_, ...), custom_call_target="tpu_custom_call" | custom-call | bytes 3145728 | tf_op jit(solution)/shard_map/pallas_call | solution.py:101
  (4 shorter events, 0.0 us)
Async XLA Ops:
  2.0 19.4 %collective-permute-start.1 = (bf16[4,2,256,128]{3,2,1,0:T(8,128)(2,1)S(1)}, bf16[4,2,256,128]{3,2,1,0:T(8,128)(2,1)S(1)}, u32[]{:S(2)}, u32[]{:S(2)}) collective-permute-start(bf16[4,2,256,128]{3,2,1,0:T(8,128)(2,1)S(1)} %get-tuple-element.29.refs_0_), channel_id=1, source_target_pairs={{0,2},{1,3},{2,0},{3,1},{4,6},{5,7},{6,4},{7,5},{8,10},{9,11},{10,... | collective-permute-start | bytes 1572872 | tf_op jit(solution)/shard_map/ppermute | solution.py:21
  5.0 16.4 %collective-permute-start = (bf16[4,2,256,128]{3,2,1,0:T(8,128)(2,1)S(1)}, bf16[4,2,256,128]{3,2,1,0:T(8,128)(2,1)S(1)}, u32[]{:S(2)}, u32[]{:S(2)}) collective-permute-start(bf16[4,2,256,128]{3,2,1,0:T(8,128)(2,1)S(1)} %get-tuple-element.29.refs_0_), channel_id=1, source_target_pairs={{0,1},{1,0},{2,3},{3,2},{4,5},{5,4},{6,7},{7,6},{8,9},{9,8},{10,11... | collective-permute-start | bytes 1572872 | tf_op jit(solution)/shard_map/ppermute | solution.py:21
  5.0 15.7 %collective-permute-start.5 = (bf16[2,2,256,128]{3,2,1,0:T(8,128)(2,1)S(1)}, bf16[2,2,256,128]{3,2,1,0:T(8,128)(2,1)S(1)}, u32[]{:S(2)}, u32[]{:S(2)}) collective-permute-start(bf16[2,2,256,128]{3,2,1,0:T(8,128)(2,1)S(1)} %get-tuple-element.31), channel_id=1, source_target_pairs={{0,8},{1,9},{2,10},{3,11},{4,12},{5,13},{6,14},{7,15},{8,0},{9,1},... | collective-permute-start | bytes 786440 | tf_op jit(solution)/shard_map/ppermute | solution.py:21
  7.6 13.8 %collective-permute-start.4 = (bf16[2,2,256,128]{3,2,1,0:T(8,128)(2,1)S(1)}, bf16[2,2,256,128]{3,2,1,0:T(8,128)(2,1)S(1)}, u32[]{:S(2)}, u32[]{:S(2)}) collective-permute-start(bf16[2,2,256,128]{3,2,1,0:T(8,128)(2,1)S(1)} %get-tuple-element.31), channel_id=1, source_target_pairs={{0,4},{1,5},{2,6},{3,7},{4,0},{5,1},{6,2},{7,3},{8,12},{9,13},{10,... | collective-permute-start | bytes 786440 | tf_op jit(solution)/shard_map/ppermute | solution.py:21
  9.2 29.9 %collective-permute-start.3 = (bf16[2,2,256,128]{3,2,1,0:T(8,128)(2,1)S(1)}, bf16[2,2,256,128]{3,2,1,0:T(8,128)(2,1)S(1)}, u32[]{:S(2)}, u32[]{:S(2)}) collective-permute-start(bf16[2,2,256,128]{3,2,1,0:T(8,128)(2,1)S(1)} %get-tuple-element.30), channel_id=1, source_target_pairs={{0,8},{1,9},{2,10},{3,11},{4,12},{5,13},{6,14},{7,15},{8,0},{9,1},... | collective-permute-start | bytes 786440 | tf_op jit(solution)/shard_map/ppermute | solution.py:21
  20.8 18.3 %collective-permute-start.2 = (bf16[2,2,256,128]{3,2,1,0:T(8,128)(2,1)S(1)}, bf16[2,2,256,128]{3,2,1,0:T(8,128)(2,1)S(1)}, u32[]{:S(2)}, u32[]{:S(2)}) collective-permute-start(bf16[2,2,256,128]{3,2,1,0:T(8,128)(2,1)S(1)} %get-tuple-element.30), channel_id=1, source_target_pairs={{0,4},{1,5},{2,6},{3,7},{4,0},{5,1},{6,2},{7,3},{8,12},{9,13},{10,... | collective-permute-start | bytes 786440 | tf_op jit(solution)/shard_map/ppermute | solution.py:21
  35.8 17.8 %collective-permute-start.6 = (bf16[2,2,256,128]{3,2,1,0:T(8,128)(2,1)S(1)}, bf16[2,2,256,128]{3,2,1,0:T(8,128)(2,1)S(1)}, u32[]{:S(2)}, u32[]{:S(2)}) collective-permute-start(bf16[2,2,256,128]{3,2,1,0:T(8,128)(2,1)S(1)} %get-tuple-element.40), channel_id=1, source_target_pairs={{0,8},{1,9},{2,10},{3,11},{4,12},{5,13},{6,14},{7,15},{8,0},{9,1},... | collective-permute-start | bytes 786440 | tf_op jit(solution)/shard_map/ppermute | solution.py:21
  39.1 14.5 %collective-permute-start.7 = (bf16[2,2,256,128]{3,2,1,0:T(8,128)(2,1)S(1)}, bf16[2,2,256,128]{3,2,1,0:T(8,128)(2,1)S(1)}, u32[]{:S(2)}, u32[]{:S(2)}) collective-permute-start(bf16[2,2,256,128]{3,2,1,0:T(8,128)(2,1)S(1)} %get-tuple-element.41), channel_id=1, source_target_pairs={{0,4},{1,5},{2,6},{3,7},{4,0},{5,1},{6,2},{7,3},{8,12},{9,13},{10,... | collective-permute-start | bytes 786440 | tf_op jit(solution)/shard_map/ppermute | solution.py:21
  53.6 15.9 %collective-permute-start.10 = (bf16[4,2,256,128]{3,2,1,0:T(8,128)(2,1)S(1)}, bf16[4,2,256,128]{3,2,1,0:T(8,128)(2,1)S(1)}, u32[]{:S(2)}, u32[]{:S(2)}) collective-permute-start(bf16[4,2,256,128]{3,2,1,0:T(8,128)(2,1)S(1)} %get-tuple-element.47), channel_id=1, source_target_pairs={{0,2},{1,3},{2,0},{3,1},{4,6},{5,7},{6,4},{7,5},{8,10},{9,11},{10,... | collective-permute-start | bytes 1572872 | tf_op jit(solution)/shard_map/ppermute | solution.py:21
  54.1 15.3 %collective-permute-start.11 = (bf16[4,2,256,128]{3,2,1,0:T(8,128)(2,1)S(1)}, bf16[4,2,256,128]{3,2,1,0:T(8,128)(2,1)S(1)}, u32[]{:S(2)}, u32[]{:S(2)}) collective-permute-start(bf16[4,2,256,128]{3,2,1,0:T(8,128)(2,1)S(1)} %get-tuple-element.49), channel_id=1, source_target_pairs={{0,1},{1,0},{2,3},{3,2},{4,5},{5,4},{6,7},{7,6},{8,9},{9,8},{10,11... | collective-permute-start | bytes 1572872 | tf_op jit(solution)/shard_map/ppermute | solution.py:21
  54.1 15.3 %collective-permute-start.8 = (bf16[2,2,256,128]{3,2,1,0:T(8,128)(2,1)S(1)}, bf16[2,2,256,128]{3,2,1,0:T(8,128)(2,1)S(1)}, u32[]{:S(2)}, u32[]{:S(2)}) collective-permute-start(bf16[2,2,256,128]{3,2,1,0:T(8,128)(2,1)S(1)} %get-tuple-element.43), channel_id=1, source_target_pairs={{0,8},{1,9},{2,10},{3,11},{4,12},{5,13},{6,14},{7,15},{8,0},{9,1},... | collective-permute-start | bytes 786440 | tf_op jit(solution)/shard_map/ppermute | solution.py:21
  54.8 14.6 %collective-permute-start.9 = (bf16[2,2,256,128]{3,2,1,0:T(8,128)(2,1)S(1)}, bf16[2,2,256,128]{3,2,1,0:T(8,128)(2,1)S(1)}, u32[]{:S(2)}, u32[]{:S(2)}) collective-permute-start(bf16[2,2,256,128]{3,2,1,0:T(8,128)(2,1)S(1)} %get-tuple-element.45), channel_id=1, source_target_pairs={{0,4},{1,5},{2,6},{3,7},{4,0},{5,1},{6,2},{7,3},{8,12},{9,13},{10,... | collective-permute-start | bytes 786440 | tf_op jit(solution)/shard_map/ppermute | solution.py:21

commit v3 on v2

v3 whole, which is shorter than its diff:
```python
import functools

import jax
import jax.numpy as jnp
from jax import lax
from jax.experimental import pallas as pl
from jax.experimental.pallas import tpu as pltpu
from jax.sharding import PartitionSpec as P

LOG2E = 1.4426950408889634
MASKED = -1e30
VMEM_LIMIT = 24 * 2**20
LOCAL = (0, 1)
REMOTE = (2, 3, 4)
HALVES = ((0, 2), (2, 4))


def from_partner(value, axis, apart):
    mask = 2**apart
    pairs = [(source, source ^ mask) for source in range(lax.axis_size(axis))]
    return lax.ppermute(value, axis, pairs)


def partner_bits(count):
    level = count.bit_length() - 1
    return (0, 1, level - 2, level - 1)


def product(left, right):
    return lax.dot_general(left, right, (((1,), (0,)), ((), ())), preferred_element_type=jnp.float32)


def product_nt(left, right):
    return lax.dot_general(left, right, (((1,), (1,)), ((), ())), preferred_element_type=jnp.float32)


VMEM = pl.BlockSpec(memory_space=pltpu.VMEM)
SMEM = pl.BlockSpec(memory_space=pltpu.SMEM)
ANY = pl.BlockSpec(memory_space=pl.ANY)


def in_hbm(array):
    return pltpu.with_memory_space_constraint(array, pltpu.HBM)


def pack_kernel(groups, bits, me_ref, mask_ref, k_ref, v_ref, bias_ref, *refs):
    outs, wide_ref = refs[:-1], refs[-1]
    tokens, heads, size = k_ref.shape
    for i, ref in enumerate((k_ref, v_ref)):
        wide_ref[i] = ref[...].astype(jnp.float32).reshape(tokens * heads, size)
        for h in range(heads):
            rows = wide_ref[i, pl.ds(h, tokens, stride=heads), :].astype(jnp.bfloat16)
            for (low, high), out in zip(groups, outs):
                if low <= h < high:
                    out[h - low, i] = rows
    me = me_ref[0]
    blocks, columns = mask_ref.shape
    mask = mask_ref[...]
    column = lax.broadcasted_iota(jnp.int32, (blocks, columns), 1)
    for s, device in enumerate([me] + [jnp.bitwise_xor(me, 1 << bit) for bit in bits]):
        for b in range(blocks):
            ones = jnp.sum(jnp.where(column == device * blocks + b, mask, 0), axis=1, keepdims=True)
            width = tokens // blocks
            bias_ref[s, :, b * width : (b + 1) * width] = jnp.broadcast_to(
                jnp.where(ones > 0, 0.0, MASKED), (blocks, width)
            )


def pack(me, block_mask, keys, values, groups, bits):
    tokens, heads, size = keys.shape
    bias = jax.ShapeDtypeStruct((len(bits) + 1, block_mask.shape[0], tokens), jnp.float32)
    return pl.pallas_call(
        functools.partial(pack_kernel, groups, bits),
        in_specs=[SMEM] + [VMEM] * 3,
        out_specs=[VMEM] * (len(groups) + 1),
        out_shape=[bias]
        + [jax.ShapeDtypeStruct((high - low, 2, tokens, size), keys.dtype) for low, high in groups],
        scratch_shapes=[pltpu.VMEM((2, tokens * heads, size), jnp.float32)],
        compiler_params=pltpu.CompilerParams(vmem_limit_bytes=VMEM_LIMIT),
        cost_estimate=pl.CostEstimate(flops=0, bytes_accessed=6 * keys.size * 2, transcendentals=0),
    )(me, in_hbm(block_mask), in_hbm(keys), in_hbm(values))


def gather_kernel(groups, *refs):
    terms, out = refs[:-1], refs[-1]
    for h in range(out.shape[0]):
        parts = [t[h - g[0]].astype(jnp.float32) for g, t in zip(groups, terms) if g[0] <= h < g[1]]
        out[h] = functools.reduce(jnp.add, parts)


def gather_terms(groups, terms, heads):
    return pl.pallas_call(
        functools.partial(gather_kernel, groups),
        in_specs=[VMEM] * len(groups),
        out_specs=VMEM,
        out_shape=jax.ShapeDtypeStruct((heads,) + terms[0].shape[1:], jnp.float32),
        compiler_params=pltpu.CompilerParams(vmem_limit_bytes=VMEM_LIMIT),
        cost_estimate=pl.CostEstimate(flops=0, bytes_accessed=8 * 2**20, transcendentals=0),
    )(*terms)


def sum_kernel(groups, *refs):
    terms, (dk_ref, dv_ref, wide_ref) = refs[: len(groups)], refs[len(groups) :]
    tokens, heads, size = dk_ref.shape
    for i, ref in enumerate((dk_ref, dv_ref)):
        for h in range(heads):
            parts = [t[h - g[0], i].astype(jnp.float32) for g, t in zip(groups, terms) if g[0] <= h < g[1]]
            wide_ref[i, pl.ds(h, tokens, stride=heads), :] = functools.reduce(jnp.add, parts)
        ref[...] = wide_ref[i].astype(ref.dtype).reshape(tokens, heads, size)


def sum_terms(groups, terms, tokens, heads, size):
    out = jax.ShapeDtypeStruct((tokens, heads, size), jnp.bfloat16)
    return pl.pallas_call(
        functools.partial(sum_kernel, groups),
        in_specs=[VMEM] * len(groups),
        out_specs=[VMEM] * 2,
        out_shape=[out, out],
        scratch_shapes=[pltpu.VMEM((2, tokens * heads, size), jnp.float32)],
        compiler_params=pltpu.CompilerParams(vmem_limit_bytes=VMEM_LIMIT),
        cost_estimate=pl.CostEstimate(flops=0, bytes_accessed=12 * tokens * heads * size * 2, transcendentals=0),
    )(*terms)


def scores_of(q, key, bias_ref, s):
    x = product_nt(q, key)
    blocks = bias_ref.shape[1]
    width = x.shape[0] // blocks
    return jnp.concatenate([x[a * width : (a + 1) * width] + bias_ref[s, a : a + 1] for a in range(blocks)], axis=0)


def pair(first, second, shape):
    lane = lax.broadcasted_iota(jnp.int32, shape, 1)
    return jnp.where(lane < shape[1] // 2, first, second)


def unpair(array):
    half = array.shape[1] // 2
    return array[:, 0:1], array[:, half : half + 1]


def local_kernel(softmax_scale, bias_ref, q_ref, *refs):
    sources = len(LOCAL)
    kv_refs = refs[:sources]
    e_ref, o_ref, stat_ref, x_ref = refs[sources:]
    scale2 = softmax_scale * LOG2E
    head_group, tokens, size = q_ref.shape
    state = {}

    def scores(g, n):
        x = scores_of(q_ref[g], kv_refs[n][0, 0], bias_ref, LOCAL[n])
        x_ref[g % 2, n] = x
        state["max", g] = jnp.maximum(state["max", g], x) if n else x

    def scores_end(g):
        state["top", g] = jnp.max(state.pop(("max", g)), axis=1, keepdims=True) * scale2

    def forward(g, n):
        e = jnp.exp2(x_ref[g % 2, n] * scale2 - state["top", g])
        narrow = e.astype(jnp.bfloat16)
        e_ref[g, n] = narrow
        state["total", g] = state["total", g] + e if n else e
        part = product(narrow, kv_refs[n][0, 1])
        state["out", g] = state["out", g] + part if n else part

    def forward_end(g):
        o_ref[g] = state.pop(("out", g))
        total = jnp.sum(state.pop(("total", g)), axis=1, keepdims=True)
        stat_ref[g] = pair(state["top", g], total, (tokens, size))

    every = range(sources)
    for n in every:
        scores(0, n)
    scores_end(0)
    for g in range(head_group):
        for n in every:
            forward(g, n)
            if g + 1 < head_group:
                scores(g + 1, n)
        forward_end(g)
        if g + 1 < head_group:
            scores_end(g + 1)


def remote_kernel(softmax_scale, unused, bias_ref, q_ref, do_ref, part_ref, stat_ref, *refs):
    sources = len(REMOTE)
    kv_refs = refs[:sources]
    refs = refs[sources + unused :]
    o_ref, dq_ref, row_ref = refs[:3]
    term_refs = refs[3 : sources + 3]
    dk_ref, dv_ref, x_ref, e_ref, p_ref = refs[sources + 3 :]
    scale2 = softmax_scale * LOG2E
    head_group, tokens, size = q_ref.shape
    state = {}

    def key(n):
        return kv_refs[n][0, 0]

    def value(n):
        return kv_refs[n][0, 1]

    def scores(g, n):
        x = scores_of(q_ref[g], key(n), bias_ref, REMOTE[n])
        x_ref[g % 2, n] = x
        state["max", g] = jnp.maximum(state["max", g], x) if n else x
        p_ref[g % 2, n] = product_nt(do_ref[g], value(n))

    def scores_end(g):
        local, total = unpair(stat_ref[g])
        top = jnp.maximum(jnp.max(state.pop(("max", g)), axis=1, keepdims=True) * scale2, local)
        state["top", g] = top
        state["share", g] = jnp.exp2(local - top)
        state["part", g] = total * state["share", g]

    def forward(g, n):
        e = jnp.exp2(x_ref[g % 2, n] * scale2 - state["top", g])
        narrow = e.astype(jnp.bfloat16)
        e_ref[g % 2, n] = narrow
        state["total", g] = state["total", g] + e if n else e
        part = product(narrow, value(n))
        state["out", g] = state["out", g] + part if n else part

    def forward_end(g):
        q, do = q_ref[g], do_ref[g].astype(jnp.float32)
        total = jnp.sum(state.pop(("total", g)), axis=1, keepdims=True) + state["part", g]
        inverse = 1.0 / total
        attended = state.pop(("out", g)) + part_ref[g] * state["share", g]
        attended = (attended * inverse).astype(jnp.bfloat16)
        o_ref[g] = attended
        delta = jnp.sum(do * attended.astype(jnp.float32), axis=1, keepdims=True)
        state["delta", g] = delta
        row_ref[g] = pair(state["share", g] * inverse, delta, (tokens, size))
        state["q", g] = (q.astype(jnp.float32) * (inverse * softmax_scale)).astype(jnp.bfloat16).T
        state["do", g] = (do * inverse).astype(jnp.bfloat16).T
        state["scale", g] = inverse * softmax_scale

    def backward(g, n):
        e = e_ref[g % 2, n]
        dv = product(state["do", g], e)
        dscore = (e.astype(jnp.float32) * (p_ref[g % 2, n] - state["delta", g])).astype(jnp.bfloat16)
        part = product(dscore, key(n))
        state["dq", g] = state["dq", g] + part if n else part
        dk = product(state["q", g], dscore)
        if g == 0:
            dk_ref[n] = dk
            dv_ref[n] = dv
        elif g < head_group - 1:
            dk_ref[n] += dk
            dv_ref[n] += dv
        else:
            term_refs[n][0, 0] = (dk_ref[n] + dk).T.astype(jnp.bfloat16)
            term_refs[n][0, 1] = (dv_ref[n] + dv).T.astype(jnp.bfloat16)

    def backward_end(g):
        dq_ref[g] = state.pop(("dq", g)) * state["scale", g]

    every = range(sources)
    for n in every:
        scores(0, n)
    scores_end(0)
    for g in range(head_group):
        for n in every:
            forward(g, n)
            if g:
                backward(g - 1, n)
        if g:
            backward_end(g - 1)
        if g + 1 < head_group:
            for n in every:
                scores(g + 1, n)
        forward_end(g)
        if g + 1 < head_group:
            scores_end(g + 1)
    for n in every:
        backward(head_group - 1, n)
    backward_end(head_group - 1)


def rest_kernel(softmax_scale, unused, q_ref, do_ref, e_ref, part_ref, row_ref, *refs):
    sources = len(LOCAL)
    kv_refs = refs[:sources]
    refs = refs[sources + unused :]
    dq_ref = refs[0]
    term_refs = refs[1 : sources + 1]
    dk_ref, dv_ref, p_ref = refs[sources + 1 :]
    head_group = q_ref.shape[0]
    state = {}

    def dprob(g, n):
        p_ref[g % 2, n] = product_nt(do_ref[g], kv_refs[n][0, 1])

    def rows(g):
        share, delta = unpair(row_ref[g])
        state["delta", g] = delta
        state["scale", g] = share * softmax_scale
        state["q", g] = (q_ref[g].astype(jnp.float32) * state["scale", g]).astype(jnp.bfloat16).T
        state["do", g] = (do_ref[g].astype(jnp.float32) * share).astype(jnp.bfloat16).T

    def backward(g, n):
        e = e_ref[g, n]
        dv = product(state["do", g], e)
        dscore = (e.astype(jnp.float32) * (p_ref[g % 2, n] - state["delta", g])).astype(jnp.bfloat16)
        part = product(dscore, kv_refs[n][0, 0])
        state["dq", g] = state["dq", g] + part if n else part
        dk = product(state["q", g], dscore)
        if g == 0:
            dk_ref[n] = dk
            dv_ref[n] = dv
        elif g < head_group - 1:
            dk_ref[n] += dk
            dv_ref[n] += dv
        else:
            term_refs[n][0, 0] = (dk_ref[n] + dk).T.astype(jnp.bfloat16)
            term_refs[n][0, 1] = (dv_ref[n] + dv).T.astype(jnp.bfloat16)

    every = range(sources)
    for n in every:
        dprob(0, n)
    rows(0)
    for g in range(head_group):
        for n in every:
            backward(g, n)
            if g + 1 < head_group:
                dprob(g + 1, n)
        dq_ref[g] = (part_ref[g] + state.pop(("dq", g)) * state["scale", g]).astype(jnp.bfloat16)
        if g + 1 < head_group:
            rows(g + 1)


def cost(products, heads, head_group, tokens, sources, size):
    scores = heads * head_group * tokens * tokens * sources
    return pl.CostEstimate(
        flops=2 * products * scores * size,
        bytes_accessed=8 * heads * head_group * tokens * size,
        transcendentals=scores,
    )


def attend(bias, queries, output_gradient, heads_all, head_group):
    tokens, size = queries.shape[1:]

    def rows(first):
        return pl.BlockSpec((head_group, tokens, size), lambda j: (first + j, 0, 0))

    def block(first, begin):
        return pl.BlockSpec((1, 2, tokens, size), lambda j: (first - begin + j, 0, 0, 0))

    def exps(first):
        return pl.BlockSpec((head_group, len(LOCAL), tokens, tokens), lambda j: (first + j, 0, 0, 0))

    scale = size ** (-0.5)
    query_heads = heads_all * head_group
    wide = jax.ShapeDtypeStruct((query_heads, tokens, size), jnp.float32)
    narrow = jax.ShapeDtypeStruct((query_heads, tokens, size), jnp.bfloat16)
    params = pltpu.CompilerParams(vmem_limit_bytes=VMEM_LIMIT)

    def term(count):
        return jax.ShapeDtypeStruct((count, 2, tokens, size), jnp.bfloat16)

    def square(count, kind=jnp.float32):
        return pltpu.VMEM((2, count, tokens, tokens), kind)

    def local(own):
        n = len(LOCAL)
        return pl.pallas_call(
            functools.partial(local_kernel, scale),
            grid=(heads_all,),
            in_specs=[VMEM, rows(0)] + [block(0, 0)] * n,
            out_specs=[exps(0), rows(0), rows(0)],
            out_shape=[jax.ShapeDtypeStruct((query_heads, n, tokens, tokens), jnp.bfloat16), wide, wide],
            scratch_shapes=[square(n)],
            compiler_params=params,
            cost_estimate=cost(2, heads_all, head_group, tokens, n, size),
        )(bias, in_hbm(queries), *own)

    def remote(heads, part, stat, others, chain):
        first, last = heads
        n = len(REMOTE)
        whole = [rows(first)] * 3 + [block(first, 0)]
        return pl.pallas_call(
            functools.partial(remote_kernel, scale, len(chain)),
            grid=(last - first,),
            in_specs=[VMEM] + [rows(first)] * 4 + [block(first, begin) for _, begin in others] + [ANY] * len(chain),
            out_specs=whole + [block(0, 0)] * (n - 1),
            out_shape=[narrow, wide, wide, term(heads_all)] + [term(last - first)] * (n - 1),
            scratch_shapes=[pltpu.VMEM((n, size, tokens), jnp.float32)] * 2
            + [square(n), square(n, jnp.bfloat16), square(n)],
            input_output_aliases={5 + n + i: i for i in range(len(chain))},
            compiler_params=params,
            cost_estimate=cost(6, last - first, head_group, tokens, n, size),
        )(bias, in_hbm(queries), in_hbm(output_gradient), part, stat, *[a for a, _ in others], *chain)

    def rest(heads, e, part, row, own, chain):
        first, last = heads
        n = len(LOCAL)
        return pl.pallas_call(
            functools.partial(rest_kernel, scale, len(chain)),
            grid=(last - first,),
            in_specs=[rows(first)] * 2
            + [exps(first)]
            + [rows(first)] * 2
            + [block(first, 0)] * n
            + [ANY] * len(chain),
            out_specs=[rows(first)] + [block(0, 0)] * n,
            out_shape=[narrow] + [term(last - first)] * n,
            scratch_shapes=[pltpu.VMEM((n, size, tokens), jnp.float32)] * 2 + [square(n)],
            input_output_aliases={5 + n + i: i for i in range(len(chain))},
            compiler_params=params,
            cost_estimate=cost(4, last - first, head_group, tokens, n, size),
        )(in_hbm(queries), in_hbm(output_gradient), e, part, row, *own, *chain)

    return local, remote, rest


def shards(block_mask, queries, keys, values, output_gradient):
    count = lax.axis_size("seq")
    me = lax.axis_index("seq").astype(jnp.int32).reshape(1)
    tokens, kv_heads, size = keys.shape
    head_group = queries.shape[1] // kv_heads
    bits = partner_bits(count)
    q = jnp.transpose(queries, (1, 0, 2))
    dout = jnp.transpose(output_gradient, (1, 0, 2))
    whole = (0, kv_heads)
    groups = (whole,) + HALVES
    bias, *arrays = pack(me, block_mask, keys, values, groups, bits)
    packed = dict(zip(groups, arrays))
    far = {(heads, bit): from_partner(packed[heads], "seq", bit) for heads in HALVES for bit in reversed(bits[2:])}
    core = from_partner(packed[whole], "seq", bits[0])
    near = from_partner(packed[whole], "seq", bits[1])
    local, remote, rest = attend(bias, q, dout, kv_heads, head_group)
    own = [packed[whole], core]
    e, part, stat = local(own)
    chain, sent, terms, term_groups = [], [], [], []
    for heads in HALVES:
        others = [(near, 0)] + [(far[heads, bit], heads[0]) for bit in bits[2:]]
        results = remote(heads, part, stat, others, chain)
        chain = results[:4]
        back = results[4:]
        for bit, term in reversed(list(zip(bits[2:], back))):
            sent.append(from_partner(term, "seq", bit))
            term_groups.append(heads)
    terms = list(sent)
    attended, grad_part, row, near_term = chain
    terms.append(from_partner(near_term, "seq", bits[1]))
    early = len(bits[2:]) * (len(HALVES) - 1)
    row = lax.optimization_barrier((row, *terms[:early]))[0]
    last_groups, last, chain = [whole], [], []
    for heads in HALVES:
        grad_queries, own_term, core_term = rest(heads, e, grad_part, row, own, chain)
        chain = [grad_queries]
        last += [from_partner(core_term, "seq", bits[0]), own_term]
        last_groups += [heads] * 2
    term_groups.append(whole)
    gathered = gather_terms(term_groups, terms, kv_heads)
    grad_keys, grad_values = sum_terms(last_groups, [gathered] + last, tokens, kv_heads, size)
    return (jnp.transpose(attended, (1, 0, 2)), jnp.transpose(grad_queries, (1, 0, 2)), grad_keys, grad_values)


def solution(mesh):
    rows = P(("groups", "seq"), None)
    cube = P(("groups", "seq"), None, None)
    return jax.shard_map(
        shards,
        mesh=mesh,
        in_specs=(rows, cube, cube, cube, cube),
        out_specs=(cube, cube, cube, cube),
        check_vma=False,
    )
```

time: 70.9 us -> 63.4 us (0.89)
  waiting for transfers between devices: 24.8 us -> 5.65 us
  Pallas kernels: 31.5 us -> 42.8 us
    ppermute x12 -> x13, waiting for transfers between devices: 24.8 us -> 5.65 us  [from_partner(): return lax.ppermute(value, axis, pairs)]
    pallas_call x2 -> x6, Pallas kernels: 28.7 us -> 40.3 us  [the longest x2 21.8 us: remote(): pl.pallas_call(functools.partial(remote_kernel, scale, len(chain)), grid=...]
    ppermute x12 -> x13, starting transfers between devices: 13.8 us -> 14 us  [from_partner(): return lax.ppermute(value, axis, pairs)]
  transfers between devices with their start and end apart: 12 -> 13, of which waited for: 3 -> 5; matrix products, arithmetic and copies ran while one was open for 0% -> 0% of each run, Pallas kernels for 41% -> 64%
where the time goes in v3:
time: 63.4 us; the launch traced here: 63.1 us
  Pallas kernels  42.8 us (68%)
  starting transfers between devices  14 us (22%)
  waiting for transfers between devices  5.65 us (9%)
  between operations  0.67 us (1%)
    pallas_call x2, Pallas kernels, remote(): pl.pallas_call(functools.partial(remote_kernel, scale, len(chain)), grid=...  21.8 us
    ppermute x13, starting transfers between devices, from_partner(): return lax.ppermute(value, axis, pairs)  14 us
    pallas_call x2, Pallas kernels, rest(): pl.pallas_call(functools.partial(rest_kernel, scale, len(chain)), grid=(l...  10.3 us
    pallas_call x1, Pallas kernels, local(): pl.pallas_call(functools.partial(local_kernel, scale), grid=(heads_all,),...  7.98 us
    ppermute x13, waiting for transfers between devices, from_partner(): return lax.ppermute(value, axis, pairs)  5.65 us
    pallas_call x1, Pallas kernels, pack(): pl.pallas_call(functools.partial(pack_kernel, groups, bits), in_specs=[SM...  1.37 us
  transfers between devices with their start and end apart: 13, of which 5 were waited for; matrix products, arithmetic and copies ran while one was open for 0% of the time, Pallas kernels for 64%

profile of v3, /device:TPU:0, one launch (start us, length us, event | category | flops | bytes accessed | tf_op | source)
XLA Modules:
  0.0 63.1 jit_solution(12932931181306366272)
XLA Ops:
  0.6 1.4 %shard_map.84 = (f32[5,2,256]{2,1,0:T(2,128)S(1)}, bf16[4,2,256,128]{3,2,1,0:T(8,128)(2,1)S(1)}, bf16[2,2,256,128]{3,2,1,0:T(8,128)(2,1)S(1)}, bf16[2,2,256,128]{3,2,1,0:T(8,128)(2,1)S(1)}) custom-call(s32[1]{0:T(128)} %bitcast.me_ref, s32[2,32]{1,0:T(2,128)} %mask_ref.1, bf16[256,4,128]{2,1,0:T(4,128)(2,1)} %k_ref.1, bf16[256,4,128]{2,1,0:T(4,128)(2,1)} %v_ref.1), custom_call_target="tpu_custom_call" | custom-call | bytes 1572864 | tf_op jit(solution)/shard_map/pallas_call | solution.py:72
  2.0 0.5 collective-permute-start
  2.5 2.6 %collective-permute-start.1 = (bf16[4,2,256,128]{3,2,1,0:T(8,128)(2,1)S(1)}, bf16[4,2,256,128]{3,2,1,0:T(8,128)(2,1)S(1)}, u32[]{:S(2)}, u32[]{:S(2)}) collective-permute-start(bf16[4,2,256,128]{3,2,1,0:T(8,128)(2,1)S(1)} %get-tuple-element.33.refs_0_), channel_id=1, source_target_pairs={{0,2},{1,3},{2,0},{3,1},{4,6},{5,7},{6,4},{7,5},{8,10},{9,11},{10,... | collective-permute-start | bytes 1572872 | tf_op jit(solution)/shard_map/ppermute | solution.py:21
  5.1 2.6 %collective-permute-start.5 = (bf16[2,2,256,128]{3,2,1,0:T(8,128)(2,1)S(1)}, bf16[2,2,256,128]{3,2,1,0:T(8,128)(2,1)S(1)}, u32[]{:S(2)}, u32[]{:S(2)}) collective-permute-start(bf16[2,2,256,128]{3,2,1,0:T(8,128)(2,1)S(1)} %get-tuple-element.37), channel_id=1, source_target_pairs={{0,8},{1,9},{2,10},{3,11},{4,12},{5,13},{6,14},{7,15},{8,0},{9,1},... | collective-permute-start | bytes 786440 | tf_op jit(solution)/shard_map/ppermute | solution.py:21
  7.7 1.6 %collective-permute-start.4 = (bf16[2,2,256,128]{3,2,1,0:T(8,128)(2,1)S(1)}, bf16[2,2,256,128]{3,2,1,0:T(8,128)(2,1)S(1)}, u32[]{:S(2)}, u32[]{:S(2)}) collective-permute-start(bf16[2,2,256,128]{3,2,1,0:T(8,128)(2,1)S(1)} %get-tuple-element.37), channel_id=1, source_target_pairs={{0,4},{1,5},{2,6},{3,7},{4,0},{5,1},{6,2},{7,3},{8,12},{9,13},{10,... | collective-permute-start | bytes 786440 | tf_op jit(solution)/shard_map/ppermute | solution.py:21
  9.3 0.3 collective-permute-start.3
  9.6 0.5 collective-permute-start.2
  10.1 8.0 %shard_map.85 = (bf16[20,2,256,256]{3,2,1,0:T(8,128)(2,1)S(1)}, f32[20,256,128]{2,1,0:T(8,128)S(1)}, f32[20,256,128]{2,1,0:T(8,128)S(1)}) custom-call(f32[5,2,256]{2,1,0:T(2,128)S(1)} %get-tuple-element.32.bias_ref, bf16[20,256,128]{2,1,0:T(8,128)(2,1)} %bitcast.5, bf16[4,2,256,128]{3,2,1,0:T(8,128)(2,1)S(1)} %get-tuple-element.33.refs_0_, ...), custom_call_target="tpu_custom_call" | custom-call | flops 1342177280 | bytes 5242880 | tf_op jit(solution)/shard_map/pallas_call | solution.py:365
  18.1 3.3 %collective-permute-done.5.refs_2_ = bf16[2,2,256,128]{3,2,1,0:T(8,128)(2,1)S(1)} collective-permute-done((bf16[2,2,256,128]{3,2,1,0:T(8,128)(2,1)S(1)}, bf16[2,2,256,128]{3,2,1,0:T(8,128)(2,1)S(1)}, u32[]{:S(2)}, u32[]{:S(2)}) %collective-permute-start.5) | collective-permute-done | bytes 262176 | tf_op jit(solution)/shard_map/ppermute | solution.py:21
  21.4 1.2 %collective-permute-done.4.refs_1_ = bf16[2,2,256,128]{3,2,1,0:T(8,128)(2,1)S(1)} collective-permute-done((bf16[2,2,256,128]{3,2,1,0:T(8,128)(2,1)S(1)}, bf16[2,2,256,128]{3,2,1,0:T(8,128)(2,1)S(1)}, u32[]{:S(2)}, u32[]{:S(2)}) %collective-permute-start.4) | collective-permute-done | bytes 262176 | tf_op jit(solution)/shard_map/ppermute | solution.py:21
  22.5 10.9 %shard_map.86 = (bf16[20,256,128]{2,1,0:T(8,128)(2,1)}, f32[20,256,128]{2,1,0:T(8,128)S(1)}, f32[20,256,128]{2,1,0:T(8,128)S(1)}, bf16[4,2,256,128]{3,2,1,0:T(8,...) custom-call(f32[5,2,256]{2,1,0:T(2,128)S(1)} %get-tuple-element.32.bias_ref, ...), custom_call_target="tpu_custom_call" | custom-call | flops 3019898880 | bytes 2621440 | tf_op jit(solution)/shard_map/pallas_call | solution.py:380
  33.4 2.4 %collective-permute-start.7 = (bf16[2,2,256,128]{3,2,1,0:T(8,128)(2,1)S(1)}, bf16[2,2,256,128]{3,2,1,0:T(8,128)(2,1)S(1)}, u32[]{:S(2)}, u32[]{:S(2)}) collective-permute-start(bf16[2,2,256,128]{3,2,1,0:T(8,128)(2,1)S(1)} %get-tuple-element.47), channel_id=1, source_target_pairs={{0,4},{1,5},{2,6},{3,7},{4,0},{5,1},{6,2},{7,3},{8,12},{9,13},{10,... | collective-permute-start | bytes 786440 | tf_op jit(solution)/shard_map/ppermute | solution.py:21
  35.9 10.9 %shard_map.87 = (bf16[20,256,128]{2,1,0:T(8,128)(2,1)}, f32[20,256,128]{2,1,0:T(8,128)S(1)}, f32[20,256,128]{2,1,0:T(8,128)S(1)}, bf16[4,2,256,128]{3,2,1,0:T(8,...) custom-call(f32[5,2,256]{2,1,0:T(2,128)S(1)} %get-tuple-element.32.b, ...), custom_call_target="tpu_custom_call", output_to_operand_aliasing={{0}: (8, {}), {1}: (9, {}), {2}: (10, {}), {3}: (11, {})} | custom-call | flops 3019898880 | bytes 2621440 | tf_op jit(solution)/shard_map/pallas_call | solution.py:380
  46.7 0.5 collective-permute-start.10
  47.3 0.5 collective-permute-start.8
  47.8 2.0 %collective-permute-start.9 = (bf16[2,2,256,128]{3,2,1,0:T(8,128)(2,1)S(1)}, bf16[2,2,256,128]{3,2,1,0:T(8,128)(2,1)S(1)}, u32[]{:S(2)}, u32[]{:S(2)}) collective-permute-start(bf16[2,2,256,128]{3,2,1,0:T(8,128)(2,1)S(1)} %get-tuple-element.52), channel_id=1, source_target_pairs={{0,4},{1,5},{2,6},{3,7},{4,0},{5,1},{6,2},{7,3},{8,12},{9,13},{10,... | collective-permute-start | bytes 786440 | tf_op jit(solution)/shard_map/ppermute | solution.py:21
  49.8 5.3 %shard_map.88 = (bf16[20,256,128]{2,1,0:T(8,128)(2,1)}, bf16[2,2,256,128]{3,2,1,0:T(8,128)(2,1)S(1)}, bf16[2,2,256,128]{3,2,1,0:T(8,128)(2,1)S(1)}) custom-call(bf16[20,256,128]{2,1,0:T(8,128)(2,1)} %bitcast.8, bf16[20,256,128]{2,1,0:T(8,128)(2,1)} %bitcast.12, bf16[20,2,256,256]{3,2,1,0:T(8,128)(2,1)S(1)} %get-tuple-element.43.e_ref, ...), custom_call_target="tpu_custom_call" | custom-call | flops 1342177280 | bytes 2621440 | tf_op jit(solution)/shard_map/pallas_call | solution.py:396
  55.0 5.1 %shard_map.89 = (bf16[20,256,128]{2,1,0:T(8,128)(2,1)}, bf16[2,2,256,128]{3,2,1,0:T(8,128)(2,1)S(1)}, bf16[2,2,256,128]{3,2,1,0:T(8,128)(2,1)S(1)}) custom-call(bf16[20,256,128]{2,1,0:T(8,128)(2,1)} %bitcast.9, bf16[20,256,128]{2,1,0:T(8,128)(2,1)} %bitcast.13, ...), custom_call_target="tpu_custom_call", output_to_operand_aliasing={{0}: (7, {})} | custom-call | flops 1342177280 | bytes 2621440 | tf_op jit(solution)/shard_map/pallas_call | solution.py:396
  60.1 0.5 collective-permute-start.11
  60.6 0.1 collective-permute-done.8.refs_2_
  60.8 0.2 shard_map.90.refs_0_
  61.0 0.7 %collective-permute-done.12.refs_3_ = bf16[2,2,256,128]{3,2,1,0:T(8,128)(2,1)S(1)} collective-permute-done((bf16[2,2,256,128]{3,2,1,0:T(8,128)(2,1)S(1)}, bf16[2,2,256,128]{3,2,1,0:T(8,128)(2,1)S(1)}, u32[]{:S(2)}, u32[]{:S(2)}) %collective-permute-start.12) | collective-permute-done | bytes 262176 | tf_op jit(solution)/shard_map/ppermute | solution.py:21
  61.6 0.4 collective-permute-done.11.refs_1_
  62.0 1.1 %shard_map.91 = (bf16[256,4,128]{2,1,0:T(4,128)(2,1)}, bf16[256,4,128]{2,1,0:T(4,128)(2,1)}) custom-call(f32[4,2,256,128]{3,2,1,0:T(8,128)S(1)} %shard_map.90.refs_0_, bf16[2,2,256,128]{3,2,1,0:T(8,128)(2,1)S(1)} %collective-permute-done.11.refs_1_, bf16[2,2,256,128]{3,2,1,0:T(8,128)(2,1)S(1)} %get-tuple-element.55.refs_2_, ...), custom_call_target="tpu_custom_call" | custom-call | bytes 3145728 | tf_op jit(solution)/shard_map/pallas_call | solution.py:114
  (10 shorter events, 0.0 us)
Async XLA Ops:
  2.0 7.6 %collective-permute-start = (bf16[4,2,256,128]{3,2,1,0:T(8,128)(2,1)S(1)}, bf16[4,2,256,128]{3,2,1,0:T(8,128)(2,1)S(1)}, u32[]{:S(2)}, u32[]{:S(2)}) collective-permute-start(bf16[4,2,256,128]{3,2,1,0:T(8,128)(2,1)S(1)} %get-tuple-element.33.refs_0_), channel_id=1, source_target_pairs={{0,1},{1,0},{2,3},{3,2},{4,5},{5,4},{6,7},{7,6},{8,9},{9,8},{10,11... | collective-permute-start | bytes 1572872 | tf_op jit(solution)/shard_map/ppermute | solution.py:21
  2.5 20.0 %collective-permute-start.1 = (bf16[4,2,256,128]{3,2,1,0:T(8,128)(2,1)S(1)}, bf16[4,2,256,128]{3,2,1,0:T(8,128)(2,1)S(1)}, u32[]{:S(2)}, u32[]{:S(2)}) collective-permute-start(bf16[4,2,256,128]{3,2,1,0:T(8,128)(2,1)S(1)} %get-tuple-element.33.refs_0_), channel_id=1, source_target_pairs={{0,2},{1,3},{2,0},{3,1},{4,6},{5,7},{6,4},{7,5},{8,10},{9,11},{10,... | collective-permute-start | bytes 1572872 | tf_op jit(solution)/shard_map/ppermute | solution.py:21
  5.1 16.2 %collective-permute-start.5 = (bf16[2,2,256,128]{3,2,1,0:T(8,128)(2,1)S(1)}, bf16[2,2,256,128]{3,2,1,0:T(8,128)(2,1)S(1)}, u32[]{:S(2)}, u32[]{:S(2)}) collective-permute-start(bf16[2,2,256,128]{3,2,1,0:T(8,128)(2,1)S(1)} %get-tuple-element.37), channel_id=1, source_target_pairs={{0,8},{1,9},{2,10},{3,11},{4,12},{5,13},{6,14},{7,15},{8,0},{9,1},... | collective-permute-start | bytes 786440 | tf_op jit(solution)/shard_map/ppermute | solution.py:21
  7.7 14.8 %collective-permute-start.4 = (bf16[2,2,256,128]{3,2,1,0:T(8,128)(2,1)S(1)}, bf16[2,2,256,128]{3,2,1,0:T(8,128)(2,1)S(1)}, u32[]{:S(2)}, u32[]{:S(2)}) collective-permute-start(bf16[2,2,256,128]{3,2,1,0:T(8,128)(2,1)S(1)} %get-tuple-element.37), channel_id=1, source_target_pairs={{0,4},{1,5},{2,6},{3,7},{4,0},{5,1},{6,2},{7,3},{8,12},{9,13},{10,... | collective-permute-start | bytes 786440 | tf_op jit(solution)/shard_map/ppermute | solution.py:21
  9.3 26.5 %collective-permute-start.3 = (bf16[2,2,256,128]{3,2,1,0:T(8,128)(2,1)S(1)}, bf16[2,2,256,128]{3,2,1,0:T(8,128)(2,1)S(1)}, u32[]{:S(2)}, u32[]{:S(2)}) collective-permute-start(bf16[2,2,256,128]{3,2,1,0:T(8,128)(2,1)S(1)} %get-tuple-element.36), channel_id=1, source_target_pairs={{0,8},{1,9},{2,10},{3,11},{4,12},{5,13},{6,14},{7,15},{8,0},{9,1},... | collective-permute-start | bytes 786440 | tf_op jit(solution)/shard_map/ppermute | solution.py:21
  9.6 26.2 %collective-permute-start.2 = (bf16[2,2,256,128]{3,2,1,0:T(8,128)(2,1)S(1)}, bf16[2,2,256,128]{3,2,1,0:T(8,128)(2,1)S(1)}, u32[]{:S(2)}, u32[]{:S(2)}) collective-permute-start(bf16[2,2,256,128]{3,2,1,0:T(8,128)(2,1)S(1)} %get-tuple-element.36), channel_id=1, source_target_pairs={{0,4},{1,5},{2,6},{3,7},{4,0},{5,1},{6,2},{7,3},{8,12},{9,13},{10,... | collective-permute-start | bytes 786440 | tf_op jit(solution)/shard_map/ppermute | solution.py:21
  33.4 16.4 %collective-permute-start.6 = (bf16[2,2,256,128]{3,2,1,0:T(8,128)(2,1)S(1)}, bf16[2,2,256,128]{3,2,1,0:T(8,128)(2,1)S(1)}, u32[]{:S(2)}, u32[]{:S(2)}) collective-permute-start(bf16[2,2,256,128]{3,2,1,0:T(8,128)(2,1)S(1)} %get-tuple-element.46), channel_id=1, source_target_pairs={{0,8},{1,9},{2,10},{3,11},{4,12},{5,13},{6,14},{7,15},{8,0},{9,1},... | collective-permute-start | bytes 786440 | tf_op jit(solution)/shard_map/ppermute | solution.py:21
  33.4 16.4 %collective-permute-start.7 = (bf16[2,2,256,128]{3,2,1,0:T(8,128)(2,1)S(1)}, bf16[2,2,256,128]{3,2,1,0:T(8,128)(2,1)S(1)}, u32[]{:S(2)}, u32[]{:S(2)}) collective-permute-start(bf16[2,2,256,128]{3,2,1,0:T(8,128)(2,1)S(1)} %get-tuple-element.47), channel_id=1, source_target_pairs={{0,4},{1,5},{2,6},{3,7},{4,0},{5,1},{6,2},{7,3},{8,12},{9,13},{10,... | collective-permute-start | bytes 786440 | tf_op jit(solution)/shard_map/ppermute | solution.py:21
  46.7 14.0 %collective-permute-start.10 = (bf16[4,2,256,128]{3,2,1,0:T(8,128)(2,1)S(1)}, bf16[4,2,256,128]{3,2,1,0:T(8,128)(2,1)S(1)}, u32[]{:S(2)}, u32[]{:S(2)}) collective-permute-start(bf16[4,2,256,128]{3,2,1,0:T(8,128)(2,1)S(1)} %get-tuple-element.53), channel_id=1, source_target_pairs={{0,2},{1,3},{2,0},{3,1},{4,6},{5,7},{6,4},{7,5},{8,10},{9,11},{10,... | collective-permute-start | bytes 1572872 | tf_op jit(solution)/shard_map/ppermute | solution.py:21
  47.3 13.5 %collective-permute-start.8 = (bf16[2,2,256,128]{3,2,1,0:T(8,128)(2,1)S(1)}, bf16[2,2,256,128]{3,2,1,0:T(8,128)(2,1)S(1)}, u32[]{:S(2)}, u32[]{:S(2)}) collective-permute-start(bf16[2,2,256,128]{3,2,1,0:T(8,128)(2,1)S(1)} %get-tuple-element.51), channel_id=1, source_target_pairs={{0,8},{1,9},{2,10},{3,11},{4,12},{5,13},{6,14},{7,15},{8,0},{9,1},... | collective-permute-start | bytes 786440 | tf_op jit(solution)/shard_map/ppermute | solution.py:21
  47.8 13.0 %collective-permute-start.9 = (bf16[2,2,256,128]{3,2,1,0:T(8,128)(2,1)S(1)}, bf16[2,2,256,128]{3,2,1,0:T(8,128)(2,1)S(1)}, u32[]{:S(2)}, u32[]{:S(2)}) collective-permute-start(bf16[2,2,256,128]{3,2,1,0:T(8,128)(2,1)S(1)} %get-tuple-element.52), channel_id=1, source_target_pairs={{0,4},{1,5},{2,6},{3,7},{4,0},{5,1},{6,2},{7,3},{8,12},{9,13},{10,... | collective-permute-start | bytes 786440 | tf_op jit(solution)/shard_map/ppermute | solution.py:21
  60.1 1.5 %collective-permute-start.12 = (bf16[2,2,256,128]{3,2,1,0:T(8,128)(2,1)S(1)}, bf16[2,2,256,128]{3,2,1,0:T(8,128)(2,1)S(1)}, u32[]{:S(2)}, u32[]{:S(2)}) collective-permute-start(bf16[2,2,256,128]{3,2,1,0:T(8,128)(2,1)S(1)} %get-tuple-element.56), channel_id=1, source_target_pairs={{0,1},{1,0},{2,3},{3,2},{4,5},{5,4},{6,7},{7,6},{8,9},{9,8},{10,11... | collective-permute-start | bytes 786440 | tf_op jit(solution)/shard_map/ppermute | solution.py:21
  60.1 1.9 %collective-permute-start.11 = (bf16[2,2,256,128]{3,2,1,0:T(8,128)(2,1)S(1)}, bf16[2,2,256,128]{3,2,1,0:T(8,128)(2,1)S(1)}, u32[]{:S(2)}, u32[]{:S(2)}) collective-permute-start(bf16[2,2,256,128]{3,2,1,0:T(8,128)(2,1)S(1)} %get-tuple-element.54), channel_id=1, source_target_pairs={{0,1},{1,0},{2,3},{3,2},{4,5},{5,4},{6,7},{7,6},{8,9},{9,8},{10,11... | collective-permute-start | bytes 786440 | tf_op jit(solution)/shard_map/ppermute | solution.py:21

commit v4 on v3

--- a/solution.py
+++ b/solution.py
@@ -129,57 +129,59 @@
     return jnp.concatenate([x[a * width : (a + 1) * width] + bias_ref[s, a : a + 1] for a in range(blocks)], axis=0)
 
 
-def pair(first, second, shape):
-    lane = lax.broadcasted_iota(jnp.int32, shape, 1)
-    return jnp.where(lane < shape[1] // 2, first, second)
-
-
-def unpair(array):
-    half = array.shape[1] // 2
-    return array[:, 0:1], array[:, half : half + 1]
+def twice(array):
+    return jnp.concatenate([array, array], axis=1)
+
+
+def fill_values(kv_refs, v_ref):
+    for n, ref in enumerate(kv_refs):
+        value = ref[0, 1]
+        v_ref[n] = jnp.concatenate([value, jnp.ones_like(value)], axis=1)
 
 
 def local_kernel(softmax_scale, bias_ref, q_ref, *refs):
     sources = len(LOCAL)
     kv_refs = refs[:sources]
-    e_ref, o_ref, stat_ref, x_ref = refs[sources:]
+    e_ref, o_ref, stat_ref, x_ref, v_ref = refs[sources:]
     scale2 = softmax_scale * LOG2E
     head_group, tokens, size = q_ref.shape
     state = {}
+    fill_values(kv_refs, v_ref)
 
     def scores(g, n):
         x = scores_of(q_ref[g], kv_refs[n][0, 0], bias_ref, LOCAL[n])
-        x_ref[g % 2, n] = x
+        x_ref[g % 3, n] = x
         state["max", g] = jnp.maximum(state["max", g], x) if n else x
 
     def scores_end(g):
         state["top", g] = jnp.max(state.pop(("max", g)), axis=1, keepdims=True) * scale2
 
     def forward(g, n):
-        e = jnp.exp2(x_ref[g % 2, n] * scale2 - state["top", g])
+        e = jnp.exp2(x_ref[g % 3, n] * scale2 - state["top", g])
         narrow = e.astype(jnp.bfloat16)
         e_ref[g, n] = narrow
-        state["total", g] = state["total", g] + e if n else e
-        part = product(narrow, kv_refs[n][0, 1])
+        part = product(narrow, v_ref[n])
         state["out", g] = state["out", g] + part if n else part
 
     def forward_end(g):
-        o_ref[g] = state.pop(("out", g))
-        total = jnp.sum(state.pop(("total", g)), axis=1, keepdims=True)
-        stat_ref[g] = pair(state["top", g], total, (tokens, size))
+        out = state.pop(("out", g))
+        o_ref[g] = out[:, :size]
+        stat_ref[g, 0] = jnp.broadcast_to(state["top", g], (tokens, size))
+        stat_ref[g, 1] = out[:, size:]
 
     every = range(sources)
-    for n in every:
-        scores(0, n)
-    scores_end(0)
+    for g in range(2):
+        for n in every:
+            scores(g, n)
+        scores_end(g)
     for g in range(head_group):
         for n in every:
             forward(g, n)
-            if g + 1 < head_group:
-                scores(g + 1, n)
+            if g + 2 < head_group:
+                scores(g + 2, n)
         forward_end(g)
-        if g + 1 < head_group:
-            scores_end(g + 1)
+        if g + 2 < head_group:
+            scores_end(g + 2)
 
 
 def remote_kernel(softmax_scale, unused, bias_ref, q_ref, do_ref, part_ref, stat_ref, *refs):
@@ -188,51 +190,51 @@
     refs = refs[sources + unused :]
     o_ref, dq_ref, row_ref = refs[:3]
     term_refs = refs[3 : sources + 3]
-    dk_ref, dv_ref, x_ref, e_ref, p_ref = refs[sources + 3 :]
+    dk_ref, dv_ref, x_ref, e_ref, p_ref, v_ref = refs[sources + 3 :]
     scale2 = softmax_scale * LOG2E
     head_group, tokens, size = q_ref.shape
     state = {}
+    fill_values(kv_refs, v_ref)
 
     def key(n):
         return kv_refs[n][0, 0]
 
-    def value(n):
-        return kv_refs[n][0, 1]
-
     def scores(g, n):
         x = scores_of(q_ref[g], key(n), bias_ref, REMOTE[n])
-        x_ref[g % 2, n] = x
+        x_ref[g % 3, n] = x
         state["max", g] = jnp.maximum(state["max", g], x) if n else x
-        p_ref[g % 2, n] = product_nt(do_ref[g], value(n))
+
+    def dprob(g, n):
+        p_ref[g % 2, n] = product_nt(do_ref[g], kv_refs[n][0, 1])
 
     def scores_end(g):
-        local, total = unpair(stat_ref[g])
+        local, total = stat_ref[g, 0], stat_ref[g, 1]
         top = jnp.maximum(jnp.max(state.pop(("max", g)), axis=1, keepdims=True) * scale2, local)
         state["top", g] = top
         state["share", g] = jnp.exp2(local - top)
         state["part", g] = total * state["share", g]
 
     def forward(g, n):
-        e = jnp.exp2(x_ref[g % 2, n] * scale2 - state["top", g])
+        e = jnp.exp2(x_ref[g % 3, n] * scale2 - twice(state["top", g]))
         narrow = e.astype(jnp.bfloat16)
         e_ref[g % 2, n] = narrow
-        state["total", g] = state["total", g] + e if n else e
-        part = product(narrow, value(n))
+        part = product(narrow, v_ref[n])
         state["out", g] = state["out", g] + part if n else part
 
     def forward_end(g):
         q, do = q_ref[g], do_ref[g].astype(jnp.float32)
-        total = jnp.sum(state.pop(("total", g)), axis=1, keepdims=True) + state["part", g]
-        inverse = 1.0 / total
-        attended = state.pop(("out", g)) + part_ref[g] * state["share", g]
-        attended = (attended * inverse).astype(jnp.bfloat16)
+        out = state.pop(("out", g))
+        share = state.pop(("share", g))
+        inverse = 1.0 / (out[:, size:] + state.pop(("part", g)))
+        attended = ((out[:, :size] + part_ref[g] * share) * inverse).astype(jnp.bfloat16)
         o_ref[g] = attended
         delta = jnp.sum(do * attended.astype(jnp.float32), axis=1, keepdims=True)
         state["delta", g] = delta
-        row_ref[g] = pair(state["share", g] * inverse, delta, (tokens, size))
-        state["q", g] = (q.astype(jnp.float32) * (inverse * softmax_scale)).astype(jnp.bfloat16).T
+        row_ref[g, 0] = share * inverse
+        row_ref[g, 1] = jnp.broadcast_to(delta, (tokens, size))
+        state["scale", g] = inverse * softmax_scale
+        state["q", g] = (q.astype(jnp.float32) * state["scale", g]).astype(jnp.bfloat16).T
         state["do", g] = (do * inverse).astype(jnp.bfloat16).T
-        state["scale", g] = inverse * softmax_scale
 
     def backward(g, n):
         e = e_ref[g % 2, n]
@@ -255,22 +257,23 @@
         dq_ref[g] = state.pop(("dq", g)) * state["scale", g]
 
     every = range(sources)
-    for n in every:
-        scores(0, n)
-    scores_end(0)
+    for g in range(2):
+        for n in every:
+            scores(g, n)
+        scores_end(g)
     for g in range(head_group):
         for n in every:
             forward(g, n)
-            if g:
+            if g + 2 < head_group:
+                scores(g + 2, n)
+            dprob(g, n)
+        forward_end(g)
+        if g + 2 < head_group:
+            scores_end(g + 2)
+        if g:
+            for n in every:
                 backward(g - 1, n)
-        if g:
             backward_end(g - 1)
-        if g + 1 < head_group:
-            for n in every:
-                scores(g + 1, n)
-        forward_end(g)
-        if g + 1 < head_group:
-            scores_end(g + 1)
     for n in every:
         backward(head_group - 1, n)
     backward_end(head_group - 1)
@@ -290,8 +293,8 @@
         p_ref[g % 2, n] = product_nt(do_ref[g], kv_refs[n][0, 1])
 
     def rows(g):
-        share, delta = unpair(row_ref[g])
-        state["delta", g] = delta
+        share = row_ref[g, 0]
+        state["delta", g] = twice(row_ref[g, 1])
         state["scale", g] = share * softmax_scale
         state["q", g] = (q_ref[g].astype(jnp.float32) * state["scale", g]).astype(jnp.bfloat16).T
         state["do", g] = (do_ref[g].astype(jnp.float32) * share).astype(jnp.bfloat16).T
@@ -318,13 +321,13 @@
         dprob(0, n)
     rows(0)
     for g in range(head_group):
+        if g + 1 < head_group:
+            rows(g + 1)
         for n in every:
             backward(g, n)
             if g + 1 < head_group:
                 dprob(g + 1, n)
         dq_ref[g] = (part_ref[g] + state.pop(("dq", g)) * state["scale", g]).astype(jnp.bfloat16)
-        if g + 1 < head_group:
-            rows(g + 1)
 
 
 def cost(products, heads, head_group, tokens, sources, size):
@@ -348,17 +351,21 @@
     def exps(first):
         return pl.BlockSpec((head_group, len(LOCAL), tokens, tokens), lambda j: (first + j, 0, 0, 0))
 
+    def columns(first):
+        return pl.BlockSpec((head_group, 2, tokens, size), lambda j: (first + j, 0, 0, 0))
+
     scale = size ** (-0.5)
     query_heads = heads_all * head_group
     wide = jax.ShapeDtypeStruct((query_heads, tokens, size), jnp.float32)
+    double = jax.ShapeDtypeStruct((query_heads, 2, tokens, size), jnp.float32)
     narrow = jax.ShapeDtypeStruct((query_heads, tokens, size), jnp.bfloat16)
     params = pltpu.CompilerParams(vmem_limit_bytes=VMEM_LIMIT)
 
     def term(count):
         return jax.ShapeDtypeStruct((count, 2, tokens, size), jnp.bfloat16)
 
-    def square(count, kind=jnp.float32):
-        return pltpu.VMEM((2, count, tokens, tokens), kind)
+    def square(depth, count, kind=jnp.float32):
+        return pltpu.VMEM((depth, count, tokens, tokens), kind)
 
     def local(own):
         n = len(LOCAL)
@@ -366,9 +373,9 @@
             functools.partial(local_kernel, scale),
             grid=(heads_all,),
             in_specs=[VMEM, rows(0)] + [block(0, 0)] * n,
-            out_specs=[exps(0), rows(0), rows(0)],
-            out_shape=[jax.ShapeDtypeStruct((query_heads, n, tokens, tokens), jnp.bfloat16), wide, wide],
-            scratch_shapes=[square(n)],
+            out_specs=[exps(0), rows(0), columns(0)],
+            out_shape=[jax.ShapeDtypeStruct((query_heads, n, tokens, tokens), jnp.bfloat16), wide, double],
+            scratch_shapes=[square(3, n), pltpu.VMEM((n, tokens, 2 * size), jnp.bfloat16)],
             compiler_params=params,
             cost_estimate=cost(2, heads_all, head_group, tokens, n, size),
         )(bias, in_hbm(queries), *own)
@@ -376,15 +383,15 @@
     def remote(heads, part, stat, others, chain):
         first, last = heads
         n = len(REMOTE)
-        whole = [rows(first)] * 3 + [block(first, 0)]
+        whole = [rows(first)] * 2 + [columns(first), block(first, 0)]
         return pl.pallas_call(
             functools.partial(remote_kernel, scale, len(chain)),
             grid=(last - first,),
-            in_specs=[VMEM] + [rows(first)] * 4 + [block(first, begin) for _, begin in others] + [ANY] * len(chain),
+            in_specs=[VMEM] + [rows(first)] * 3 + [columns(first)] + [block(first, begin) for _, begin in others] + [ANY] * len(chain),
             out_specs=whole + [block(0, 0)] * (n - 1),
-            out_shape=[narrow, wide, wide, term(heads_all)] + [term(last - first)] * (n - 1),
+            out_shape=[narrow, wide, double, term(heads_all)] + [term(last - first)] * (n - 1),
             scratch_shapes=[pltpu.VMEM((n, size, tokens), jnp.float32)] * 2
-            + [square(n), square(n, jnp.bfloat16), square(n)],
+            + [square(3, n), square(2, n, jnp.bfloat16), square(2, n), pltpu.VMEM((n, tokens, 2 * size), jnp.bfloat16)],
             input_output_aliases={5 + n + i: i for i in range(len(chain))},
             compiler_params=params,
             cost_estimate=cost(6, last - first, head_group, tokens, n, size),
@@ -398,12 +405,12 @@
             grid=(last - first,),
             in_specs=[rows(first)] * 2
             + [exps(first)]
-            + [rows(first)] * 2
+            + [rows(first), columns(first)]
             + [block(first, 0)] * n
             + [ANY] * len(chain),
             out_specs=[rows(first)] + [block(0, 0)] * n,
             out_shape=[narrow] + [term(last - first)] * n,
-            scratch_shapes=[pltpu.VMEM((n, size, tokens), jnp.float32)] * 2 + [square(n)],
+            scratch_shapes=[pltpu.VMEM((n, size, tokens), jnp.float32)] * 2 + [square(2, n)],
             input_output_aliases={5 + n + i: i for i in range(len(chain))},
             compiler_params=params,
             cost_estimate=cost(4, last - first, head_group, tokens, n, size),
@@ -424,15 +431,19 @@
     groups = (whole,) + HALVES
     bias, *arrays = pack(me, block_mask, keys, values, groups, bits)
     packed = dict(zip(groups, arrays))
-    far = {(heads, bit): from_partner(packed[heads], "seq", bit) for heads in HALVES for bit in reversed(bits[2:])}
+    far = {(HALVES[0], bit): from_partner(packed[HALVES[0]], "seq", bit) for bit in reversed(bits[2:])}
     core = from_partner(packed[whole], "seq", bits[0])
-    near = from_partner(packed[whole], "seq", bits[1])
+    near = {HALVES[0]: from_partner(packed[HALVES[0]], "seq", bits[1])}
     local, remote, rest = attend(bias, q, dout, kv_heads, head_group)
     own = [packed[whole], core]
     e, part, stat = local(own)
+    for heads in HALVES[1:]:
+        later = lax.optimization_barrier((packed[heads], stat))[0]
+        far.update({(heads, bit): from_partner(later, "seq", bit) for bit in reversed(bits[2:])})
+        near[heads] = from_partner(later, "seq", bits[1])
     chain, sent, terms, term_groups = [], [], [], []
     for heads in HALVES:
-        others = [(near, 0)] + [(far[heads, bit], heads[0]) for bit in bits[2:]]
+        others = [(near[heads], heads[0])] + [(far[heads, bit], heads[0]) for bit in bits[2:]]
         results = remote(heads, part, stat, others, chain)
         chain = results[:4]
         back = results[4:]

time: 63.4 us -> 58 us (0.915)
  Pallas kernels: 42.8 us -> 35.5 us
  starting transfers between devices: 14 us -> 16.5 us
    pallas_call x2, Pallas kernels: 21.8 us -> 17.7 us  [remote(): pl.pallas_call(functools.partial(remote_kernel, scale, len(chain)), grid=...]
    ppermute x13 -> x14, starting transfers between devices: 14 us -> 16.5 us  [from_partner(): return lax.ppermute(value, axis, pairs)]
    pallas_call x1, Pallas kernels: 7.98 us -> 5.74 us  [local(): pl.pallas_call(functools.partial(local_kernel, scale), grid=(heads_all,),...]
    pallas_call x2, Pallas kernels: 10.3 us -> 9.46 us  [rest(): pl.pallas_call(functools.partial(rest_kernel, scale, len(chain)), grid=(l...]
    ppermute x13 -> x14, waiting for transfers between devices: 5.65 us -> 5.02 us  [from_partner(): return lax.ppermute(value, axis, pairs)]
  transfers between devices with their start and end apart: 13 -> 14, of which waited for: 5 -> 2; matrix products, arithmetic and copies ran while one was open for 0% -> 0% of each run, Pallas kernels for 64% -> 57%
where the time goes in v4:
time: 58 us; the launch traced here: 57.7 us
  Pallas kernels  35.5 us (61%)
  starting transfers between devices  16.5 us (28%)
  waiting for transfers between devices  5.02 us (9%)
  between operations  0.69 us (1%)
    pallas_call x2, Pallas kernels, remote(): pl.pallas_call(functools.partial(remote_kernel, scale, len(chain)), grid=...  17.7 us
    ppermute x14, starting transfers between devices, from_partner(): return lax.ppermute(value, axis, pairs)  16.5 us
    pallas_call x2, Pallas kernels, rest(): pl.pallas_call(functools.partial(rest_kernel, scale, len(chain)), grid=(l...  9.46 us
    pallas_call x1, Pallas kernels, local(): pl.pallas_call(functools.partial(local_kernel, scale), grid=(heads_all,),...  5.74 us
    ppermute x14, waiting for transfers between devices, from_partner(): return lax.ppermute(value, axis, pairs)  5.02 us
    pallas_call x1, Pallas kernels, pack(): pl.pallas_call(functools.partial(pack_kernel, groups, bits), in_specs=[SM...  1.37 us
  transfers between devices with their start and end apart: 14, of which 2 were waited for; matrix products, arithmetic and copies ran while one was open for 0% of the time, Pallas kernels for 57%

profile of v4, /device:TPU:0, one launch (start us, length us, event | category | flops | bytes accessed | tf_op | source)
XLA Modules:
  0.0 57.7 jit_solution(2349783696223391486)
XLA Ops:
  0.6 1.4 %shard_map.84 = (f32[5,2,256]{2,1,0:T(2,128)S(1)}, bf16[4,2,256,128]{3,2,1,0:T(8,128)(2,1)S(1)}, bf16[2,2,256,128]{3,2,1,0:T(8,128)(2,1)S(1)}, bf16[2,2,256,128]{3,2,1,0:T(8,128)(2,1)S(1)}) custom-call(s32[1]{0:T(128)} %bitcast.me_ref, s32[2,32]{1,0:T(2,128)} %mask_ref.1, bf16[256,4,128]{2,1,0:T(4,128)(2,1)} %k_ref.1, bf16[256,4,128]{2,1,0:T(4,128)(2,1)} %v_ref.1), custom_call_target="tpu_custom_call" | custom-call | bytes 1572864 | tf_op jit(solution)/shard_map/pallas_call | solution.py:72
  2.0 0.5 collective-permute-start
  2.5 3.7 %collective-permute-start.6 = (bf16[2,2,256,128]{3,2,1,0:T(8,128)(2,1)S(1)}, bf16[2,2,256,128]{3,2,1,0:T(8,128)(2,1)S(1)}, u32[]{:S(2)}, u32[]{:S(2)}) collective-permute-start(bf16[2,2,256,128]{3,2,1,0:T(8,128)(2,1)S(1)} %get-tuple-element.39), channel_id=1, source_target_pairs={{0,8},{1,9},{2,10},{3,11},{4,12},{5,13},{6,14},{7,15},{8,0},{9,1},... | collective-permute-start | bytes 786440 | tf_op jit(solution)/shard_map/ppermute | solution.py:21
  6.2 1.6 %collective-permute-start.5 = (bf16[2,2,256,128]{3,2,1,0:T(8,128)(2,1)S(1)}, bf16[2,2,256,128]{3,2,1,0:T(8,128)(2,1)S(1)}, u32[]{:S(2)}, u32[]{:S(2)}) collective-permute-start(bf16[2,2,256,128]{3,2,1,0:T(8,128)(2,1)S(1)} %get-tuple-element.39), channel_id=1, source_target_pairs={{0,4},{1,5},{2,6},{3,7},{4,0},{5,1},{6,2},{7,3},{8,12},{9,13},{10,... | collective-permute-start | bytes 786440 | tf_op jit(solution)/shard_map/ppermute | solution.py:21
  7.8 1.5 %collective-permute-start.4 = (bf16[2,2,256,128]{3,2,1,0:T(8,128)(2,1)S(1)}, bf16[2,2,256,128]{3,2,1,0:T(8,128)(2,1)S(1)}, u32[]{:S(2)}, u32[]{:S(2)}) collective-permute-start(bf16[2,2,256,128]{3,2,1,0:T(8,128)(2,1)S(1)} %get-tuple-element.39), channel_id=1, source_target_pairs={{0,2},{1,3},{2,0},{3,1},{4,6},{5,7},{6,4},{7,5},{8,10},{9,11},{10,... | collective-permute-start | bytes 786440 | tf_op jit(solution)/shard_map/ppermute | solution.py:21
  9.3 0.0 collective-permute-done.refs_1_
  9.3 5.7 %shard_map.85 = (bf16[20,2,256,256]{3,2,1,0:T(8,128)(2,1)S(1)}, f32[20,256,128]{2,1,0:T(8,128)S(1)}, f32[20,2,256,128]{3,2,1,0:T(8,128)S(1)}) custom-call(f32[5,2,256]{2,1,0:T(2,128)S(1)} %get-tuple-element.33.bias_ref, bf16[20,256,128]{2,1,0:T(8,128)(2,1)} %bitcast.5, bf16[4,2,256,128]{3,2,1,0:T(8,128)(2,1)S(1)} %get-tuple-element.34.refs_0_, ...), custom_call_target="tpu_custom_call" | custom-call | flops 1342177280 | bytes 5242880 | tf_op jit(solution)/shard_map/pallas_call | solution.py:372
  15.0 0.4 collective-permute-start.3
  15.4 0.4 collective-permute-start.2
  15.9 3.2 %collective-permute-done.6.refs_2_ = bf16[2,2,256,128]{3,2,1,0:T(8,128)(2,1)S(1)} collective-permute-done((bf16[2,2,256,128]{3,2,1,0:T(8,128)(2,1)S(1)}, bf16[2,2,256,128]{3,2,1,0:T(8,128)(2,1)S(1)}, u32[]{:S(2)}, u32[]{:S(2)}) %collective-permute-start.6) | collective-permute-done | bytes 262176 | tf_op jit(solution)/shard_map/ppermute | solution.py:21
  19.1 1.8 %collective-permute-start.1 = (bf16[2,2,256,128]{3,2,1,0:T(8,128)(2,1)S(1)}, bf16[2,2,256,128]{3,2,1,0:T(8,128)(2,1)S(1)}, u32[]{:S(2)}, u32[]{:S(2)}) collective-permute-start(bf16[2,2,256,128]{3,2,1,0:T(8,128)(2,1)S(1)} %get-tuple-element.38), channel_id=1, source_target_pairs={{0,2},{1,3},{2,0},{3,1},{4,6},{5,7},{6,4},{7,5},{8,10},{9,11},{10,... | collective-permute-start | bytes 786440 | tf_op jit(solution)/shard_map/ppermute | solution.py:21
  20.8 0.0 collective-permute-done.4.refs_0_
  20.9 8.9 %shard_map.86 = (bf16[20,256,128]{2,1,0:T(8,128)(2,1)}, f32[20,256,128]{2,1,0:T(8,128)S(1)}, f32[20,2,256,128]{3,2,1,0:T(8,128)S(1)}, bf16[4,2,256,128]{3,2,1,0:...) custom-call(f32[5,2,256]{2,1,0:T(2,128)S(1)} %get-tuple-element.33.bias_ref, ...), custom_call_target="tpu_custom_call" | custom-call | flops 3019898880 | bytes 2621440 | tf_op jit(solution)/shard_map/pallas_call | solution.py:387
  29.7 4.0 %collective-permute-start.8 = (bf16[2,2,256,128]{3,2,1,0:T(8,128)(2,1)S(1)}, bf16[2,2,256,128]{3,2,1,0:T(8,128)(2,1)S(1)}, u32[]{:S(2)}, u32[]{:S(2)}) collective-permute-start(bf16[2,2,256,128]{3,2,1,0:T(8,128)(2,1)S(1)} %get-tuple-element.49), channel_id=1, source_target_pairs={{0,4},{1,5},{2,6},{3,7},{4,0},{5,1},{6,2},{7,3},{8,12},{9,13},{10,... | collective-permute-start | bytes 786440 | tf_op jit(solution)/shard_map/ppermute | solution.py:21
  33.8 8.8 %shard_map.87 = (bf16[20,256,128]{2,1,0:T(8,128)(2,1)}, f32[20,256,128]{2,1,0:T(8,128)S(1)}, f32[20,2,256,128]{3,2,1,0:T(8,128)S(1)}, bf16[4,2,256,128]{3,2,1,0:...) custom-call(f32[5,2,256]{2,1,0:T(2,128)S(1)} %get-tuple-element.33.b, ...), custom_call_target="tpu_custom_call", output_to_operand_aliasing={{0}: (8, {}), {1}: (9, {}), {2}: (10, {}), {3}: (11, {})} | custom-call | flops 3019898880 | bytes 2621440 | tf_op jit(solution)/shard_map/pallas_call | solution.py:387
  42.6 0.5 collective-permute-start.11
  43.1 0.0 collective-permute-start.9
  43.1 1.5 %collective-permute-start.10 = (bf16[2,2,256,128]{3,2,1,0:T(8,128)(2,1)S(1)}, bf16[2,2,256,128]{3,2,1,0:T(8,128)(2,1)S(1)}, u32[]{:S(2)}, u32[]{:S(2)}) collective-permute-start(bf16[2,2,256,128]{3,2,1,0:T(8,128)(2,1)S(1)} %get-tuple-element.54), channel_id=1, source_target_pairs={{0,4},{1,5},{2,6},{3,7},{4,0},{5,1},{6,2},{7,3},{8,12},{9,13},{10,... | collective-permute-start | bytes 786440 | tf_op jit(solution)/shard_map/ppermute | solution.py:21
  44.6 4.7 %shard_map.88 = (bf16[20,256,128]{2,1,0:T(8,128)(2,1)}, bf16[2,2,256,128]{3,2,1,0:T(8,128)(2,1)S(1)}, bf16[2,2,256,128]{3,2,1,0:T(8,128)(2,1)S(1)}) custom-call(bf16[20,256,128]{2,1,0:T(8,128)(2,1)} %bitcast.8, bf16[20,256,128]{2,1,0:T(8,128)(2,1)} %bitcast.12, bf16[20,2,256,256]{3,2,1,0:T(8,128)(2,1)S(1)} %get-tuple-element.45.e_ref, ...), custom_call_target="tpu_custom_call" | custom-call | flops 1342177280 | bytes 2621440 | tf_op jit(solution)/shard_map/pallas_call | solution.py:403
  49.4 4.7 %shard_map.89 = (bf16[20,256,128]{2,1,0:T(8,128)(2,1)}, bf16[2,2,256,128]{3,2,1,0:T(8,128)(2,1)S(1)}, bf16[2,2,256,128]{3,2,1,0:T(8,128)(2,1)S(1)}) custom-call(bf16[20,256,128]{2,1,0:T(8,128)(2,1)} %bitcast.9, bf16[20,256,128]{2,1,0:T(8,128)(2,1)} %bitcast.13, ...), custom_call_target="tpu_custom_call", output_to_operand_aliasing={{0}: (7, {})} | custom-call | flops 1342177280 | bytes 2621440 | tf_op jit(solution)/shard_map/pallas_call | solution.py:403
  54.1 0.5 collective-permute-start.12
  54.6 1.8 %collective-permute-done.9.refs_2_ = bf16[2,2,256,128]{3,2,1,0:T(8,128)(2,1)S(1)} collective-permute-done((bf16[2,2,256,128]{3,2,1,0:T(8,128)(2,1)S(1)}, bf16[2,2,256,128]{3,2,1,0:T(8,128)(2,1)S(1)}, u32[]{:S(2)}, u32[]{:S(2)}) %collective-permute-start.9) | collective-permute-done | bytes 262176 | tf_op jit(solution)/shard_map/ppermute | solution.py:21
  56.4 0.2 shard_map.90.refs_0_
  56.6 1.1 %shard_map.91 = (bf16[256,4,128]{2,1,0:T(4,128)(2,1)}, bf16[256,4,128]{2,1,0:T(4,128)(2,1)}) custom-call(f32[4,2,256,128]{3,2,1,0:T(8,128)S(1)} %shard_map.90.refs_0_, bf16[2,2,256,128]{3,2,1,0:T(8,128)(2,1)S(1)} %collective-permute-done.12.refs_1_, bf16[2,2,256,128]{3,2,1,0:T(8,128)(2,1)S(1)} %get-tuple-element.57.refs_2_, ...), custom_call_target="tpu_custom_call" | custom-call | bytes 3145728 | tf_op jit(solution)/shard_map/pallas_call | solution.py:114
  (12 shorter events, 0.0 us)
Async XLA Ops:
  2.0 7.3 %collective-permute-start = (bf16[4,2,256,128]{3,2,1,0:T(8,128)(2,1)S(1)}, bf16[4,2,256,128]{3,2,1,0:T(8,128)(2,1)S(1)}, u32[]{:S(2)}, u32[]{:S(2)}) collective-permute-start(bf16[4,2,256,128]{3,2,1,0:T(8,128)(2,1)S(1)} %get-tuple-element.34.refs_0_), channel_id=1, source_target_pairs={{0,1},{1,0},{2,3},{3,2},{4,5},{5,4},{6,7},{7,6},{8,9},{9,8},{10,11... | collective-permute-start | bytes 1572872 | tf_op jit(solution)/shard_map/ppermute | solution.py:21
  2.5 16.5 %collective-permute-start.6 = (bf16[2,2,256,128]{3,2,1,0:T(8,128)(2,1)S(1)}, bf16[2,2,256,128]{3,2,1,0:T(8,128)(2,1)S(1)}, u32[]{:S(2)}, u32[]{:S(2)}) collective-permute-start(bf16[2,2,256,128]{3,2,1,0:T(8,128)(2,1)S(1)} %get-tuple-element.39), channel_id=1, source_target_pairs={{0,8},{1,9},{2,10},{3,11},{4,12},{5,13},{6,14},{7,15},{8,0},{9,1},... | collective-permute-start | bytes 786440 | tf_op jit(solution)/shard_map/ppermute | solution.py:21
  6.2 14.7 %collective-permute-start.5 = (bf16[2,2,256,128]{3,2,1,0:T(8,128)(2,1)S(1)}, bf16[2,2,256,128]{3,2,1,0:T(8,128)(2,1)S(1)}, u32[]{:S(2)}, u32[]{:S(2)}) collective-permute-start(bf16[2,2,256,128]{3,2,1,0:T(8,128)(2,1)S(1)} %get-tuple-element.39), channel_id=1, source_target_pairs={{0,4},{1,5},{2,6},{3,7},{4,0},{5,1},{6,2},{7,3},{8,12},{9,13},{10,... | collective-permute-start | bytes 786440 | tf_op jit(solution)/shard_map/ppermute | solution.py:21
  7.8 13.1 %collective-permute-start.4 = (bf16[2,2,256,128]{3,2,1,0:T(8,128)(2,1)S(1)}, bf16[2,2,256,128]{3,2,1,0:T(8,128)(2,1)S(1)}, u32[]{:S(2)}, u32[]{:S(2)}) collective-permute-start(bf16[2,2,256,128]{3,2,1,0:T(8,128)(2,1)S(1)} %get-tuple-element.39), channel_id=1, source_target_pairs={{0,2},{1,3},{2,0},{3,1},{4,6},{5,7},{6,4},{7,5},{8,10},{9,11},{10,... | collective-permute-start | bytes 786440 | tf_op jit(solution)/shard_map/ppermute | solution.py:21
  15.0 18.7 %collective-permute-start.3 = (bf16[2,2,256,128]{3,2,1,0:T(8,128)(2,1)S(1)}, bf16[2,2,256,128]{3,2,1,0:T(8,128)(2,1)S(1)}, u32[]{:S(2)}, u32[]{:S(2)}) collective-permute-start(bf16[2,2,256,128]{3,2,1,0:T(8,128)(2,1)S(1)} %get-tuple-element.38), channel_id=1, source_target_pairs={{0,8},{1,9},{2,10},{3,11},{4,12},{5,13},{6,14},{7,15},{8,0},{9,1},... | collective-permute-start | bytes 786440 | tf_op jit(solution)/shard_map/ppermute | solution.py:21
  15.4 18.3 %collective-permute-start.2 = (bf16[2,2,256,128]{3,2,1,0:T(8,128)(2,1)S(1)}, bf16[2,2,256,128]{3,2,1,0:T(8,128)(2,1)S(1)}, u32[]{:S(2)}, u32[]{:S(2)}) collective-permute-start(bf16[2,2,256,128]{3,2,1,0:T(8,128)(2,1)S(1)} %get-tuple-element.38), channel_id=1, source_target_pairs={{0,4},{1,5},{2,6},{3,7},{4,0},{5,1},{6,2},{7,3},{8,12},{9,13},{10,... | collective-permute-start | bytes 786440 | tf_op jit(solution)/shard_map/ppermute | solution.py:21
  19.1 14.7 %collective-permute-start.1 = (bf16[2,2,256,128]{3,2,1,0:T(8,128)(2,1)S(1)}, bf16[2,2,256,128]{3,2,1,0:T(8,128)(2,1)S(1)}, u32[]{:S(2)}, u32[]{:S(2)}) collective-permute-start(bf16[2,2,256,128]{3,2,1,0:T(8,128)(2,1)S(1)} %get-tuple-element.38), channel_id=1, source_target_pairs={{0,2},{1,3},{2,0},{3,1},{4,6},{5,7},{6,4},{7,5},{8,10},{9,11},{10,... | collective-permute-start | bytes 786440 | tf_op jit(solution)/shard_map/ppermute | solution.py:21
  29.7 14.9 %collective-permute-start.7 = (bf16[2,2,256,128]{3,2,1,0:T(8,128)(2,1)S(1)}, bf16[2,2,256,128]{3,2,1,0:T(8,128)(2,1)S(1)}, u32[]{:S(2)}, u32[]{:S(2)}) collective-permute-start(bf16[2,2,256,128]{3,2,1,0:T(8,128)(2,1)S(1)} %get-tuple-element.48), channel_id=1, source_target_pairs={{0,8},{1,9},{2,10},{3,11},{4,12},{5,13},{6,14},{7,15},{8,0},{9,1},... | collective-permute-start | bytes 786440 | tf_op jit(solution)/shard_map/ppermute | solution.py:21
  29.7 14.9 %collective-permute-start.8 = (bf16[2,2,256,128]{3,2,1,0:T(8,128)(2,1)S(1)}, bf16[2,2,256,128]{3,2,1,0:T(8,128)(2,1)S(1)}, u32[]{:S(2)}, u32[]{:S(2)}) collective-permute-start(bf16[2,2,256,128]{3,2,1,0:T(8,128)(2,1)S(1)} %get-tuple-element.49), channel_id=1, source_target_pairs={{0,4},{1,5},{2,6},{3,7},{4,0},{5,1},{6,2},{7,3},{8,12},{9,13},{10,... | collective-permute-start | bytes 786440 | tf_op jit(solution)/shard_map/ppermute | solution.py:21
  42.6 13.8 %collective-permute-start.11 = (bf16[4,2,256,128]{3,2,1,0:T(8,128)(2,1)S(1)}, bf16[4,2,256,128]{3,2,1,0:T(8,128)(2,1)S(1)}, u32[]{:S(2)}, u32[]{:S(2)}) collective-permute-start(bf16[4,2,256,128]{3,2,1,0:T(8,128)(2,1)S(1)} %get-tuple-element.55), channel_id=1, source_target_pairs={{0,2},{1,3},{2,0},{3,1},{4,6},{5,7},{6,4},{7,5},{8,10},{9,11},{10,... | collective-permute-start | bytes 1572872 | tf_op jit(solution)/shard_map/ppermute | solution.py:21
  43.1 13.3 %collective-permute-start.9 = (bf16[2,2,256,128]{3,2,1,0:T(8,128)(2,1)S(1)}, bf16[2,2,256,128]{3,2,1,0:T(8,128)(2,1)S(1)}, u32[]{:S(2)}, u32[]{:S(2)}) collective-permute-start(bf16[2,2,256,128]{3,2,1,0:T(8,128)(2,1)S(1)} %get-tuple-element.53), channel_id=1, source_target_pairs={{0,8},{1,9},{2,10},{3,11},{4,12},{5,13},{6,14},{7,15},{8,0},{9,1},... | collective-permute-start | bytes 786440 | tf_op jit(solution)/shard_map/ppermute | solution.py:21
  43.1 13.3 %collective-permute-start.10 = (bf16[2,2,256,128]{3,2,1,0:T(8,128)(2,1)S(1)}, bf16[2,2,256,128]{3,2,1,0:T(8,128)(2,1)S(1)}, u32[]{:S(2)}, u32[]{:S(2)}) collective-permute-start(bf16[2,2,256,128]{3,2,1,0:T(8,128)(2,1)S(1)} %get-tuple-element.54), channel_id=1, source_target_pairs={{0,4},{1,5},{2,6},{3,7},{4,0},{5,1},{6,2},{7,3},{8,12},{9,13},{10,... | collective-permute-start | bytes 786440 | tf_op jit(solution)/shard_map/ppermute | solution.py:21
  54.1 2.5 %collective-permute-start.13 = (bf16[2,2,256,128]{3,2,1,0:T(8,128)(2,1)S(1)}, bf16[2,2,256,128]{3,2,1,0:T(8,128)(2,1)S(1)}, u32[]{:S(2)}, u32[]{:S(2)}) collective-permute-start(bf16[2,2,256,128]{3,2,1,0:T(8,128)(2,1)S(1)} %get-tuple-element.58), channel_id=1, source_target_pairs={{0,1},{1,0},{2,3},{3,2},{4,5},{5,4},{6,7},{7,6},{8,9},{9,8},{10,11... | collective-permute-start | bytes 786440 | tf_op jit(solution)/shard_map/ppermute | solution.py:21
  54.1 2.5 %collective-permute-start.12 = (bf16[2,2,256,128]{3,2,1,0:T(8,128)(2,1)S(1)}, bf16[2,2,256,128]{3,2,1,0:T(8,128)(2,1)S(1)}, u32[]{:S(2)}, u32[]{:S(2)}) collective-permute-start(bf16[2,2,256,128]{3,2,1,0:T(8,128)(2,1)S(1)} %get-tuple-element.56), channel_id=1, source_target_pairs={{0,1},{1,0},{2,3},{3,2},{4,5},{5,4},{6,7},{7,6},{8,9},{9,8},{10,11... | collective-permute-start | bytes 786440 | tf_op jit(solution)/shard_map/ppermute | solution.py:21

commit v5 on v4

--- a/solution.py
+++ b/solution.py
@@ -10,6 +10,7 @@
 LOG2E = 1.4426950408889634
 MASKED = -1e30
 VMEM_LIMIT = 24 * 2**20
+PAD = 32
 LOCAL = (0, 1)
 REMOTE = (2, 3, 4)
 HALVES = ((0, 2), (2, 4))
@@ -43,42 +44,54 @@
     return pltpu.with_memory_space_constraint(array, pltpu.HBM)
 
 
-def pack_kernel(groups, bits, me_ref, mask_ref, k_ref, v_ref, bias_ref, *refs):
+def pack_kernel(groups, k_ref, v_ref, *refs):
     outs, wide_ref = refs[:-1], refs[-1]
     tokens, heads, size = k_ref.shape
     for i, ref in enumerate((k_ref, v_ref)):
-        wide_ref[i] = ref[...].astype(jnp.float32).reshape(tokens * heads, size)
+        wide_ref[i, : tokens * heads] = ref[...].astype(jnp.float32).reshape(tokens * heads, size)
         for h in range(heads):
             rows = wide_ref[i, pl.ds(h, tokens, stride=heads), :].astype(jnp.bfloat16)
             for (low, high), out in zip(groups, outs):
                 if low <= h < high:
                     out[h - low, i] = rows
+
+
+def pack(keys, values, groups):
+    tokens, heads, size = keys.shape
+    return pl.pallas_call(
+        functools.partial(pack_kernel, groups),
+        in_specs=[VMEM] * 2,
+        out_specs=[VMEM] * len(groups),
+        out_shape=[jax.ShapeDtypeStruct((high - low, 2, tokens, size), keys.dtype) for low, high in groups],
+        scratch_shapes=[pltpu.VMEM((2, tokens * heads + PAD, size), jnp.float32)],
+        compiler_params=pltpu.CompilerParams(vmem_limit_bytes=VMEM_LIMIT),
+        cost_estimate=pl.CostEstimate(flops=0, bytes_accessed=6 * keys.size * 2, transcendentals=0),
+    )(in_hbm(keys), in_hbm(values))
+
+
+def mask_kernel(bits, me_ref, mask_ref, bias_ref):
     me = me_ref[0]
     blocks, columns = mask_ref.shape
+    width = bias_ref.shape[2] // blocks
     mask = mask_ref[...]
     column = lax.broadcasted_iota(jnp.int32, (blocks, columns), 1)
     for s, device in enumerate([me] + [jnp.bitwise_xor(me, 1 << bit) for bit in bits]):
         for b in range(blocks):
             ones = jnp.sum(jnp.where(column == device * blocks + b, mask, 0), axis=1, keepdims=True)
-            width = tokens // blocks
             bias_ref[s, :, b * width : (b + 1) * width] = jnp.broadcast_to(
                 jnp.where(ones > 0, 0.0, MASKED), (blocks, width)
             )
 
 
-def pack(me, block_mask, keys, values, groups, bits):
-    tokens, heads, size = keys.shape
-    bias = jax.ShapeDtypeStruct((len(bits) + 1, block_mask.shape[0], tokens), jnp.float32)
+def mask_rows(me, block_mask, tokens, bits):
     return pl.pallas_call(
-        functools.partial(pack_kernel, groups, bits),
-        in_specs=[SMEM] + [VMEM] * 3,
-        out_specs=[VMEM] * (len(groups) + 1),
-        out_shape=[bias]
-        + [jax.ShapeDtypeStruct((high - low, 2, tokens, size), keys.dtype) for low, high in groups],
-        scratch_shapes=[pltpu.VMEM((2, tokens * heads, size), jnp.float32)],
+        functools.partial(mask_kernel, bits),
+        in_specs=[SMEM, VMEM],
+        out_specs=VMEM,
+        out_shape=jax.ShapeDtypeStruct((len(bits) + 1, block_mask.shape[0], tokens), jnp.float32),
         compiler_params=pltpu.CompilerParams(vmem_limit_bytes=VMEM_LIMIT),
-        cost_estimate=pl.CostEstimate(flops=0, bytes_accessed=6 * keys.size * 2, transcendentals=0),
-    )(me, in_hbm(block_mask), in_hbm(keys), in_hbm(values))
+        cost_estimate=pl.CostEstimate(flops=0, bytes_accessed=2**14, transcendentals=0),
+    )(me, in_hbm(block_mask))
 
 
 def gather_kernel(groups, *refs):
@@ -106,7 +119,7 @@
         for h in range(heads):
             parts = [t[h - g[0], i].astype(jnp.float32) for g, t in zip(groups, terms) if g[0] <= h < g[1]]
             wide_ref[i, pl.ds(h, tokens, stride=heads), :] = functools.reduce(jnp.add, parts)
-        ref[...] = wide_ref[i].astype(ref.dtype).reshape(tokens, heads, size)
+        ref[...] = wide_ref[i, : tokens * heads].astype(ref.dtype).reshape(tokens, heads, size)
 
 
 def sum_terms(groups, terms, tokens, heads, size):
@@ -116,7 +129,7 @@
         in_specs=[VMEM] * len(groups),
         out_specs=[VMEM] * 2,
         out_shape=[out, out],
-        scratch_shapes=[pltpu.VMEM((2, tokens * heads, size), jnp.float32)],
+        scratch_shapes=[pltpu.VMEM((2, tokens * heads + PAD, size), jnp.float32)],
         compiler_params=pltpu.CompilerParams(vmem_limit_bytes=VMEM_LIMIT),
         cost_estimate=pl.CostEstimate(flops=0, bytes_accessed=12 * tokens * heads * size * 2, transcendentals=0),
     )(*terms)
@@ -429,8 +442,8 @@
     dout = jnp.transpose(output_gradient, (1, 0, 2))
     whole = (0, kv_heads)
     groups = (whole,) + HALVES
-    bias, *arrays = pack(me, block_mask, keys, values, groups, bits)
-    packed = dict(zip(groups, arrays))
+    packed = dict(zip(groups, pack(keys, values, groups)))
+    bias = mask_rows(me, block_mask, tokens, bits)
     far = {(HALVES[0], bit): from_partner(packed[HALVES[0]], "seq", bit) for bit in reversed(bits[2:])}
     core = from_partner(packed[whole], "seq", bits[0])
     near = {HALVES[0]: from_partner(packed[HALVES[0]], "seq", bits[1])}

time: 58 us -> 57.7 us (level)
  waiting for transfers between devices: 5.02 us -> 3.7 us
  Pallas kernels: 35.5 us -> 36.2 us
    ppermute x14, waiting for transfers between devices: 5.02 us -> 3.7 us  [from_partner(): return lax.ppermute(value, axis, pairs)]
    pallas_call x1 -> x2, Pallas kernels: 1.37 us -> 2.04 us  [the longest x1 1.26 us: pack(): pl.pallas_call(functools.partial(pack_kernel, groups), in_specs=[VMEM] *...]
  transfers between devices with their start and end apart: 14 -> 14, of which waited for: 2 -> 2; matrix products, arithmetic and copies ran while one was open for 0% -> 0% of each run, Pallas kernels for 57% -> 59%
where the time goes in v5:
time: 57.7 us; the launch traced here: 57.5 us
  Pallas kernels  36.2 us (63%)
  starting transfers between devices  16.9 us (29%)
  waiting for transfers between devices  3.7 us (6%)
  between operations  0.7 us (1%)
    pallas_call x2, Pallas kernels, remote(): pl.pallas_call(functools.partial(remote_kernel, scale, len(chain)), grid=...  17.6 us
    ppermute x14, starting transfers between devices, from_partner(): return lax.ppermute(value, axis, pairs)  16.9 us
    pallas_call x2, Pallas kernels, rest(): pl.pallas_call(functools.partial(rest_kernel, scale, len(chain)), grid=(l...  9.45 us
    pallas_call x1, Pallas kernels, local(): pl.pallas_call(functools.partial(local_kernel, scale), grid=(heads_all,),...  5.76 us
    ppermute x14, waiting for transfers between devices, from_partner(): return lax.ppermute(value, axis, pairs)  3.7 us
    pallas_call x1, Pallas kernels, pack(): pl.pallas_call(functools.partial(pack_kernel, groups), in_specs=[VMEM] *...  1.26 us
  transfers between devices with their start and end apart: 14, of which 2 were waited for; matrix products, arithmetic and copies ran while one was open for 0% of the time, Pallas kernels for 59%

profile of v5, /device:TPU:0, one launch (start us, length us, event | category | flops | bytes accessed | tf_op | source)
XLA Modules:
  0.0 57.5 jit_solution(16430565906061748405)
XLA Ops:
  0.6 1.3 %shard_map.85 = (bf16[4,2,256,128]{3,2,1,0:T(8,128)(2,1)S(1)}, bf16[2,2,256,128]{3,2,1,0:T(8,128)(2,1)S(1)}, bf16[2,2,256,128]{3,2,1,0:T(8,128)(2,1)S(1)}) custom-call(bf16[256,4,128]{2,1,0:T(4,128)(2,1)} %k_ref.1, bf16[256,4,128]{2,1,0:T(4,128)(2,1)} %v_ref.1), custom_call_target="tpu_custom_call" | custom-call | bytes 1572864 | tf_op jit(solution)/shard_map/pallas_call | solution.py:61
  1.9 0.5 collective-permute-start
  2.4 3.7 %collective-permute-start.6 = (bf16[2,2,256,128]{3,2,1,0:T(8,128)(2,1)S(1)}, bf16[2,2,256,128]{3,2,1,0:T(8,128)(2,1)S(1)}, u32[]{:S(2)}, u32[]{:S(2)}) collective-permute-start(bf16[2,2,256,128]{3,2,1,0:T(8,128)(2,1)S(1)} %get-tuple-element.37), channel_id=1, source_target_pairs={{0,8},{1,9},{2,10},{3,11},{4,12},{5,13},{6,14},{7,15},{8,0},{9,1},... | collective-permute-start | bytes 786440 | tf_op jit(solution)/shard_map/ppermute | solution.py:22
  6.1 1.6 %collective-permute-start.5 = (bf16[2,2,256,128]{3,2,1,0:T(8,128)(2,1)S(1)}, bf16[2,2,256,128]{3,2,1,0:T(8,128)(2,1)S(1)}, u32[]{:S(2)}, u32[]{:S(2)}) collective-permute-start(bf16[2,2,256,128]{3,2,1,0:T(8,128)(2,1)S(1)} %get-tuple-element.37), channel_id=1, source_target_pairs={{0,4},{1,5},{2,6},{3,7},{4,0},{5,1},{6,2},{7,3},{8,12},{9,13},{10,... | collective-permute-start | bytes 786440 | tf_op jit(solution)/shard_map/ppermute | solution.py:22
  7.7 1.5 %collective-permute-start.4 = (bf16[2,2,256,128]{3,2,1,0:T(8,128)(2,1)S(1)}, bf16[2,2,256,128]{3,2,1,0:T(8,128)(2,1)S(1)}, u32[]{:S(2)}, u32[]{:S(2)}) collective-permute-start(bf16[2,2,256,128]{3,2,1,0:T(8,128)(2,1)S(1)} %get-tuple-element.37), channel_id=1, source_target_pairs={{0,2},{1,3},{2,0},{3,1},{4,6},{5,7},{6,4},{7,5},{8,10},{9,11},{10,... | collective-permute-start | bytes 786440 | tf_op jit(solution)/shard_map/ppermute | solution.py:22
  9.2 0.8 %shard_map.84.bias_ref = f32[5,2,256]{2,1,0:T(2,128)S(1)} custom-call(s32[1]{0:T(128)} %bitcast.me_ref, s32[2,32]{1,0:T(2,128)} %mask_ref.1), custom_call_target="tpu_custom_call" | custom-call | bytes 16384 | tf_op jit(solution)/shard_map/pallas_call | solution.py:87
  10.0 5.8 %shard_map.86 = (bf16[20,2,256,256]{3,2,1,0:T(8,128)(2,1)S(1)}, f32[20,256,128]{2,1,0:T(8,128)S(1)}, f32[20,2,256,128]{3,2,1,0:T(8,128)S(1)}) custom-call(f32[5,2,256]{2,1,0:T(2,128)S(1)} %shard_map.84.bias_ref, bf16[20,256,128]{2,1,0:T(8,128)(2,1)} %bitcast.5, bf16[4,2,256,128]{3,2,1,0:T(8,128)(2,1)S(1)} %get-tuple-element.32.refs_0_, ...), custom_call_target="tpu_custom_call" | custom-call | flops 1342177280 | bytes 5242880 | tf_op jit(solution)/shard_map/pallas_call | solution.py:385
  15.7 0.4 collective-permute-start.3
  16.1 0.4 collective-permute-start.2
  16.6 2.1 %collective-permute-done.6.refs_2_ = bf16[2,2,256,128]{3,2,1,0:T(8,128)(2,1)S(1)} collective-permute-done((bf16[2,2,256,128]{3,2,1,0:T(8,128)(2,1)S(1)}, bf16[2,2,256,128]{3,2,1,0:T(8,128)(2,1)S(1)}, u32[]{:S(2)}, u32[]{:S(2)}) %collective-permute-start.6) | collective-permute-done | bytes 262176 | tf_op jit(solution)/shard_map/ppermute | solution.py:22
  18.7 2.0 %collective-permute-start.1 = (bf16[2,2,256,128]{3,2,1,0:T(8,128)(2,1)S(1)}, bf16[2,2,256,128]{3,2,1,0:T(8,128)(2,1)S(1)}, u32[]{:S(2)}, u32[]{:S(2)}) collective-permute-start(bf16[2,2,256,128]{3,2,1,0:T(8,128)(2,1)S(1)} %get-tuple-element.36), channel_id=1, source_target_pairs={{0,2},{1,3},{2,0},{3,1},{4,6},{5,7},{6,4},{7,5},{8,10},{9,11},{10,... | collective-permute-start | bytes 786440 | tf_op jit(solution)/shard_map/ppermute | solution.py:22
  20.7 8.8 %shard_map.87 = (bf16[20,256,128]{2,1,0:T(8,128)(2,1)}, f32[20,256,128]{2,1,0:T(8,128)S(1)}, f32[20,2,256,128]{3,2,1,0:T(8,128)S(1)}, bf16[4,2,256,128]{3,2,1,0:...) custom-call(f32[5,2,256]{2,1,0:T(2,128)S(1)} %shard_map.84.bias_ref, ...), custom_call_target="tpu_custom_call" | custom-call | flops 3019898880 | bytes 2621440 | tf_op jit(solution)/shard_map/pallas_call | solution.py:400
  29.5 0.0 collective-permute-start.7
  29.5 4.0 %collective-permute-start.8 = (bf16[2,2,256,128]{3,2,1,0:T(8,128)(2,1)S(1)}, bf16[2,2,256,128]{3,2,1,0:T(8,128)(2,1)S(1)}, u32[]{:S(2)}, u32[]{:S(2)}) collective-permute-start(bf16[2,2,256,128]{3,2,1,0:T(8,128)(2,1)S(1)} %get-tuple-element.47), channel_id=1, source_target_pairs={{0,4},{1,5},{2,6},{3,7},{4,0},{5,1},{6,2},{7,3},{8,12},{9,13},{10,... | collective-permute-start | bytes 786440 | tf_op jit(solution)/shard_map/ppermute | solution.py:22
  33.6 8.9 %shard_map.88 = (bf16[20,256,128]{2,1,0:T(8,128)(2,1)}, f32[20,256,128]{2,1,0:T(8,128)S(1)}, f32[20,2,256,128]{3,2,1,0:T(8,128)S(1)}, bf16[4,2,256,128]{3,2,1,0:...) custom-call(f32[5,2,256]{2,1,0:T(2,128)S(1)} %shard_map.84.bias_ref,, ...), custom_call_target="tpu_custom_call", output_to_operand_aliasing={{0}: (8, {}), {1}: (9, {}), {2}: (10, {}), {3}: (11, {})} | custom-call | flops 3019898880 | bytes 2621440 | tf_op jit(solution)/shard_map/pallas_call | solution.py:400
  42.4 0.5 collective-permute-start.11
  42.9 0.0 collective-permute-start.9
  42.9 1.7 %collective-permute-start.10 = (bf16[2,2,256,128]{3,2,1,0:T(8,128)(2,1)S(1)}, bf16[2,2,256,128]{3,2,1,0:T(8,128)(2,1)S(1)}, u32[]{:S(2)}, u32[]{:S(2)}) collective-permute-start(bf16[2,2,256,128]{3,2,1,0:T(8,128)(2,1)S(1)} %get-tuple-element.52), channel_id=1, source_target_pairs={{0,4},{1,5},{2,6},{3,7},{4,0},{5,1},{6,2},{7,3},{8,12},{9,13},{10,... | collective-permute-start | bytes 786440 | tf_op jit(solution)/shard_map/ppermute | solution.py:22
  44.6 4.7 %shard_map.89 = (bf16[20,256,128]{2,1,0:T(8,128)(2,1)}, bf16[2,2,256,128]{3,2,1,0:T(8,128)(2,1)S(1)}, bf16[2,2,256,128]{3,2,1,0:T(8,128)(2,1)S(1)}) custom-call(bf16[20,256,128]{2,1,0:T(8,128)(2,1)} %bitcast.8, bf16[20,256,128]{2,1,0:T(8,128)(2,1)} %bitcast.12, bf16[20,2,256,256]{3,2,1,0:T(8,128)(2,1)S(1)} %get-tuple-element.43.e_ref, ...), custom_call_target="tpu_custom_call" | custom-call | flops 1342177280 | bytes 2621440 | tf_op jit(solution)/shard_map/pallas_call | solution.py:416
  49.4 4.7 %shard_map.90 = (bf16[20,256,128]{2,1,0:T(8,128)(2,1)}, bf16[2,2,256,128]{3,2,1,0:T(8,128)(2,1)S(1)}, bf16[2,2,256,128]{3,2,1,0:T(8,128)(2,1)S(1)}) custom-call(bf16[20,256,128]{2,1,0:T(8,128)(2,1)} %bitcast.9, bf16[20,256,128]{2,1,0:T(8,128)(2,1)} %bitcast.13, ...), custom_call_target="tpu_custom_call", output_to_operand_aliasing={{0}: (7, {})} | custom-call | flops 1342177280 | bytes 2621440 | tf_op jit(solution)/shard_map/pallas_call | solution.py:416
  54.1 0.5 collective-permute-start.12
  54.6 1.6 %collective-permute-done.9.refs_2_ = bf16[2,2,256,128]{3,2,1,0:T(8,128)(2,1)S(1)} collective-permute-done((bf16[2,2,256,128]{3,2,1,0:T(8,128)(2,1)S(1)}, bf16[2,2,256,128]{3,2,1,0:T(8,128)(2,1)S(1)}, u32[]{:S(2)}, u32[]{:S(2)}) %collective-permute-start.9) | collective-permute-done | bytes 262176 | tf_op jit(solution)/shard_map/ppermute | solution.py:22
  56.2 0.2 shard_map.91.refs_0_
  56.4 1.1 %shard_map.92 = (bf16[256,4,128]{2,1,0:T(4,128)(2,1)}, bf16[256,4,128]{2,1,0:T(4,128)(2,1)}) custom-call(f32[4,2,256,128]{3,2,1,0:T(8,128)S(1)} %shard_map.91.refs_0_, bf16[2,2,256,128]{3,2,1,0:T(8,128)(2,1)S(1)} %collective-permute-done.12.refs_1_, bf16[2,2,256,128]{3,2,1,0:T(8,128)(2,1)S(1)} %get-tuple-element.55.refs_2_, ...), custom_call_target="tpu_custom_call" | custom-call | bytes 3145728 | tf_op jit(solution)/shard_map/pallas_call | solution.py:127
  (13 shorter events, 0.0 us)
Async XLA Ops:
  1.9 8.1 %collective-permute-start = (bf16[4,2,256,128]{3,2,1,0:T(8,128)(2,1)S(1)}, bf16[4,2,256,128]{3,2,1,0:T(8,128)(2,1)S(1)}, u32[]{:S(2)}, u32[]{:S(2)}) collective-permute-start(bf16[4,2,256,128]{3,2,1,0:T(8,128)(2,1)S(1)} %get-tuple-element.32.refs_0_), channel_id=1, source_target_pairs={{0,1},{1,0},{2,3},{3,2},{4,5},{5,4},{6,7},{7,6},{8,9},{9,8},{10,11... | collective-permute-start | bytes 1572872 | tf_op jit(solution)/shard_map/ppermute | solution.py:22
  2.4 16.3 %collective-permute-start.6 = (bf16[2,2,256,128]{3,2,1,0:T(8,128)(2,1)S(1)}, bf16[2,2,256,128]{3,2,1,0:T(8,128)(2,1)S(1)}, u32[]{:S(2)}, u32[]{:S(2)}) collective-permute-start(bf16[2,2,256,128]{3,2,1,0:T(8,128)(2,1)S(1)} %get-tuple-element.37), channel_id=1, source_target_pairs={{0,8},{1,9},{2,10},{3,11},{4,12},{5,13},{6,14},{7,15},{8,0},{9,1},... | collective-permute-start | bytes 786440 | tf_op jit(solution)/shard_map/ppermute | solution.py:22
  6.1 14.7 %collective-permute-start.5 = (bf16[2,2,256,128]{3,2,1,0:T(8,128)(2,1)S(1)}, bf16[2,2,256,128]{3,2,1,0:T(8,128)(2,1)S(1)}, u32[]{:S(2)}, u32[]{:S(2)}) collective-permute-start(bf16[2,2,256,128]{3,2,1,0:T(8,128)(2,1)S(1)} %get-tuple-element.37), channel_id=1, source_target_pairs={{0,4},{1,5},{2,6},{3,7},{4,0},{5,1},{6,2},{7,3},{8,12},{9,13},{10,... | collective-permute-start | bytes 786440 | tf_op jit(solution)/shard_map/ppermute | solution.py:22
  7.7 13.1 %collective-permute-start.4 = (bf16[2,2,256,128]{3,2,1,0:T(8,128)(2,1)S(1)}, bf16[2,2,256,128]{3,2,1,0:T(8,128)(2,1)S(1)}, u32[]{:S(2)}, u32[]{:S(2)}) collective-permute-start(bf16[2,2,256,128]{3,2,1,0:T(8,128)(2,1)S(1)} %get-tuple-element.37), channel_id=1, source_target_pairs={{0,2},{1,3},{2,0},{3,1},{4,6},{5,7},{6,4},{7,5},{8,10},{9,11},{10,... | collective-permute-start | bytes 786440 | tf_op jit(solution)/shard_map/ppermute | solution.py:22
  15.7 17.8 %collective-permute-start.3 = (bf16[2,2,256,128]{3,2,1,0:T(8,128)(2,1)S(1)}, bf16[2,2,256,128]{3,2,1,0:T(8,128)(2,1)S(1)}, u32[]{:S(2)}, u32[]{:S(2)}) collective-permute-start(bf16[2,2,256,128]{3,2,1,0:T(8,128)(2,1)S(1)} %get-tuple-element.36), channel_id=1, source_target_pairs={{0,8},{1,9},{2,10},{3,11},{4,12},{5,13},{6,14},{7,15},{8,0},{9,1},... | collective-permute-start | bytes 786440 | tf_op jit(solution)/shard_map/ppermute | solution.py:22
  16.1 17.4 %collective-permute-start.2 = (bf16[2,2,256,128]{3,2,1,0:T(8,128)(2,1)S(1)}, bf16[2,2,256,128]{3,2,1,0:T(8,128)(2,1)S(1)}, u32[]{:S(2)}, u32[]{:S(2)}) collective-permute-start(bf16[2,2,256,128]{3,2,1,0:T(8,128)(2,1)S(1)} %get-tuple-element.36), channel_id=1, source_target_pairs={{0,4},{1,5},{2,6},{3,7},{4,0},{5,1},{6,2},{7,3},{8,12},{9,13},{10,... | collective-permute-start | bytes 786440 | tf_op jit(solution)/shard_map/ppermute | solution.py:22
  18.7 14.9 %collective-permute-start.1 = (bf16[2,2,256,128]{3,2,1,0:T(8,128)(2,1)S(1)}, bf16[2,2,256,128]{3,2,1,0:T(8,128)(2,1)S(1)}, u32[]{:S(2)}, u32[]{:S(2)}) collective-permute-start(bf16[2,2,256,128]{3,2,1,0:T(8,128)(2,1)S(1)} %get-tuple-element.36), channel_id=1, source_target_pairs={{0,2},{1,3},{2,0},{3,1},{4,6},{5,7},{6,4},{7,5},{8,10},{9,11},{10,... | collective-permute-start | bytes 786440 | tf_op jit(solution)/shard_map/ppermute | solution.py:22
  29.5 15.1 %collective-permute-start.7 = (bf16[2,2,256,128]{3,2,1,0:T(8,128)(2,1)S(1)}, bf16[2,2,256,128]{3,2,1,0:T(8,128)(2,1)S(1)}, u32[]{:S(2)}, u32[]{:S(2)}) collective-permute-start(bf16[2,2,256,128]{3,2,1,0:T(8,128)(2,1)S(1)} %get-tuple-element.46), channel_id=1, source_target_pairs={{0,8},{1,9},{2,10},{3,11},{4,12},{5,13},{6,14},{7,15},{8,0},{9,1},... | collective-permute-start | bytes 786440 | tf_op jit(solution)/shard_map/ppermute | solution.py:22
  29.5 15.1 %collective-permute-start.8 = (bf16[2,2,256,128]{3,2,1,0:T(8,128)(2,1)S(1)}, bf16[2,2,256,128]{3,2,1,0:T(8,128)(2,1)S(1)}, u32[]{:S(2)}, u32[]{:S(2)}) collective-permute-start(bf16[2,2,256,128]{3,2,1,0:T(8,128)(2,1)S(1)} %get-tuple-element.47), channel_id=1, source_target_pairs={{0,4},{1,5},{2,6},{3,7},{4,0},{5,1},{6,2},{7,3},{8,12},{9,13},{10,... | collective-permute-start | bytes 786440 | tf_op jit(solution)/shard_map/ppermute | solution.py:22
  42.4 13.7 %collective-permute-start.11 = (bf16[4,2,256,128]{3,2,1,0:T(8,128)(2,1)S(1)}, bf16[4,2,256,128]{3,2,1,0:T(8,128)(2,1)S(1)}, u32[]{:S(2)}, u32[]{:S(2)}) collective-permute-start(bf16[4,2,256,128]{3,2,1,0:T(8,128)(2,1)S(1)} %get-tuple-element.53), channel_id=1, source_target_pairs={{0,2},{1,3},{2,0},{3,1},{4,6},{5,7},{6,4},{7,5},{8,10},{9,11},{10,... | collective-permute-start | bytes 1572872 | tf_op jit(solution)/shard_map/ppermute | solution.py:22
  42.9 13.2 %collective-permute-start.9 = (bf16[2,2,256,128]{3,2,1,0:T(8,128)(2,1)S(1)}, bf16[2,2,256,128]{3,2,1,0:T(8,128)(2,1)S(1)}, u32[]{:S(2)}, u32[]{:S(2)}) collective-permute-start(bf16[2,2,256,128]{3,2,1,0:T(8,128)(2,1)S(1)} %get-tuple-element.51), channel_id=1, source_target_pairs={{0,8},{1,9},{2,10},{3,11},{4,12},{5,13},{6,14},{7,15},{8,0},{9,1},... | collective-permute-start | bytes 786440 | tf_op jit(solution)/shard_map/ppermute | solution.py:22
  42.9 13.2 %collective-permute-start.10 = (bf16[2,2,256,128]{3,2,1,0:T(8,128)(2,1)S(1)}, bf16[2,2,256,128]{3,2,1,0:T(8,128)(2,1)S(1)}, u32[]{:S(2)}, u32[]{:S(2)}) collective-permute-start(bf16[2,2,256,128]{3,2,1,0:T(8,128)(2,1)S(1)} %get-tuple-element.52), channel_id=1, source_target_pairs={{0,4},{1,5},{2,6},{3,7},{4,0},{5,1},{6,2},{7,3},{8,12},{9,13},{10,... | collective-permute-start | bytes 786440 | tf_op jit(solution)/shard_map/ppermute | solution.py:22
  54.1 2.3 %collective-permute-start.13 = (bf16[2,2,256,128]{3,2,1,0:T(8,128)(2,1)S(1)}, bf16[2,2,256,128]{3,2,1,0:T(8,128)(2,1)S(1)}, u32[]{:S(2)}, u32[]{:S(2)}) collective-permute-start(bf16[2,2,256,128]{3,2,1,0:T(8,128)(2,1)S(1)} %get-tuple-element.56), channel_id=1, source_target_pairs={{0,1},{1,0},{2,3},{3,2},{4,5},{5,4},{6,7},{7,6},{8,9},{9,8},{10,11... | collective-permute-start | bytes 786440 | tf_op jit(solution)/shard_map/ppermute | solution.py:22
  54.1 2.3 %collective-permute-start.12 = (bf16[2,2,256,128]{3,2,1,0:T(8,128)(2,1)S(1)}, bf16[2,2,256,128]{3,2,1,0:T(8,128)(2,1)S(1)}, u32[]{:S(2)}, u32[]{:S(2)}) collective-permute-start(bf16[2,2,256,128]{3,2,1,0:T(8,128)(2,1)S(1)} %get-tuple-element.54), channel_id=1, source_target_pairs={{0,1},{1,0},{2,3},{3,2},{4,5},{5,4},{6,7},{7,6},{8,9},{9,8},{10,11... | collective-permute-start | bytes 786440 | tf_op jit(solution)/shard_map/ppermute | solution.py:22

commit v6 on v5

--- a/solution.py
+++ b/solution.py
@@ -203,11 +203,13 @@
     refs = refs[sources + unused :]
     o_ref, dq_ref, row_ref = refs[:3]
     term_refs = refs[3 : sources + 3]
-    dk_ref, dv_ref, x_ref, e_ref, p_ref, v_ref = refs[sources + 3 :]
+    dk_ref, dv_ref, x_ref, e_ref, p_ref, d_ref, v_ref, k_ref = refs[sources + 3 :]
     scale2 = softmax_scale * LOG2E
     head_group, tokens, size = q_ref.shape
     state = {}
     fill_values(kv_refs, v_ref)
+    for n in range(sources):
+        k_ref[n * tokens : (n + 1) * tokens] = kv_refs[n][0, 0]
 
     def key(n):
         return kv_refs[n][0, 0]
@@ -230,7 +232,7 @@
     def forward(g, n):
         e = jnp.exp2(x_ref[g % 3, n] * scale2 - twice(state["top", g]))
         narrow = e.astype(jnp.bfloat16)
-        e_ref[g % 2, n] = narrow
+        e_ref[n, g * tokens : (g + 1) * tokens] = narrow
         part = product(narrow, v_ref[n])
         state["out", g] = state["out", g] + part if n else part
 
@@ -246,28 +248,18 @@
         row_ref[g, 0] = share * inverse
         row_ref[g, 1] = jnp.broadcast_to(delta, (tokens, size))
         state["scale", g] = inverse * softmax_scale
-        state["q", g] = (q.astype(jnp.float32) * state["scale", g]).astype(jnp.bfloat16).T
-        state["do", g] = (do * inverse).astype(jnp.bfloat16).T
+        dk_ref[:, g * tokens : (g + 1) * tokens] = (q.astype(jnp.float32) * state["scale", g]).astype(jnp.bfloat16).T
+        dv_ref[:, g * tokens : (g + 1) * tokens] = (do * inverse).astype(jnp.bfloat16).T
 
     def backward(g, n):
-        e = e_ref[g % 2, n]
-        dv = product(state["do", g], e)
+        e = e_ref[n, g * tokens : (g + 1) * tokens]
         dscore = (e.astype(jnp.float32) * (p_ref[g % 2, n] - state["delta", g])).astype(jnp.bfloat16)
-        part = product(dscore, key(n))
-        state["dq", g] = state["dq", g] + part if n else part
-        dk = product(state["q", g], dscore)
-        if g == 0:
-            dk_ref[n] = dk
-            dv_ref[n] = dv
-        elif g < head_group - 1:
-            dk_ref[n] += dk
-            dv_ref[n] += dv
-        else:
-            term_refs[n][0, 0] = (dk_ref[n] + dk).T.astype(jnp.bfloat16)
-            term_refs[n][0, 1] = (dv_ref[n] + dv).T.astype(jnp.bfloat16)
+        state["d", g, n] = dscore
+        d_ref[n, g * tokens : (g + 1) * tokens] = dscore
 
     def backward_end(g):
-        dq_ref[g] = state.pop(("dq", g)) * state["scale", g]
+        dscore = jnp.concatenate([state.pop(("d", g, n)) for n in every], axis=1)
+        dq_ref[g] = product(dscore, k_ref[...]) * state["scale", g]
 
     every = range(sources)
     for g in range(2):
@@ -290,6 +282,9 @@
     for n in every:
         backward(head_group - 1, n)
     backward_end(head_group - 1)
+    for n in every:
+        term_refs[n][0, 0] = product(dk_ref[...], d_ref[n]).T.astype(jnp.bfloat16)
+        term_refs[n][0, 1] = product(dv_ref[...], e_ref[n]).T.astype(jnp.bfloat16)
 
 
 def rest_kernel(softmax_scale, unused, q_ref, do_ref, e_ref, part_ref, row_ref, *refs):
@@ -403,8 +398,8 @@
             in_specs=[VMEM] + [rows(first)] * 3 + [columns(first)] + [block(first, begin) for _, begin in others] + [ANY] * len(chain),
             out_specs=whole + [block(0, 0)] * (n - 1),
             out_shape=[narrow, wide, double, term(heads_all)] + [term(last - first)] * (n - 1),
-            scratch_shapes=[pltpu.VMEM((n, size, tokens), jnp.float32)] * 2
-            + [square(3, n), square(2, n, jnp.bfloat16), square(2, n), pltpu.VMEM((n, tokens, 2 * size), jnp.bfloat16)],
+            scratch_shapes=[pltpu.VMEM((size, head_group * tokens), jnp.bfloat16)] * 2
+            + [square(3, n), pltpu.VMEM((n, head_group * tokens, tokens), jnp.bfloat16), square(2, n), pltpu.VMEM((n, head_group * tokens, tokens), jnp.bfloat16), pltpu.VMEM((n, tokens, 2 * size), jnp.bfloat16), pltpu.VMEM((n * tokens, size), jnp.bfloat16)],
             input_output_aliases={5 + n + i: i for i in range(len(chain))},
             compiler_params=params,
             cost_estimate=cost(6, last - first, head_group, tokens, n, size),

time: 57.7 us -> 57.8 us (level)
  no operation moved by 1% of the time
where the time goes in v6:
time: 57.8 us; the launch traced here: 57.5 us
  Pallas kernels  36.1 us (62%)
  starting transfers between devices  17 us (29%)
  waiting for transfers between devices  3.71 us (6%)
  between operations  0.7 us (1%)
    pallas_call x2, Pallas kernels, remote(): pl.pallas_call(functools.partial(remote_kernel, scale, len(chain)), grid=...  17.6 us
    ppermute x14, starting transfers between devices, from_partner(): return lax.ppermute(value, axis, pairs)  17 us
    pallas_call x2, Pallas kernels, rest(): pl.pallas_call(functools.partial(rest_kernel, scale, len(chain)), grid=(l...  9.46 us
    pallas_call x1, Pallas kernels, local(): pl.pallas_call(functools.partial(local_kernel, scale), grid=(heads_all,),...  5.76 us
    ppermute x14, waiting for transfers between devices, from_partner(): return lax.ppermute(value, axis, pairs)  3.71 us
    pallas_call x1, Pallas kernels, pack(): pl.pallas_call(functools.partial(pack_kernel, groups), in_specs=[VMEM] *...  1.26 us
  transfers between devices with their start and end apart: 14, of which 2 were waited for; matrix products, arithmetic and copies ran while one was open for 0% of the time, Pallas kernels for 59%

profile of v6, /device:TPU:0, one launch (start us, length us, event | category | flops | bytes accessed | tf_op | source)
XLA Modules:
  0.0 57.5 jit_solution(13298743699532347553)
XLA Ops:
  0.6 1.3 %shard_map.85 = (bf16[4,2,256,128]{3,2,1,0:T(8,128)(2,1)S(1)}, bf16[2,2,256,128]{3,2,1,0:T(8,128)(2,1)S(1)}, bf16[2,2,256,128]{3,2,1,0:T(8,128)(2,1)S(1)}) custom-call(bf16[256,4,128]{2,1,0:T(4,128)(2,1)} %k_ref.1, bf16[256,4,128]{2,1,0:T(4,128)(2,1)} %v_ref.1), custom_call_target="tpu_custom_call" | custom-call | bytes 1572864 | tf_op jit(solution)/shard_map/pallas_call | solution.py:61
  1.9 0.5 collective-permute-start
  2.4 3.7 %collective-permute-start.6 = (bf16[2,2,256,128]{3,2,1,0:T(8,128)(2,1)S(1)}, bf16[2,2,256,128]{3,2,1,0:T(8,128)(2,1)S(1)}, u32[]{:S(2)}, u32[]{:S(2)}) collective-permute-start(bf16[2,2,256,128]{3,2,1,0:T(8,128)(2,1)S(1)} %get-tuple-element.37), channel_id=1, source_target_pairs={{0,8},{1,9},{2,10},{3,11},{4,12},{5,13},{6,14},{7,15},{8,0},{9,1},... | collective-permute-start | bytes 786440 | tf_op jit(solution)/shard_map/ppermute | solution.py:22
  6.1 1.6 %collective-permute-start.5 = (bf16[2,2,256,128]{3,2,1,0:T(8,128)(2,1)S(1)}, bf16[2,2,256,128]{3,2,1,0:T(8,128)(2,1)S(1)}, u32[]{:S(2)}, u32[]{:S(2)}) collective-permute-start(bf16[2,2,256,128]{3,2,1,0:T(8,128)(2,1)S(1)} %get-tuple-element.37), channel_id=1, source_target_pairs={{0,4},{1,5},{2,6},{3,7},{4,0},{5,1},{6,2},{7,3},{8,12},{9,13},{10,... | collective-permute-start | bytes 786440 | tf_op jit(solution)/shard_map/ppermute | solution.py:22
  7.7 1.5 %collective-permute-start.4 = (bf16[2,2,256,128]{3,2,1,0:T(8,128)(2,1)S(1)}, bf16[2,2,256,128]{3,2,1,0:T(8,128)(2,1)S(1)}, u32[]{:S(2)}, u32[]{:S(2)}) collective-permute-start(bf16[2,2,256,128]{3,2,1,0:T(8,128)(2,1)S(1)} %get-tuple-element.37), channel_id=1, source_target_pairs={{0,2},{1,3},{2,0},{3,1},{4,6},{5,7},{6,4},{7,5},{8,10},{9,11},{10,... | collective-permute-start | bytes 786440 | tf_op jit(solution)/shard_map/ppermute | solution.py:22
  9.2 0.8 %shard_map.84.bias_ref = f32[5,2,256]{2,1,0:T(2,128)S(1)} custom-call(s32[1]{0:T(128)} %bitcast.me_ref, s32[2,32]{1,0:T(2,128)} %mask_ref.1), custom_call_target="tpu_custom_call" | custom-call | bytes 16384 | tf_op jit(solution)/shard_map/pallas_call | solution.py:87
  10.0 0.0 collective-permute-done.refs_1_
  10.0 5.8 %shard_map.86 = (bf16[20,2,256,256]{3,2,1,0:T(8,128)(2,1)S(1)}, f32[20,256,128]{2,1,0:T(8,128)S(1)}, f32[20,2,256,128]{3,2,1,0:T(8,128)S(1)}) custom-call(f32[5,2,256]{2,1,0:T(2,128)S(1)} %shard_map.84.bias_ref, bf16[20,256,128]{2,1,0:T(8,128)(2,1)} %bitcast.5, bf16[4,2,256,128]{3,2,1,0:T(8,128)(2,1)S(1)} %get-tuple-element.32.refs_0_, ...), custom_call_target="tpu_custom_call" | custom-call | flops 1342177280 | bytes 5242880 | tf_op jit(solution)/shard_map/pallas_call | solution.py:380
  15.7 0.4 collective-permute-start.3
  16.1 0.4 collective-permute-start.2
  16.6 2.1 %collective-permute-done.6.refs_2_ = bf16[2,2,256,128]{3,2,1,0:T(8,128)(2,1)S(1)} collective-permute-done((bf16[2,2,256,128]{3,2,1,0:T(8,128)(2,1)S(1)}, bf16[2,2,256,128]{3,2,1,0:T(8,128)(2,1)S(1)}, u32[]{:S(2)}, u32[]{:S(2)}) %collective-permute-start.6) | collective-permute-done | bytes 262176 | tf_op jit(solution)/shard_map/ppermute | solution.py:22
  18.7 2.0 %collective-permute-start.1 = (bf16[2,2,256,128]{3,2,1,0:T(8,128)(2,1)S(1)}, bf16[2,2,256,128]{3,2,1,0:T(8,128)(2,1)S(1)}, u32[]{:S(2)}, u32[]{:S(2)}) collective-permute-start(bf16[2,2,256,128]{3,2,1,0:T(8,128)(2,1)S(1)} %get-tuple-element.36), channel_id=1, source_target_pairs={{0,2},{1,3},{2,0},{3,1},{4,6},{5,7},{6,4},{7,5},{8,10},{9,11},{10,... | collective-permute-start | bytes 786440 | tf_op jit(solution)/shard_map/ppermute | solution.py:22
  20.7 8.7 %shard_map.87 = (bf16[20,256,128]{2,1,0:T(8,128)(2,1)}, f32[20,256,128]{2,1,0:T(8,128)S(1)}, f32[20,2,256,128]{3,2,1,0:T(8,128)S(1)}, bf16[4,2,256,128]{3,2,1,0:...) custom-call(f32[5,2,256]{2,1,0:T(2,128)S(1)} %shard_map.84.bias_ref, ...), custom_call_target="tpu_custom_call" | custom-call | flops 3019898880 | bytes 2621440 | tf_op jit(solution)/shard_map/pallas_call | solution.py:395
  29.5 4.0 %collective-permute-start.8 = (bf16[2,2,256,128]{3,2,1,0:T(8,128)(2,1)S(1)}, bf16[2,2,256,128]{3,2,1,0:T(8,128)(2,1)S(1)}, u32[]{:S(2)}, u32[]{:S(2)}) collective-permute-start(bf16[2,2,256,128]{3,2,1,0:T(8,128)(2,1)S(1)} %get-tuple-element.47), channel_id=1, source_target_pairs={{0,4},{1,5},{2,6},{3,7},{4,0},{5,1},{6,2},{7,3},{8,12},{9,13},{10,... | collective-permute-start | bytes 786440 | tf_op jit(solution)/shard_map/ppermute | solution.py:22
  33.5 8.9 %shard_map.88 = (bf16[20,256,128]{2,1,0:T(8,128)(2,1)}, f32[20,256,128]{2,1,0:T(8,128)S(1)}, f32[20,2,256,128]{3,2,1,0:T(8,128)S(1)}, bf16[4,2,256,128]{3,2,1,0:...) custom-call(f32[5,2,256]{2,1,0:T(2,128)S(1)} %shard_map.84.bias_ref,, ...), custom_call_target="tpu_custom_call", output_to_operand_aliasing={{0}: (8, {}), {1}: (9, {}), {2}: (10, {}), {3}: (11, {})} | custom-call | flops 3019898880 | bytes 2621440 | tf_op jit(solution)/shard_map/pallas_call | solution.py:395
  42.4 0.4 collective-permute-start.11
  42.8 0.0 collective-permute-start.9
  42.9 1.8 %collective-permute-start.10 = (bf16[2,2,256,128]{3,2,1,0:T(8,128)(2,1)S(1)}, bf16[2,2,256,128]{3,2,1,0:T(8,128)(2,1)S(1)}, u32[]{:S(2)}, u32[]{:S(2)}) collective-permute-start(bf16[2,2,256,128]{3,2,1,0:T(8,128)(2,1)S(1)} %get-tuple-element.52), channel_id=1, source_target_pairs={{0,4},{1,5},{2,6},{3,7},{4,0},{5,1},{6,2},{7,3},{8,12},{9,13},{10,... | collective-permute-start | bytes 786440 | tf_op jit(solution)/shard_map/ppermute | solution.py:22
  44.7 4.7 %shard_map.89 = (bf16[20,256,128]{2,1,0:T(8,128)(2,1)}, bf16[2,2,256,128]{3,2,1,0:T(8,128)(2,1)S(1)}, bf16[2,2,256,128]{3,2,1,0:T(8,128)(2,1)S(1)}) custom-call(bf16[20,256,128]{2,1,0:T(8,128)(2,1)} %bitcast.8, bf16[20,256,128]{2,1,0:T(8,128)(2,1)} %bitcast.12, bf16[20,2,256,256]{3,2,1,0:T(8,128)(2,1)S(1)} %get-tuple-element.43.e_ref, ...), custom_call_target="tpu_custom_call" | custom-call | flops 1342177280 | bytes 2621440 | tf_op jit(solution)/shard_map/pallas_call | solution.py:411
  49.4 4.7 %shard_map.90 = (bf16[20,256,128]{2,1,0:T(8,128)(2,1)}, bf16[2,2,256,128]{3,2,1,0:T(8,128)(2,1)S(1)}, bf16[2,2,256,128]{3,2,1,0:T(8,128)(2,1)S(1)}) custom-call(bf16[20,256,128]{2,1,0:T(8,128)(2,1)} %bitcast.9, bf16[20,256,128]{2,1,0:T(8,128)(2,1)} %bitcast.13, ...), custom_call_target="tpu_custom_call", output_to_operand_aliasing={{0}: (7, {})} | custom-call | flops 1342177280 | bytes 2621440 | tf_op jit(solution)/shard_map/pallas_call | solution.py:411
  54.1 0.5 collective-permute-start.12
  54.6 1.6 %collective-permute-done.9.refs_2_ = bf16[2,2,256,128]{3,2,1,0:T(8,128)(2,1)S(1)} collective-permute-done((bf16[2,2,256,128]{3,2,1,0:T(8,128)(2,1)S(1)}, bf16[2,2,256,128]{3,2,1,0:T(8,128)(2,1)S(1)}, u32[]{:S(2)}, u32[]{:S(2)}) %collective-permute-start.9) | collective-permute-done | bytes 262176 | tf_op jit(solution)/shard_map/ppermute | solution.py:22
  56.2 0.2 shard_map.91.refs_0_
  56.4 1.1 %shard_map.92 = (bf16[256,4,128]{2,1,0:T(4,128)(2,1)}, bf16[256,4,128]{2,1,0:T(4,128)(2,1)}) custom-call(f32[4,2,256,128]{3,2,1,0:T(8,128)S(1)} %shard_map.91.refs_0_, bf16[2,2,256,128]{3,2,1,0:T(8,128)(2,1)S(1)} %collective-permute-done.12.refs_1_, bf16[2,2,256,128]{3,2,1,0:T(8,128)(2,1)S(1)} %get-tuple-element.55.refs_2_, ...), custom_call_target="tpu_custom_call" | custom-call | bytes 3145728 | tf_op jit(solution)/shard_map/pallas_call | solution.py:127
  (13 shorter events, 0.0 us)
Async XLA Ops:
  1.9 8.1 %collective-permute-start = (bf16[4,2,256,128]{3,2,1,0:T(8,128)(2,1)S(1)}, bf16[4,2,256,128]{3,2,1,0:T(8,128)(2,1)S(1)}, u32[]{:S(2)}, u32[]{:S(2)}) collective-permute-start(bf16[4,2,256,128]{3,2,1,0:T(8,128)(2,1)S(1)} %get-tuple-element.32.refs_0_), channel_id=1, source_target_pairs={{0,1},{1,0},{2,3},{3,2},{4,5},{5,4},{6,7},{7,6},{8,9},{9,8},{10,11... | collective-permute-start | bytes 1572872 | tf_op jit(solution)/shard_map/ppermute | solution.py:22
  2.4 16.3 %collective-permute-start.6 = (bf16[2,2,256,128]{3,2,1,0:T(8,128)(2,1)S(1)}, bf16[2,2,256,128]{3,2,1,0:T(8,128)(2,1)S(1)}, u32[]{:S(2)}, u32[]{:S(2)}) collective-permute-start(bf16[2,2,256,128]{3,2,1,0:T(8,128)(2,1)S(1)} %get-tuple-element.37), channel_id=1, source_target_pairs={{0,8},{1,9},{2,10},{3,11},{4,12},{5,13},{6,14},{7,15},{8,0},{9,1},... | collective-permute-start | bytes 786440 | tf_op jit(solution)/shard_map/ppermute | solution.py:22
  6.1 14.7 %collective-permute-start.5 = (bf16[2,2,256,128]{3,2,1,0:T(8,128)(2,1)S(1)}, bf16[2,2,256,128]{3,2,1,0:T(8,128)(2,1)S(1)}, u32[]{:S(2)}, u32[]{:S(2)}) collective-permute-start(bf16[2,2,256,128]{3,2,1,0:T(8,128)(2,1)S(1)} %get-tuple-element.37), channel_id=1, source_target_pairs={{0,4},{1,5},{2,6},{3,7},{4,0},{5,1},{6,2},{7,3},{8,12},{9,13},{10,... | collective-permute-start | bytes 786440 | tf_op jit(solution)/shard_map/ppermute | solution.py:22
  7.7 13.1 %collective-permute-start.4 = (bf16[2,2,256,128]{3,2,1,0:T(8,128)(2,1)S(1)}, bf16[2,2,256,128]{3,2,1,0:T(8,128)(2,1)S(1)}, u32[]{:S(2)}, u32[]{:S(2)}) collective-permute-start(bf16[2,2,256,128]{3,2,1,0:T(8,128)(2,1)S(1)} %get-tuple-element.37), channel_id=1, source_target_pairs={{0,2},{1,3},{2,0},{3,1},{4,6},{5,7},{6,4},{7,5},{8,10},{9,11},{10,... | collective-permute-start | bytes 786440 | tf_op jit(solution)/shard_map/ppermute | solution.py:22
  15.7 17.8 %collective-permute-start.3 = (bf16[2,2,256,128]{3,2,1,0:T(8,128)(2,1)S(1)}, bf16[2,2,256,128]{3,2,1,0:T(8,128)(2,1)S(1)}, u32[]{:S(2)}, u32[]{:S(2)}) collective-permute-start(bf16[2,2,256,128]{3,2,1,0:T(8,128)(2,1)S(1)} %get-tuple-element.36), channel_id=1, source_target_pairs={{0,8},{1,9},{2,10},{3,11},{4,12},{5,13},{6,14},{7,15},{8,0},{9,1},... | collective-permute-start | bytes 786440 | tf_op jit(solution)/shard_map/ppermute | solution.py:22
  16.1 17.4 %collective-permute-start.2 = (bf16[2,2,256,128]{3,2,1,0:T(8,128)(2,1)S(1)}, bf16[2,2,256,128]{3,2,1,0:T(8,128)(2,1)S(1)}, u32[]{:S(2)}, u32[]{:S(2)}) collective-permute-start(bf16[2,2,256,128]{3,2,1,0:T(8,128)(2,1)S(1)} %get-tuple-element.36), channel_id=1, source_target_pairs={{0,4},{1,5},{2,6},{3,7},{4,0},{5,1},{6,2},{7,3},{8,12},{9,13},{10,... | collective-permute-start | bytes 786440 | tf_op jit(solution)/shard_map/ppermute | solution.py:22
  18.7 14.8 %collective-permute-start.1 = (bf16[2,2,256,128]{3,2,1,0:T(8,128)(2,1)S(1)}, bf16[2,2,256,128]{3,2,1,0:T(8,128)(2,1)S(1)}, u32[]{:S(2)}, u32[]{:S(2)}) collective-permute-start(bf16[2,2,256,128]{3,2,1,0:T(8,128)(2,1)S(1)} %get-tuple-element.36), channel_id=1, source_target_pairs={{0,2},{1,3},{2,0},{3,1},{4,6},{5,7},{6,4},{7,5},{8,10},{9,11},{10,... | collective-permute-start | bytes 786440 | tf_op jit(solution)/shard_map/ppermute | solution.py:22
  29.5 15.2 %collective-permute-start.7 = (bf16[2,2,256,128]{3,2,1,0:T(8,128)(2,1)S(1)}, bf16[2,2,256,128]{3,2,1,0:T(8,128)(2,1)S(1)}, u32[]{:S(2)}, u32[]{:S(2)}) collective-permute-start(bf16[2,2,256,128]{3,2,1,0:T(8,128)(2,1)S(1)} %get-tuple-element.46), channel_id=1, source_target_pairs={{0,8},{1,9},{2,10},{3,11},{4,12},{5,13},{6,14},{7,15},{8,0},{9,1},... | collective-permute-start | bytes 786440 | tf_op jit(solution)/shard_map/ppermute | solution.py:22
  29.5 15.2 %collective-permute-start.8 = (bf16[2,2,256,128]{3,2,1,0:T(8,128)(2,1)S(1)}, bf16[2,2,256,128]{3,2,1,0:T(8,128)(2,1)S(1)}, u32[]{:S(2)}, u32[]{:S(2)}) collective-permute-start(bf16[2,2,256,128]{3,2,1,0:T(8,128)(2,1)S(1)} %get-tuple-element.47), channel_id=1, source_target_pairs={{0,4},{1,5},{2,6},{3,7},{4,0},{5,1},{6,2},{7,3},{8,12},{9,13},{10,... | collective-permute-start | bytes 786440 | tf_op jit(solution)/shard_map/ppermute | solution.py:22
  42.4 13.8 %collective-permute-start.11 = (bf16[4,2,256,128]{3,2,1,0:T(8,128)(2,1)S(1)}, bf16[4,2,256,128]{3,2,1,0:T(8,128)(2,1)S(1)}, u32[]{:S(2)}, u32[]{:S(2)}) collective-permute-start(bf16[4,2,256,128]{3,2,1,0:T(8,128)(2,1)S(1)} %get-tuple-element.53), channel_id=1, source_target_pairs={{0,2},{1,3},{2,0},{3,1},{4,6},{5,7},{6,4},{7,5},{8,10},{9,11},{10,... | collective-permute-start | bytes 1572872 | tf_op jit(solution)/shard_map/ppermute | solution.py:22
  42.8 13.4 %collective-permute-start.9 = (bf16[2,2,256,128]{3,2,1,0:T(8,128)(2,1)S(1)}, bf16[2,2,256,128]{3,2,1,0:T(8,128)(2,1)S(1)}, u32[]{:S(2)}, u32[]{:S(2)}) collective-permute-start(bf16[2,2,256,128]{3,2,1,0:T(8,128)(2,1)S(1)} %get-tuple-element.51), channel_id=1, source_target_pairs={{0,8},{1,9},{2,10},{3,11},{4,12},{5,13},{6,14},{7,15},{8,0},{9,1},... | collective-permute-start | bytes 786440 | tf_op jit(solution)/shard_map/ppermute | solution.py:22
  42.9 13.3 %collective-permute-start.10 = (bf16[2,2,256,128]{3,2,1,0:T(8,128)(2,1)S(1)}, bf16[2,2,256,128]{3,2,1,0:T(8,128)(2,1)S(1)}, u32[]{:S(2)}, u32[]{:S(2)}) collective-permute-start(bf16[2,2,256,128]{3,2,1,0:T(8,128)(2,1)S(1)} %get-tuple-element.52), channel_id=1, source_target_pairs={{0,4},{1,5},{2,6},{3,7},{4,0},{5,1},{6,2},{7,3},{8,12},{9,13},{10,... | collective-permute-start | bytes 786440 | tf_op jit(solution)/shard_map/ppermute | solution.py:22
  54.1 2.3 %collective-permute-start.13 = (bf16[2,2,256,128]{3,2,1,0:T(8,128)(2,1)S(1)}, bf16[2,2,256,128]{3,2,1,0:T(8,128)(2,1)S(1)}, u32[]{:S(2)}, u32[]{:S(2)}) collective-permute-start(bf16[2,2,256,128]{3,2,1,0:T(8,128)(2,1)S(1)} %get-tuple-element.56), channel_id=1, source_target_pairs={{0,1},{1,0},{2,3},{3,2},{4,5},{5,4},{6,7},{7,6},{8,9},{9,8},{10,11... | collective-permute-start | bytes 786440 | tf_op jit(solution)/shard_map/ppermute | solution.py:22
  54.1 2.3 %collective-permute-start.12 = (bf16[2,2,256,128]{3,2,1,0:T(8,128)(2,1)S(1)}, bf16[2,2,256,128]{3,2,1,0:T(8,128)(2,1)S(1)}, u32[]{:S(2)}, u32[]{:S(2)}) collective-permute-start(bf16[2,2,256,128]{3,2,1,0:T(8,128)(2,1)S(1)} %get-tuple-element.54), channel_id=1, source_target_pairs={{0,1},{1,0},{2,3},{3,2},{4,5},{5,4},{6,7},{7,6},{8,9},{9,8},{10,11... | collective-permute-start | bytes 786440 | tf_op jit(solution)/shard_map/ppermute | solution.py:22

commit v7 on v6

--- a/solution.py
+++ b/solution.py
@@ -233,12 +233,12 @@
         e = jnp.exp2(x_ref[g % 3, n] * scale2 - twice(state["top", g]))
         narrow = e.astype(jnp.bfloat16)
         e_ref[n, g * tokens : (g + 1) * tokens] = narrow
-        part = product(narrow, v_ref[n])
-        state["out", g] = state["out", g] + part if n else part
+        state["e", g, n] = narrow
 
     def forward_end(g):
         q, do = q_ref[g], do_ref[g].astype(jnp.float32)
-        out = state.pop(("out", g))
+        narrow = jnp.concatenate([state.pop(("e", g, n)) for n in every], axis=1)
+        out = product(narrow, v_ref[...].reshape(sources * tokens, 2 * size))
         share = state.pop(("share", g))
         inverse = 1.0 / (out[:, size:] + state.pop(("part", g)))
         attended = ((out[:, :size] + part_ref[g] * share) * inverse).astype(jnp.bfloat16)

time: 57.8 us -> 57.8 us (level)
  transfers between devices with their start and end apart: 14 -> 14, of which waited for: 2 -> 3; matrix products, arithmetic and copies ran while one was open for 0% -> 0% of each run, Pallas kernels for 59% -> 58%
where the time goes in v7:
time: 57.8 us; the launch traced here: 57.5 us
  Pallas kernels  35.7 us (62%)
  starting transfers between devices  17.5 us (30%)
  waiting for transfers between devices  3.59 us (6%)
  between operations  0.7 us (1%)
    ppermute x14, starting transfers between devices, from_partner(): return lax.ppermute(value, axis, pairs)  17.5 us
    pallas_call x2, Pallas kernels, remote(): pl.pallas_call(functools.partial(remote_kernel, scale, len(chain)), grid=...  17.2 us
    pallas_call x2, Pallas kernels, rest(): pl.pallas_call(functools.partial(rest_kernel, scale, len(chain)), grid=(l...  9.46 us
    pallas_call x1, Pallas kernels, local(): pl.pallas_call(functools.partial(local_kernel, scale), grid=(heads_all,),...  5.76 us
    ppermute x14, waiting for transfers between devices, from_partner(): return lax.ppermute(value, axis, pairs)  3.59 us
    pallas_call x1, Pallas kernels, pack(): pl.pallas_call(functools.partial(pack_kernel, groups), in_specs=[VMEM] *...  1.26 us
  transfers between devices with their start and end apart: 14, of which 3 were waited for; matrix products, arithmetic and copies ran while one was open for 0% of the time, Pallas kernels for 58%

profile of v7, /device:TPU:0, one launch (start us, length us, event | category | flops | bytes accessed | tf_op | source)
XLA Modules:
  0.0 57.5 jit_solution(14856889313184533267)
XLA Ops:
  0.6 1.3 %shard_map.85 = (bf16[4,2,256,128]{3,2,1,0:T(8,128)(2,1)S(1)}, bf16[2,2,256,128]{3,2,1,0:T(8,128)(2,1)S(1)}, bf16[2,2,256,128]{3,2,1,0:T(8,128)(2,1)S(1)}) custom-call(bf16[256,4,128]{2,1,0:T(4,128)(2,1)} %k_ref.1, bf16[256,4,128]{2,1,0:T(4,128)(2,1)} %v_ref.1), custom_call_target="tpu_custom_call" | custom-call | bytes 1572864 | tf_op jit(solution)/shard_map/pallas_call | solution.py:61
  1.9 0.5 collective-permute-start
  2.4 3.7 %collective-permute-start.6 = (bf16[2,2,256,128]{3,2,1,0:T(8,128)(2,1)S(1)}, bf16[2,2,256,128]{3,2,1,0:T(8,128)(2,1)S(1)}, u32[]{:S(2)}, u32[]{:S(2)}) collective-permute-start(bf16[2,2,256,128]{3,2,1,0:T(8,128)(2,1)S(1)} %get-tuple-element.37), channel_id=1, source_target_pairs={{0,8},{1,9},{2,10},{3,11},{4,12},{5,13},{6,14},{7,15},{8,0},{9,1},... | collective-permute-start | bytes 786440 | tf_op jit(solution)/shard_map/ppermute | solution.py:22
  6.1 1.6 %collective-permute-start.5 = (bf16[2,2,256,128]{3,2,1,0:T(8,128)(2,1)S(1)}, bf16[2,2,256,128]{3,2,1,0:T(8,128)(2,1)S(1)}, u32[]{:S(2)}, u32[]{:S(2)}) collective-permute-start(bf16[2,2,256,128]{3,2,1,0:T(8,128)(2,1)S(1)} %get-tuple-element.37), channel_id=1, source_target_pairs={{0,4},{1,5},{2,6},{3,7},{4,0},{5,1},{6,2},{7,3},{8,12},{9,13},{10,... | collective-permute-start | bytes 786440 | tf_op jit(solution)/shard_map/ppermute | solution.py:22
  7.7 1.5 %collective-permute-start.4 = (bf16[2,2,256,128]{3,2,1,0:T(8,128)(2,1)S(1)}, bf16[2,2,256,128]{3,2,1,0:T(8,128)(2,1)S(1)}, u32[]{:S(2)}, u32[]{:S(2)}) collective-permute-start(bf16[2,2,256,128]{3,2,1,0:T(8,128)(2,1)S(1)} %get-tuple-element.37), channel_id=1, source_target_pairs={{0,2},{1,3},{2,0},{3,1},{4,6},{5,7},{6,4},{7,5},{8,10},{9,11},{10,... | collective-permute-start | bytes 786440 | tf_op jit(solution)/shard_map/ppermute | solution.py:22
  9.2 0.8 %shard_map.84.bias_ref = f32[5,2,256]{2,1,0:T(2,128)S(1)} custom-call(s32[1]{0:T(128)} %bitcast.me_ref, s32[2,32]{1,0:T(2,128)} %mask_ref.1), custom_call_target="tpu_custom_call" | custom-call | bytes 16384 | tf_op jit(solution)/shard_map/pallas_call | solution.py:87
  10.0 5.8 %shard_map.86 = (bf16[20,2,256,256]{3,2,1,0:T(8,128)(2,1)S(1)}, f32[20,256,128]{2,1,0:T(8,128)S(1)}, f32[20,2,256,128]{3,2,1,0:T(8,128)S(1)}) custom-call(f32[5,2,256]{2,1,0:T(2,128)S(1)} %shard_map.84.bias_ref, bf16[20,256,128]{2,1,0:T(8,128)(2,1)} %bitcast.5, bf16[4,2,256,128]{3,2,1,0:T(8,128)(2,1)S(1)} %get-tuple-element.32.refs_0_, ...), custom_call_target="tpu_custom_call" | custom-call | flops 1342177280 | bytes 5242880 | tf_op jit(solution)/shard_map/pallas_call | solution.py:380
  15.7 0.4 collective-permute-start.3
  16.1 0.4 collective-permute-start.2
  16.6 2.1 %collective-permute-done.6.refs_2_ = bf16[2,2,256,128]{3,2,1,0:T(8,128)(2,1)S(1)} collective-permute-done((bf16[2,2,256,128]{3,2,1,0:T(8,128)(2,1)S(1)}, bf16[2,2,256,128]{3,2,1,0:T(8,128)(2,1)S(1)}, u32[]{:S(2)}, u32[]{:S(2)}) %collective-permute-start.6) | collective-permute-done | bytes 262176 | tf_op jit(solution)/shard_map/ppermute | solution.py:22
  18.7 2.0 %collective-permute-start.1 = (bf16[2,2,256,128]{3,2,1,0:T(8,128)(2,1)S(1)}, bf16[2,2,256,128]{3,2,1,0:T(8,128)(2,1)S(1)}, u32[]{:S(2)}, u32[]{:S(2)}) collective-permute-start(bf16[2,2,256,128]{3,2,1,0:T(8,128)(2,1)S(1)} %get-tuple-element.36), channel_id=1, source_target_pairs={{0,2},{1,3},{2,0},{3,1},{4,6},{5,7},{6,4},{7,5},{8,10},{9,11},{10,... | collective-permute-start | bytes 786440 | tf_op jit(solution)/shard_map/ppermute | solution.py:22
  20.7 8.3 %shard_map.87 = (bf16[20,256,128]{2,1,0:T(8,128)(2,1)}, f32[20,256,128]{2,1,0:T(8,128)S(1)}, f32[20,2,256,128]{3,2,1,0:T(8,128)S(1)}, bf16[4,2,256,128]{3,2,1,0:...) custom-call(f32[5,2,256]{2,1,0:T(2,128)S(1)} %shard_map.84.bias_ref, ...), custom_call_target="tpu_custom_call" | custom-call | flops 3019898880 | bytes 2621440 | tf_op jit(solution)/shard_map/pallas_call | solution.py:395
  29.1 4.0 %collective-permute-start.8 = (bf16[2,2,256,128]{3,2,1,0:T(8,128)(2,1)S(1)}, bf16[2,2,256,128]{3,2,1,0:T(8,128)(2,1)S(1)}, u32[]{:S(2)}, u32[]{:S(2)}) collective-permute-start(bf16[2,2,256,128]{3,2,1,0:T(8,128)(2,1)S(1)} %get-tuple-element.47), channel_id=1, source_target_pairs={{0,4},{1,5},{2,6},{3,7},{4,0},{5,1},{6,2},{7,3},{8,12},{9,13},{10,... | collective-permute-start | bytes 786440 | tf_op jit(solution)/shard_map/ppermute | solution.py:22
  33.2 8.9 %shard_map.88 = (bf16[20,256,128]{2,1,0:T(8,128)(2,1)}, f32[20,256,128]{2,1,0:T(8,128)S(1)}, f32[20,2,256,128]{3,2,1,0:T(8,128)S(1)}, bf16[4,2,256,128]{3,2,1,0:...) custom-call(f32[5,2,256]{2,1,0:T(2,128)S(1)} %shard_map.84.bias_ref,, ...), custom_call_target="tpu_custom_call", output_to_operand_aliasing={{0}: (8, {}), {1}: (9, {}), {2}: (10, {}), {3}: (11, {})} | custom-call | flops 3019898880 | bytes 2621440 | tf_op jit(solution)/shard_map/pallas_call | solution.py:395
  42.0 0.4 collective-permute-start.11
  42.5 0.1 collective-permute-start.9
  42.6 2.2 %collective-permute-start.10 = (bf16[2,2,256,128]{3,2,1,0:T(8,128)(2,1)S(1)}, bf16[2,2,256,128]{3,2,1,0:T(8,128)(2,1)S(1)}, u32[]{:S(2)}, u32[]{:S(2)}) collective-permute-start(bf16[2,2,256,128]{3,2,1,0:T(8,128)(2,1)S(1)} %get-tuple-element.52), channel_id=1, source_target_pairs={{0,4},{1,5},{2,6},{3,7},{4,0},{5,1},{6,2},{7,3},{8,12},{9,13},{10,... | collective-permute-start | bytes 786440 | tf_op jit(solution)/shard_map/ppermute | solution.py:22
  44.8 4.7 %shard_map.89 = (bf16[20,256,128]{2,1,0:T(8,128)(2,1)}, bf16[2,2,256,128]{3,2,1,0:T(8,128)(2,1)S(1)}, bf16[2,2,256,128]{3,2,1,0:T(8,128)(2,1)S(1)}) custom-call(bf16[20,256,128]{2,1,0:T(8,128)(2,1)} %bitcast.8, bf16[20,256,128]{2,1,0:T(8,128)(2,1)} %bitcast.12, bf16[20,2,256,256]{3,2,1,0:T(8,128)(2,1)S(1)} %get-tuple-element.43.e_ref, ...), custom_call_target="tpu_custom_call" | custom-call | flops 1342177280 | bytes 2621440 | tf_op jit(solution)/shard_map/pallas_call | solution.py:411
  49.5 4.7 %shard_map.90 = (bf16[20,256,128]{2,1,0:T(8,128)(2,1)}, bf16[2,2,256,128]{3,2,1,0:T(8,128)(2,1)S(1)}, bf16[2,2,256,128]{3,2,1,0:T(8,128)(2,1)S(1)}) custom-call(bf16[20,256,128]{2,1,0:T(8,128)(2,1)} %bitcast.9, bf16[20,256,128]{2,1,0:T(8,128)(2,1)} %bitcast.13, ...), custom_call_target="tpu_custom_call", output_to_operand_aliasing={{0}: (7, {})} | custom-call | flops 1342177280 | bytes 2621440 | tf_op jit(solution)/shard_map/pallas_call | solution.py:411
  54.3 0.5 collective-permute-start.12
  54.8 1.4 %collective-permute-done.9.refs_2_ = bf16[2,2,256,128]{3,2,1,0:T(8,128)(2,1)S(1)} collective-permute-done((bf16[2,2,256,128]{3,2,1,0:T(8,128)(2,1)S(1)}, bf16[2,2,256,128]{3,2,1,0:T(8,128)(2,1)S(1)}, u32[]{:S(2)}, u32[]{:S(2)}) %collective-permute-start.9) | collective-permute-done | bytes 262176 | tf_op jit(solution)/shard_map/ppermute | solution.py:22
  56.2 0.1 collective-permute-done.10.refs_3_
  56.2 0.2 shard_map.91.refs_0_
  56.4 1.1 %shard_map.92 = (bf16[256,4,128]{2,1,0:T(4,128)(2,1)}, bf16[256,4,128]{2,1,0:T(4,128)(2,1)}) custom-call(f32[4,2,256,128]{3,2,1,0:T(8,128)S(1)} %shard_map.91.refs_0_, bf16[2,2,256,128]{3,2,1,0:T(8,128)(2,1)S(1)} %collective-permute-done.12.refs_1_, bf16[2,2,256,128]{3,2,1,0:T(8,128)(2,1)S(1)} %get-tuple-element.55.refs_2_, ...), custom_call_target="tpu_custom_call" | custom-call | bytes 3145728 | tf_op jit(solution)/shard_map/pallas_call | solution.py:127
  (13 shorter events, 0.1 us)
Async XLA Ops:
  1.9 8.1 %collective-permute-start = (bf16[4,2,256,128]{3,2,1,0:T(8,128)(2,1)S(1)}, bf16[4,2,256,128]{3,2,1,0:T(8,128)(2,1)S(1)}, u32[]{:S(2)}, u32[]{:S(2)}) collective-permute-start(bf16[4,2,256,128]{3,2,1,0:T(8,128)(2,1)S(1)} %get-tuple-element.32.refs_0_), channel_id=1, source_target_pairs={{0,1},{1,0},{2,3},{3,2},{4,5},{5,4},{6,7},{7,6},{8,9},{9,8},{10,11... | collective-permute-start | bytes 1572872 | tf_op jit(solution)/shard_map/ppermute | solution.py:22
  2.4 16.3 %collective-permute-start.6 = (bf16[2,2,256,128]{3,2,1,0:T(8,128)(2,1)S(1)}, bf16[2,2,256,128]{3,2,1,0:T(8,128)(2,1)S(1)}, u32[]{:S(2)}, u32[]{:S(2)}) collective-permute-start(bf16[2,2,256,128]{3,2,1,0:T(8,128)(2,1)S(1)} %get-tuple-element.37), channel_id=1, source_target_pairs={{0,8},{1,9},{2,10},{3,11},{4,12},{5,13},{6,14},{7,15},{8,0},{9,1},... | collective-permute-start | bytes 786440 | tf_op jit(solution)/shard_map/ppermute | solution.py:22
  6.1 14.7 %collective-permute-start.5 = (bf16[2,2,256,128]{3,2,1,0:T(8,128)(2,1)S(1)}, bf16[2,2,256,128]{3,2,1,0:T(8,128)(2,1)S(1)}, u32[]{:S(2)}, u32[]{:S(2)}) collective-permute-start(bf16[2,2,256,128]{3,2,1,0:T(8,128)(2,1)S(1)} %get-tuple-element.37), channel_id=1, source_target_pairs={{0,4},{1,5},{2,6},{3,7},{4,0},{5,1},{6,2},{7,3},{8,12},{9,13},{10,... | collective-permute-start | bytes 786440 | tf_op jit(solution)/shard_map/ppermute | solution.py:22
  7.7 13.1 %collective-permute-start.4 = (bf16[2,2,256,128]{3,2,1,0:T(8,128)(2,1)S(1)}, bf16[2,2,256,128]{3,2,1,0:T(8,128)(2,1)S(1)}, u32[]{:S(2)}, u32[]{:S(2)}) collective-permute-start(bf16[2,2,256,128]{3,2,1,0:T(8,128)(2,1)S(1)} %get-tuple-element.37), channel_id=1, source_target_pairs={{0,2},{1,3},{2,0},{3,1},{4,6},{5,7},{6,4},{7,5},{8,10},{9,11},{10,... | collective-permute-start | bytes 786440 | tf_op jit(solution)/shard_map/ppermute | solution.py:22
  15.7 17.4 %collective-permute-start.3 = (bf16[2,2,256,128]{3,2,1,0:T(8,128)(2,1)S(1)}, bf16[2,2,256,128]{3,2,1,0:T(8,128)(2,1)S(1)}, u32[]{:S(2)}, u32[]{:S(2)}) collective-permute-start(bf16[2,2,256,128]{3,2,1,0:T(8,128)(2,1)S(1)} %get-tuple-element.36), channel_id=1, source_target_pairs={{0,8},{1,9},{2,10},{3,11},{4,12},{5,13},{6,14},{7,15},{8,0},{9,1},... | collective-permute-start | bytes 786440 | tf_op jit(solution)/shard_map/ppermute | solution.py:22
  16.1 17.0 %collective-permute-start.2 = (bf16[2,2,256,128]{3,2,1,0:T(8,128)(2,1)S(1)}, bf16[2,2,256,128]{3,2,1,0:T(8,128)(2,1)S(1)}, u32[]{:S(2)}, u32[]{:S(2)}) collective-permute-start(bf16[2,2,256,128]{3,2,1,0:T(8,128)(2,1)S(1)} %get-tuple-element.36), channel_id=1, source_target_pairs={{0,4},{1,5},{2,6},{3,7},{4,0},{5,1},{6,2},{7,3},{8,12},{9,13},{10,... | collective-permute-start | bytes 786440 | tf_op jit(solution)/shard_map/ppermute | solution.py:22
  18.7 14.5 %collective-permute-start.1 = (bf16[2,2,256,128]{3,2,1,0:T(8,128)(2,1)S(1)}, bf16[2,2,256,128]{3,2,1,0:T(8,128)(2,1)S(1)}, u32[]{:S(2)}, u32[]{:S(2)}) collective-permute-start(bf16[2,2,256,128]{3,2,1,0:T(8,128)(2,1)S(1)} %get-tuple-element.36), channel_id=1, source_target_pairs={{0,2},{1,3},{2,0},{3,1},{4,6},{5,7},{6,4},{7,5},{8,10},{9,11},{10,... | collective-permute-start | bytes 786440 | tf_op jit(solution)/shard_map/ppermute | solution.py:22
  29.1 15.7 %collective-permute-start.7 = (bf16[2,2,256,128]{3,2,1,0:T(8,128)(2,1)S(1)}, bf16[2,2,256,128]{3,2,1,0:T(8,128)(2,1)S(1)}, u32[]{:S(2)}, u32[]{:S(2)}) collective-permute-start(bf16[2,2,256,128]{3,2,1,0:T(8,128)(2,1)S(1)} %get-tuple-element.46), channel_id=1, source_target_pairs={{0,8},{1,9},{2,10},{3,11},{4,12},{5,13},{6,14},{7,15},{8,0},{9,1},... | collective-permute-start | bytes 786440 | tf_op jit(solution)/shard_map/ppermute | solution.py:22
  29.1 15.7 %collective-permute-start.8 = (bf16[2,2,256,128]{3,2,1,0:T(8,128)(2,1)S(1)}, bf16[2,2,256,128]{3,2,1,0:T(8,128)(2,1)S(1)}, u32[]{:S(2)}, u32[]{:S(2)}) collective-permute-start(bf16[2,2,256,128]{3,2,1,0:T(8,128)(2,1)S(1)} %get-tuple-element.47), channel_id=1, source_target_pairs={{0,4},{1,5},{2,6},{3,7},{4,0},{5,1},{6,2},{7,3},{8,12},{9,13},{10,... | collective-permute-start | bytes 786440 | tf_op jit(solution)/shard_map/ppermute | solution.py:22
  42.0 14.2 %collective-permute-start.11 = (bf16[4,2,256,128]{3,2,1,0:T(8,128)(2,1)S(1)}, bf16[4,2,256,128]{3,2,1,0:T(8,128)(2,1)S(1)}, u32[]{:S(2)}, u32[]{:S(2)}) collective-permute-start(bf16[4,2,256,128]{3,2,1,0:T(8,128)(2,1)S(1)} %get-tuple-element.53), channel_id=1, source_target_pairs={{0,2},{1,3},{2,0},{3,1},{4,6},{5,7},{6,4},{7,5},{8,10},{9,11},{10,... | collective-permute-start | bytes 1572872 | tf_op jit(solution)/shard_map/ppermute | solution.py:22
  42.5 13.7 %collective-permute-start.9 = (bf16[2,2,256,128]{3,2,1,0:T(8,128)(2,1)S(1)}, bf16[2,2,256,128]{3,2,1,0:T(8,128)(2,1)S(1)}, u32[]{:S(2)}, u32[]{:S(2)}) collective-permute-start(bf16[2,2,256,128]{3,2,1,0:T(8,128)(2,1)S(1)} %get-tuple-element.51), channel_id=1, source_target_pairs={{0,8},{1,9},{2,10},{3,11},{4,12},{5,13},{6,14},{7,15},{8,0},{9,1},... | collective-permute-start | bytes 786440 | tf_op jit(solution)/shard_map/ppermute | solution.py:22
  42.6 13.6 %collective-permute-start.10 = (bf16[2,2,256,128]{3,2,1,0:T(8,128)(2,1)S(1)}, bf16[2,2,256,128]{3,2,1,0:T(8,128)(2,1)S(1)}, u32[]{:S(2)}, u32[]{:S(2)}) collective-permute-start(bf16[2,2,256,128]{3,2,1,0:T(8,128)(2,1)S(1)} %get-tuple-element.52), channel_id=1, source_target_pairs={{0,4},{1,5},{2,6},{3,7},{4,0},{5,1},{6,2},{7,3},{8,12},{9,13},{10,... | collective-permute-start | bytes 786440 | tf_op jit(solution)/shard_map/ppermute | solution.py:22
  54.3 2.1 %collective-permute-start.13 = (bf16[2,2,256,128]{3,2,1,0:T(8,128)(2,1)S(1)}, bf16[2,2,256,128]{3,2,1,0:T(8,128)(2,1)S(1)}, u32[]{:S(2)}, u32[]{:S(2)}) collective-permute-start(bf16[2,2,256,128]{3,2,1,0:T(8,128)(2,1)S(1)} %get-tuple-element.56), channel_id=1, source_target_pairs={{0,1},{1,0},{2,3},{3,2},{4,5},{5,4},{6,7},{7,6},{8,9},{9,8},{10,11... | collective-permute-start | bytes 786440 | tf_op jit(solution)/shard_map/ppermute | solution.py:22
  54.3 2.1 %collective-permute-start.12 = (bf16[2,2,256,128]{3,2,1,0:T(8,128)(2,1)S(1)}, bf16[2,2,256,128]{3,2,1,0:T(8,128)(2,1)S(1)}, u32[]{:S(2)}, u32[]{:S(2)}) collective-permute-start(bf16[2,2,256,128]{3,2,1,0:T(8,128)(2,1)S(1)} %get-tuple-element.54), channel_id=1, source_target_pairs={{0,1},{1,0},{2,3},{3,2},{4,5},{5,4},{6,7},{7,6},{8,9},{9,8},{10,11... | collective-permute-start | bytes 786440 | tf_op jit(solution)/shard_map/ppermute | solution.py:22
